TPU v7x, 32 devices: a whole 2x2x4 slice. The times are simulated.
32 devices in a mesh: dp: 2 (over y), seq: 4 (over z), ctx: 4 (over x, core).
Axes of the slice: x: 2, y: 2, z: 4, core: 2. Of those that a mesh axis runs over, the one named last changes fastest.
Arguments:
- tokens: bfloat16 [8192, 2048], P(('dp', 'seq', 'ctx')), may hold values from -6 to 6
- positions: int32 [8192], P(('dp', 'seq', 'ctx')), may hold values from 0 to 7920, as said below
- cotangent: bfloat16 [8192, 2048], P(('dp', 'seq', 'ctx')), may hold values from -6 to 6
- query_weight: bfloat16 [2048, 2048], P(('dp', 'ctx')), may hold values from -0.125 to 0.125
- key_weight: bfloat16 [2048, 256], P(('dp', 'ctx')), may hold values from -0.125 to 0.125
- value_weight: bfloat16 [2048, 256], P(('dp', 'ctx')), may hold values from -0.125 to 0.125
- output_weight: bfloat16 [2048, 2048], P(('dp', 'ctx')), may hold values from -4 to 4
- gate_weight: bfloat16 [2048, 5632], P(('dp', 'ctx')), may hold values from -0.125 to 0.125
- up_weight: bfloat16 [2048, 5632], P(('dp', 'ctx')), may hold values from -0.125 to 0.125
- down_weight: bfloat16 [5632, 2048], P(('dp', 'ctx')), may hold values from -0.078125 to 0.078125
- first_gain: bfloat16 [2048], P(('dp', 'ctx')), may hold values from 0.25 to 1.75
- second_gain: bfloat16 [2048], P(('dp', 'ctx')), may hold values from 0.25 to 1.75
Outputs:
- layer_output: bfloat16 [8192, 2048], P(('dp', 'seq', 'ctx'))
- input_gradient: float32 [8192, 2048], P(('dp', 'seq', 'ctx'))
- query_gradient: float32 [2048, 2048], P(('dp', 'ctx'))
- key_gradient: float32 [2048, 256], P(('dp', 'ctx'))
- value_gradient: float32 [2048, 256], P(('dp', 'ctx'))
- output_gradient: float32 [2048, 2048], P(('dp', 'ctx'))
- gate_gradient: float32 [2048, 5632], P(('dp', 'ctx'))
- up_gradient: float32 [2048, 5632], P(('dp', 'ctx'))
- down_gradient: float32 [5632, 2048], P(('dp', 'ctx'))
- first_gradient: float32 [2048], P(('dp', 'ctx'))
- second_gradient: float32 [2048], P(('dp', 'ctx'))
Inputs may be any that keep to these rules, and one draw needn't show every extreme that they name: Within a sequence, positions rise by one inside each 256-token block; each block starts at or after the end of the block before it, at most 255 positions later, and every sequence starts at position 0.
All inputs are finite; a program needn't handle non-finite values.
Results may differ from a plain program's by a relative error of at most 0.023.
Values may be sent and summed in bfloat16 or wider, within the bound.
No kernel may reach another device: no remote copies, remote signals or barrier semaphores. Data moves between devices by JAX's collectives and lax.ppermute only.
A program may use at most 256 MiB of HBM per device.

v0:
```python
from functools import partial

import jax
import jax.numpy as jnp
from jax import lax
from jax.sharding import PartitionSpec as P

HEADS = 32
KV_HEADS = 4
HEAD_DIM = 64
BLOCK = 256


epsilon = 1e-05
rotary_base = 10000.0
masked_score = -1e30


def product(left, right):
    return jnp.dot(left, right, preferred_element_type=jnp.float32)


def inner_rows(left, right):
    return lax.dot_general(
        left, right, (((0,), (0,)), ((), ())), preferred_element_type=jnp.float32
    )


def inner_columns(left, right):
    return lax.dot_general(
        left, right, (((1,), (1,)), ((), ())), preferred_element_type=jnp.float32
    )


def rotate(features, positions):
    half_width = HEAD_DIM // 2
    exponent = jnp.arange(half_width).astype(jnp.float32) * (2.0 / HEAD_DIM)
    frequency = rotary_base ** (-exponent)
    angles = positions.astype(jnp.float32)[:, None] * frequency[None, :]
    cosine = jnp.cos(angles)[:, None, :]
    sine = jnp.sin(angles)[:, None, :]
    shaped = features.reshape(features.shape[0], -1, HEAD_DIM)
    first_half = shaped[:, :, :half_width]
    second_half = shaped[:, :, half_width:]
    turned = jnp.concatenate(
        [first_half * cosine - second_half * sine, second_half * cosine + first_half * sine], axis=2
    )
    return turned.reshape(features.shape)


def normalize(features):
    inverse_rms = lax.rsqrt(jnp.mean(features * features, axis=-1, keepdims=True) + epsilon)
    return (features * inverse_rms, inverse_rms)


def norm_backward(slopes, normed, inverse_rms):
    return inverse_rms * (slopes - normed * jnp.mean(slopes * normed, axis=-1, keepdims=True))


def attention_rows(query_weight, key_weight, value_weight, first_gain, normed, slopes):
    row_count = normed.shape[0]
    if slopes is None:
        initial = (
            jnp.zeros((row_count, query_weight.shape[1]), jnp.float32),
            jnp.zeros((row_count, key_weight.shape[1]), jnp.float32),
            jnp.zeros((row_count, value_weight.shape[1]), jnp.float32),
        )

        def combine(running, portions, anchor):
            query_part, key_part, value_part, gain_part = portions
            scaled = (normed * gain_part.astype(jnp.float32)[None, :]).astype(jnp.bfloat16)
            return (
                product(scaled, query_part),
                product(scaled, key_part),
                product(scaled, value_part),
            )

    else:
        query_slope, key_slope, value_slope = slopes
        full_width = normed.shape[1]
        initial = (
            jnp.zeros((row_count, full_width), jnp.float32),
            jnp.zeros((full_width,), jnp.float32),
            jnp.zeros((full_width, query_slope.shape[1]), jnp.float32),
            jnp.zeros((full_width, key_slope.shape[1]), jnp.float32),
            jnp.zeros((full_width, value_slope.shape[1]), jnp.float32),
        )

        def combine(running, portions, anchor):
            query_part, key_part, value_part, gain_part = portions
            gain_values = gain_part.astype(jnp.float32)[None, :]
            scaled = (normed * gain_values).astype(jnp.bfloat16)
            normed_slope = (
                inner_columns(query_slope, query_part)
                + inner_columns(key_slope, key_part)
                + inner_columns(value_slope, value_part)
            )
            return (
                normed_slope * gain_values,
                jnp.sum(normed_slope * normed, axis=0),
                inner_rows(scaled, query_slope),
                inner_rows(scaled, key_slope),
                inner_rows(scaled, value_slope),
            )

    return combine(
        initial,
        (
            lax.all_gather(query_weight, ("dp", "ctx"), axis=0, tiled=True),
            lax.all_gather(key_weight, ("dp", "ctx"), axis=0, tiled=True),
            lax.all_gather(value_weight, ("dp", "ctx"), axis=0, tiled=True),
            lax.all_gather(first_gain, ("dp", "ctx"), axis=0, tiled=True),
        ),
        jnp.int32(0),
    )


def feed_rows(gate_weight, up_weight, second_gain, normed, slopes):
    row_count = normed.shape[0]
    column_total = gate_weight.shape[1]
    if slopes is None:
        initial = (
            jnp.zeros((row_count, column_total), jnp.float32),
            jnp.zeros((row_count, column_total), jnp.float32),
        )

        def combine(running, portions, anchor):
            gate_part, up_part, gain_part = portions
            scaled = (normed * gain_part.astype(jnp.float32)[None, :]).astype(jnp.bfloat16)
            return (product(scaled, gate_part), product(scaled, up_part))

    else:
        gate_slope, up_slope = slopes
        full_width = normed.shape[1]
        initial = (
            jnp.zeros((row_count, full_width), jnp.float32),
            jnp.zeros((full_width,), jnp.float32),
            jnp.zeros((full_width, column_total), jnp.float32),
            jnp.zeros((full_width, column_total), jnp.float32),
        )

        def combine(running, portions, anchor):
            gate_part, up_part, gain_part = portions
            gain_values = gain_part.astype(jnp.float32)[None, :]
            scaled = (normed * gain_values).astype(jnp.bfloat16)
            normed_slope = inner_columns(gate_slope, gate_part) + inner_columns(up_slope, up_part)
            return (
                normed_slope * gain_values,
                jnp.sum(normed_slope * normed, axis=0),
                inner_rows(scaled, gate_slope),
                inner_rows(scaled, up_slope),
            )

    return combine(
        initial,
        (
            lax.all_gather(gate_weight, ("dp", "ctx"), axis=0, tiled=True),
            lax.all_gather(up_weight, ("dp", "ctx"), axis=0, tiled=True),
            lax.all_gather(second_gain, ("dp", "ctx"), axis=0, tiled=True),
        ),
        jnp.int32(0),
    )


def single_rows(weight, operand, backward):
    owner_count = lax.axis_size(("dp", "ctx"))
    if backward:
        initial = jnp.zeros((operand.shape[0], weight.shape[0] * owner_count), jnp.float32)

        def combine(running, portion, anchor):
            return inner_columns(operand, portion)

    else:
        initial = jnp.zeros((operand.shape[0], weight.shape[1]), jnp.float32)

        def combine(running, portion, anchor):
            return product(operand, portion)

    return combine(initial, lax.all_gather(weight, ("dp", "ctx"), axis=0, tiled=True), jnp.int32(0))


def sum_shares(shares):
    return lax.psum_scatter(
        shares.astype(jnp.bfloat16), "seq", scatter_dimension=0, tiled=True
    ).astype(jnp.float32)


def pick_columns(weight, owner_count, group_count, group_index):
    row_count = weight.shape[0]
    shaped = weight.reshape(row_count, owner_count, group_count, -1)
    picked = lax.dynamic_slice_in_dim(shaped, group_index, 1, 2)
    return picked.reshape(row_count, -1)


def place_columns(values, owner_count, group_count, group_index):
    row_count = values.shape[0]
    shaped = values.reshape(row_count, owner_count, 1, -1)
    filled = jnp.zeros((row_count, owner_count, group_count, shaped.shape[3]), values.dtype)
    return lax.dynamic_update_slice_in_dim(filled, shaped, group_index, 2).reshape(row_count, -1)


def place_rows(values, group_count, group_index):
    filled = jnp.zeros((values.shape[0] * group_count, values.shape[1]), values.dtype)
    return lax.dynamic_update_slice_in_dim(filled, values, group_index * values.shape[0], 0)


def block_mask(row_count, key_count, token_count, context_count, context_index):
    query_rows = jnp.arange(row_count)
    query_place = (
        query_rows // token_count * (context_count * token_count)
        + context_index * token_count
        + query_rows % token_count
    )
    key_rows = jnp.arange(key_count)
    key_local = key_rows % row_count
    key_place = (
        key_local // token_count * (context_count * token_count)
        + key_rows // row_count * token_count
        + key_local % token_count
    )
    return (key_place // BLOCK)[None, :] <= (query_place // BLOCK)[:, None]


def head_scores(queries, paired, allowed, head_number, group_size):
    query_columns = lax.dynamic_slice_in_dim(queries, head_number * HEAD_DIM, HEAD_DIM, 1)
    base_column = head_number // group_size * (2 * HEAD_DIM)
    key_columns = lax.dynamic_slice_in_dim(paired, base_column, HEAD_DIM, 1)
    value_columns = lax.dynamic_slice_in_dim(paired, base_column + HEAD_DIM, HEAD_DIM, 1)
    scores = jnp.where(
        allowed, inner_columns(query_columns, key_columns) * HEAD_DIM ** (-0.5), masked_score
    )
    return (query_columns, key_columns, value_columns, scores)


def attend_forward(queries, paired, allowed, group_size):
    head_count = queries.shape[1] // HEAD_DIM

    def one_head(head_number, carried):
        outputs, log_sums = carried
        query_columns, key_columns, value_columns, scores = head_scores(
            queries, paired, allowed, head_number, group_size
        )
        row_peak = jnp.max(scores, axis=1, keepdims=True)
        row_total = jnp.sum(jnp.exp(scores - row_peak), axis=1, keepdims=True)
        log_total = row_peak + jnp.log(row_total)
        weights = jnp.exp(scores - log_total).astype(jnp.bfloat16)
        head_output = product(weights, value_columns).astype(jnp.bfloat16)
        outputs = lax.dynamic_update_slice_in_dim(outputs, head_output, head_number * HEAD_DIM, 1)
        log_sums = lax.dynamic_update_slice_in_dim(log_sums, log_total, head_number, 1)
        return (outputs, log_sums)

    initial = (
        jnp.zeros(queries.shape, jnp.bfloat16),
        jnp.zeros((queries.shape[0], head_count), jnp.float32),
    )
    return lax.fori_loop(0, head_count, one_head, initial)


def attend_backward(queries, paired, allowed, group_size, log_sums, slopes):
    head_count = queries.shape[1] // HEAD_DIM
    scale = HEAD_DIM ** (-0.5)

    def one_head(head_number, carried):
        query_slope, pair_slope = carried
        query_columns, key_columns, value_columns, scores = head_scores(
            queries, paired, allowed, head_number, group_size
        )
        log_total = lax.dynamic_slice_in_dim(log_sums, head_number, 1, 1)
        weights = jnp.exp(scores - log_total)
        slope_columns = lax.dynamic_slice_in_dim(slopes, head_number * HEAD_DIM, HEAD_DIM, 1)
        weight_slope = inner_columns(slope_columns, value_columns)
        row_terms = jnp.sum(weights * weight_slope, axis=1, keepdims=True)
        score_slope = (weights * (weight_slope - row_terms)).astype(jnp.bfloat16)
        query_part = product(score_slope, key_columns) * scale
        key_part = inner_rows(score_slope, query_columns) * scale
        value_part = inner_rows(weights.astype(jnp.bfloat16), slope_columns)
        previous = pair_slope
        pair_slope = previous + jnp.concatenate([key_part, value_part], axis=1)
        query_slope = lax.dynamic_update_slice_in_dim(
            query_slope, query_part, head_number * HEAD_DIM, 1
        )
        return (query_slope, pair_slope)

    initial = (jnp.zeros(queries.shape, jnp.float32), jnp.zeros(paired.shape, jnp.float32))
    return lax.fori_loop(0, head_count, one_head, initial)


def on_device(
    tokens,
    positions,
    cotangent,
    query_weight,
    key_weight,
    value_weight,
    output_weight,
    gate_weight,
    up_weight,
    down_weight,
    first_gain,
    second_gain,
):
    token_count = tokens.shape[0]
    context_count = lax.axis_size("ctx")
    sequence_count = lax.axis_size("seq")
    owner_count = lax.axis_size(("dp", "ctx"))
    context_index = lax.axis_index("ctx")
    sequence_index = lax.axis_index("seq")
    group_size = HEADS // KV_HEADS
    inputs = tokens.astype(jnp.float32)
    first_normed, first_inverse = normalize(inputs)
    query_linear, key_linear, value_linear = attention_rows(
        query_weight, key_weight, value_weight, first_gain, first_normed, None
    )
    queries = rotate(query_linear, positions).astype(jnp.bfloat16)
    key_heads = rotate(key_linear, positions).reshape(token_count, -1, 1, HEAD_DIM)
    value_heads = value_linear.reshape(token_count, -1, 1, HEAD_DIM)
    paired = (
        jnp.concatenate([key_heads, value_heads], axis=2)
        .reshape(token_count, -1)
        .astype(jnp.bfloat16)
    )
    head_queries, head_pairs = (
        lax.all_to_all(queries, "seq", split_axis=1, concat_axis=0, tiled=True),
        lax.all_to_all(paired, "seq", split_axis=1, concat_axis=0, tiled=True),
    )
    all_pairs = lax.all_gather(head_pairs, "ctx", axis=0, tiled=True)
    allowed = block_mask(
        head_queries.shape[0], all_pairs.shape[0], token_count, context_count, context_index
    )
    head_outputs, log_sums = attend_forward(head_queries, all_pairs, allowed, group_size)
    attended = lax.all_to_all(head_outputs, "seq", split_axis=0, concat_axis=1, tiled=True)
    middle = inputs + single_rows(output_weight, attended, False)
    second_normed, second_inverse = normalize(middle)
    gate_use = pick_columns(gate_weight, owner_count, sequence_count, sequence_index)
    up_use = pick_columns(up_weight, owner_count, sequence_count, sequence_index)
    part_rows = down_weight.shape[0] // sequence_count
    down_use = lax.dynamic_slice_in_dim(down_weight, sequence_index * part_rows, part_rows, 0)
    feed_normed = lax.all_gather(second_normed, "seq", axis=0, tiled=True)
    gate_values, up_values = feed_rows(gate_use, up_use, second_gain, feed_normed, None)
    gate_sigmoid = jax.nn.sigmoid(gate_values)
    hidden = (gate_values * gate_sigmoid * up_values).astype(jnp.bfloat16)
    feed_output = single_rows(down_use, hidden, False)
    feed_output = sum_shares(feed_output)
    layer_output = (middle + feed_output).astype(jnp.bfloat16)
    feed_slope = lax.all_gather(cotangent, "seq", axis=0, tiled=True)
    hidden_slope = single_rows(down_use, feed_slope, True)
    down_gradient = inner_rows(hidden, feed_slope)
    gate_slope = (
        hidden_slope * up_values * gate_sigmoid * (1.0 + gate_values * (1.0 - gate_sigmoid))
    ).astype(jnp.bfloat16)
    up_slope = (hidden_slope * gate_values * gate_sigmoid).astype(jnp.bfloat16)
    second_slope, second_gradient, gate_gradient, up_gradient = feed_rows(
        gate_use, up_use, second_gain, feed_normed, (gate_slope, up_slope)
    )
    second_slope = sum_shares(second_slope)
    middle_slope = cotangent.astype(jnp.float32) + norm_backward(
        second_slope, second_normed, second_inverse
    )
    attention_slope = middle_slope.astype(jnp.bfloat16)
    output_gradient = inner_rows(attended, attention_slope)
    attended_slope = single_rows(output_weight, attention_slope, True).astype(jnp.bfloat16)
    head_slopes = lax.all_to_all(attended_slope, "seq", split_axis=1, concat_axis=0, tiled=True)
    query_turned, pair_terms = attend_backward(
        head_queries, all_pairs, allowed, group_size, log_sums, head_slopes
    )
    pair_slope = lax.psum_scatter(
        pair_terms.astype(jnp.bfloat16), "ctx", scatter_dimension=0, tiled=True
    )
    token_query, token_pair = (
        lax.all_to_all(
            query_turned.astype(jnp.bfloat16), "seq", split_axis=0, concat_axis=1, tiled=True
        ),
        lax.all_to_all(pair_slope, "seq", split_axis=0, concat_axis=1, tiled=True),
    )
    pair_shaped = token_pair.reshape(token_count, -1, 2, HEAD_DIM)
    key_turned = pair_shaped[:, :, 0, :].reshape(token_count, -1)
    value_slope = pair_shaped[:, :, 1, :].reshape(token_count, -1)
    unused_query, query_turn = jax.vjp(partial(rotate, positions=positions), query_linear)
    query_slope = query_turn(token_query.astype(jnp.float32))[0].astype(jnp.bfloat16)
    unused_key, key_turn = jax.vjp(partial(rotate, positions=positions), key_linear)
    key_slope = key_turn(key_turned.astype(jnp.float32))[0].astype(jnp.bfloat16)
    first_slope, first_gradient, query_gradient, key_gradient, value_gradient = attention_rows(
        query_weight,
        key_weight,
        value_weight,
        first_gain,
        first_normed,
        (query_slope, key_slope, value_slope),
    )
    input_gradient = middle_slope + norm_backward(first_slope, first_normed, first_inverse)
    reduced = (
        lax.psum_scatter(
            query_gradient.astype(jnp.bfloat16), ("dp", "ctx"), scatter_dimension=0, tiled=True
        ).astype(jnp.float32),
        lax.psum_scatter(
            key_gradient.astype(jnp.bfloat16), ("dp", "ctx"), scatter_dimension=0, tiled=True
        ).astype(jnp.float32),
        lax.psum_scatter(
            value_gradient.astype(jnp.bfloat16), ("dp", "ctx"), scatter_dimension=0, tiled=True
        ).astype(jnp.float32),
        lax.psum_scatter(
            output_gradient.astype(jnp.bfloat16), ("dp", "ctx"), scatter_dimension=0, tiled=True
        ).astype(jnp.float32),
        lax.psum_scatter(
            gate_gradient.astype(jnp.bfloat16), ("dp", "ctx"), scatter_dimension=0, tiled=True
        ).astype(jnp.float32),
        lax.psum_scatter(
            up_gradient.astype(jnp.bfloat16), ("dp", "ctx"), scatter_dimension=0, tiled=True
        ).astype(jnp.float32),
        lax.psum_scatter(
            down_gradient.astype(jnp.bfloat16), ("dp", "ctx"), scatter_dimension=0, tiled=True
        ).astype(jnp.float32),
        lax.psum_scatter(
            first_gradient.astype(jnp.bfloat16), ("dp", "ctx"), scatter_dimension=0, tiled=True
        ).astype(jnp.float32),
        lax.psum_scatter(
            second_gradient.astype(jnp.bfloat16), ("dp", "ctx"), scatter_dimension=0, tiled=True
        ).astype(jnp.float32),
    )
    gate_owned = reduced[4]
    up_owned = reduced[5]
    down_owned = reduced[6]
    gate_owned = place_columns(gate_owned, owner_count, sequence_count, sequence_index)
    up_owned = place_columns(up_owned, owner_count, sequence_count, sequence_index)
    down_owned = place_rows(down_owned, sequence_count, sequence_index)
    summed = (
        lax.psum(reduced[0].astype(jnp.bfloat16), "seq").astype(jnp.float32),
        lax.psum(reduced[1].astype(jnp.bfloat16), "seq").astype(jnp.float32),
        lax.psum(reduced[2].astype(jnp.bfloat16), "seq").astype(jnp.float32),
        lax.psum(reduced[3].astype(jnp.bfloat16), "seq").astype(jnp.float32),
        lax.psum(gate_owned.astype(jnp.bfloat16), "seq").astype(jnp.float32),
        lax.psum(up_owned.astype(jnp.bfloat16), "seq").astype(jnp.float32),
        lax.psum(down_owned.astype(jnp.bfloat16), "seq").astype(jnp.float32),
        lax.psum(reduced[7].astype(jnp.bfloat16), "seq").astype(jnp.float32),
        lax.psum(reduced[8].astype(jnp.bfloat16), "seq").astype(jnp.float32),
    )
    return (
        layer_output,
        input_gradient,
        summed[0],
        summed[1],
        summed[2],
        summed[3],
        summed[4],
        summed[5],
        summed[6],
        summed[7],
        summed[8],
    )


def solution(mesh):
    return jax.shard_map(
        on_device,
        mesh=mesh,
        in_specs=(
            P(("dp", "seq", "ctx"), None),
            P(("dp", "seq", "ctx")),
            P(("dp", "seq", "ctx"), None),
            P(("dp", "ctx"), None),
            P(("dp", "ctx"), None),
            P(("dp", "ctx"), None),
            P(("dp", "ctx"), None),
            P(("dp", "ctx"), None),
            P(("dp", "ctx"), None),
            P(("dp", "ctx"), None),
            P(("dp", "ctx")),
            P(("dp", "ctx")),
        ),
        out_specs=(
            P(("dp", "seq", "ctx"), None),
            P(("dp", "seq", "ctx"), None),
            P(("dp", "ctx"), None),
            P(("dp", "ctx"), None),
            P(("dp", "ctx"), None),
            P(("dp", "ctx"), None),
            P(("dp", "ctx"), None),
            P(("dp", "ctx"), None),
            P(("dp", "ctx"), None),
            P(("dp", "ctx")),
            P(("dp", "ctx")),
        ),
        check_vma=False,
    )
```

profile of v0, /device:TPU:0, one launch (start us, length us, event | category | flops | bytes accessed | tf_op | source)
XLA Modules:
  0.0 2067.1 jit_solution(8112807368731733711)
XLA Ops:
  10.1 10.3 all-gather
  22.9 13.2 all-gather.15.cloned.1.call-done
  38.4 23.1 %all-gather.17.cloned.1.call-done = bf16[2048,256]{1,0:T(8,128)(2,1)} async-done(((bf16[256,256]{1,0:T(8,128)(2,1)}), bf16[2048,256]{1,0:T(8,128)(2,1)}) %all-gather.17.cloned.1.call-update) | async-done | bytes 1048592 | tf_op jit(solution)/shard_map/all_gather | solution.py:111
  63.8 13.7 all_to_all.99
  79.5 38.3 %all-gather.13.cloned.1.call-done = bf16[2048,2048]{1,0:T(8,128)(2,1)} async-done(((bf16[256,2048]{1,0:T(8,128)(2,1)}), bf16[2048,2048]{1,0:T(8,128)(2,1)}) %all-gather.13.cloned.1.call-update) | async-done | bytes 8388624 | tf_op jit(solution)/shard_map/all_gather | solution.py:109
  132.3 25.0 %all-to-all-done = bf16[256,4,512]{0,2,1:T(8,128)(2,1)} async-done(((bf16[256,4,512]{0,2,1:T(8,128)(2,1)}), bf16[256,4,512]{0,2,1:T(8,128)(2,1)}, u32[]{:S(2)}, u32[]{:S(2)}) %all-to-all-start) | async-done | bytes 1048608 | tf_op jit(solution)/shard_map/all_to_all | solution.py:323
  160.0 210.6 %while.36 = (s32[]{:T(128)}, bf16[1024,512]{0,1:T(8,128)(2,1)}, f32[1024,8]{0,1:T(8,128)}, bf16[1024,512]{1,0:T(8,128)(2,1)S(1)}, bf16[4096,128]{1,0:T(8,128)(2,...) while((s32[]{:T(128)}, bf16[1024,512]{0,1:T(8,128)(2,1)}, ...), condition=%wide.region_4.5_spmd.clone, body=%wide.region_1.4_spmd.clone.sunk | while | flops 1132526592 | bytes 124223928 | solution.py:256
  176.6 9.1 fusion.151
  202.6 9.4 fusion.151
  228.9 9.1 fusion.151
  254.9 9.1 fusion.151
  280.8 9.7 fusion.151
  308.1 9.2 fusion.151
  334.1 9.1 fusion.151
  360.1 9.1 fusion.151
  373.2 29.7 %all_to_all.100 = bf16[4,256,512]{2,1,0:T(8,128)(2,1)} all-to-all(bf16[4,256,512]{2,1,0:T(8,128)(2,1)} %bitcast.121), channel_id=1, replica_groups=mesh['dp'=2,'seq'=4,'ctx'=4] {'seq'}, dimensions={0} | all-to-all | bytes 2097152 | tf_op jit(solution)/shard_map/all_to_all | solution.py:331
  426.8 9.2 all-gather.1
  436.1 11.8 fusion.96
  447.9 113.1 %all-gather.23.cloned.1.call-done = f32[1024,2048]{1,0:T(8,128)} async-done(((f32[256,2048]{1,0:T(8,128)}), f32[1024,2048]{1,0:T(8,128)}) %all-gather.23.cloned.1.call-update) | async-done | bytes 8388624 | tf_op jit(solution)/shard_map/all_gather | solution.py:338
  567.6 38.5 %all-gather.27.cloned.1.call-done = bf16[2048,1408]{0,1:T(8,128)(2,1)} async-done(((bf16[256,1408]{0,1:T(8,128)(2,1)}), bf16[2048,1408]{0,1:T(8,128)(2,1)}) %all-gather.27.cloned.1.call-update) | async-done | bytes 5767184 | tf_op jit(solution)/shard_map/all_gather | solution.py:158
  606.1 11.8 fusion.95
  617.9 34.4 %all-gather.25.cloned.1.call-done = bf16[2048,1408]{0,1:T(8,128)(2,1)} async-done(((bf16[256,1408]{0,1:T(8,128)(2,1)}), bf16[2048,1408]{0,1:T(8,128)(2,1)}) %all-gather.25.cloned.1.call-update) | async-done | bytes 5767184 | tf_op jit(solution)/shard_map/all_gather | solution.py:157
  652.2 17.0 fusion.36
  669.3 10.6 fusion.97
  679.9 12.5 multiply_reduce_fusion.1
  692.5 76.9 %reduce-scatter.13.cloned.1.call-done = bf16[256,2048]{1,0:T(8,128)(2,1)} async-done(((bf16[1024,2048]{1,0:T(8,128)(2,1)}), bf16[256,2048]{1,0:T(8,128)(2,1)}) %reduce-scatter.13.cloned.1.call-update) | async-done | bytes 1048592 | tf_op jit(solution)/shard_map/reduce_scatter | solution.py:183
  784.8 26.3 %all-to-all-done.3 = bf16[256,4,512]{2,0,1:T(8,128)(2,1)} async-done(((bf16[256,4,512]{2,0,1:T(8,128)(2,1)}), bf16[256,4,512]{2,0,1:T(8,128)(2,1)}, u32[]{:S(2)}, u32[]{:S(2)}) %all-to-all-start.3) | async-done | bytes 1048608 | tf_op jit(solution)/shard_map/all_to_all | solution.py:362
  812.2 317.6 %while.37 = (s32[]{:T(128)}, bf16[1024,512]{0,1:T(8,128)(2,1)}, f32[4096,128]{0,1:T(8,128)}, bf16[1024,512]{1,0:T(8,128)(2,1)}, bf16[4096,128]{1,0:T(8,128)(2,1)...) while((s32[]{:T(128)}, bf16[1024,512]{0,1:T(8,128)(2,1)}, ...), condition=%wide.region_11.12_spmd.clone, body=%wide.region_9.11_spmd.clone.sunk | while | flops 2728197120 | bytes 142909920 | solution.py:285
  812.5 9.2 fusion.160
  822.4 9.1 multiply_reduce_fusion.4
  831.5 7.9 multiply_convert_fusion.5
  850.7 9.2 fusion.160
  860.7 9.1 multiply_reduce_fusion.4
  869.8 7.9 multiply_convert_fusion.5
  890.6 9.2 fusion.160
  900.6 9.1 multiply_reduce_fusion.4
  930.5 9.2 fusion.160
  940.4 9.1 multiply_reduce_fusion.4
  949.6 7.9 multiply_convert_fusion.5
  970.4 9.2 fusion.160
  980.3 9.1 multiply_reduce_fusion.4
  989.4 7.9 multiply_convert_fusion.5
  1010.2 9.2 fusion.160
  1020.2 9.1 multiply_reduce_fusion.4
  1050.1 9.2 fusion.160
  1060.0 9.1 multiply_reduce_fusion.4
  1090.0 9.2 fusion.160
  1099.9 9.1 multiply_reduce_fusion.4
  1132.6 11.2 convolution_convert_fusion.2
  1145.6 10.8 convolution_convert_fusion.1
  1158.3 10.7 convolution_convert_fusion
  1169.1 12.3 all_to_all.101
  1193.8 27.8 %all_to_all.102 = bf16[4,256,512]{2,1,0:T(8,128)(2,1)S(1)} all-to-all(bf16[4,256,512]{2,1,0:T(8,128)(2,1)S(1)} %bitcast.123), channel_id=1, replica_groups=mesh['dp'=2,'seq'=4,'ctx'=4] {'seq'}, dimensions={0} | all-to-all | bytes 2097152 | tf_op jit(solution)/shard_map/all_to_all | solution.py:370
  1232.8 11.7 convolution_convert_fusion.5
  1246.2 36.6 %reduce-scatter.27.cloned.1.call-done = bf16[256,1408]{1,0:T(8,128)(2,1)} async-done(((bf16[2048,1408]{1,0:T(8,128)(2,1)}), bf16[256,1408]{1,0:T(8,128)(2,1)}) %reduce-scatter.27.cloned.1.call-update) | async-done | bytes 720912 | tf_op jit(solution)/shard_map/reduce_scatter | solution.py:407
  1289.6 56.1 %reduce-scatter.29.cloned.1.call-done = bf16[176,2048]{1,0:T(8,128)(2,1)} async-done(((bf16[1408,2048]{1,0:T(8,128)(2,1)}), bf16[176,2048]{1,0:T(8,128)(2,1)}) %reduce-scatter.29.cloned.1.call-update) | async-done | bytes 720912 | tf_op jit(solution)/shard_map/reduce_scatter | solution.py:410
  1349.7 35.4 %reduce-scatter.19.cloned.1.call-done = bf16[256,256]{1,0:T(8,128)(2,1)} async-done(((bf16[2048,256]{1,0:T(8,128)(2,1)}), bf16[256,256]{1,0:T(8,128)(2,1)}) %reduce-scatter.19.cloned.1.call-update) | async-done | bytes 131088 | tf_op jit(solution)/shard_map/reduce_scatter | solution.py:395
  1385.1 39.4 %reduce-scatter.21.cloned.1.call-done = bf16[256,256]{1,0:T(8,128)(2,1)} async-done(((bf16[2048,256]{1,0:T(8,128)(2,1)}), bf16[256,256]{1,0:T(8,128)(2,1)}) %reduce-scatter.21.cloned.1.call-update) | async-done | bytes 131088 | tf_op jit(solution)/shard_map/reduce_scatter | solution.py:398
  1424.5 75.0 %reduce-scatter.23.cloned.1.call-done = bf16[256,2048]{1,0:T(8,128)(2,1)} async-done(((bf16[2048,2048]{1,0:T(8,128)(2,1)}), bf16[256,2048]{1,0:T(8,128)(2,1)}) %reduce-scatter.23.cloned.1.call-update) | async-done | bytes 1048592 | tf_op jit(solution)/shard_map/reduce_scatter | solution.py:401
  1499.5 74.8 %reduce-scatter.17.cloned.1.call-done = bf16[256,2048]{1,0:T(8,128)(2,1)} async-done(((bf16[2048,2048]{1,0:T(8,128)(2,1)}), bf16[256,2048]{1,0:T(8,128)(2,1)}) %reduce-scatter.17.cloned.1.call-update) | async-done | bytes 1048592 | tf_op jit(solution)/shard_map/reduce_scatter | solution.py:392
  1576.2 77.1 %reduce-scatter.11.cloned.1.call-done = bf16[256,2048]{1,0:T(8,128)(2,1)} async-done(((bf16[1024,2048]{1,0:T(8,128)(2,1)}), bf16[256,2048]{1,0:T(8,128)(2,1)}) %reduce-scatter.11.cloned.1.call-update) | async-done | bytes 1048592 | tf_op jit(solution)/shard_map/reduce_scatter | solution.py:183
  1665.3 14.8 all-reduce.6
  1680.2 12.6 all-reduce.7
  1697.4 340.8 %all-reduce.11.cloned.1.call-done = (bf16[256,5632]{0,1:T(8,128)(2,1)}, bf16[256,5632]{0,1:T(8,128)(2,1)}, bf16[256,2048]{1,0:T(8,128)(2,1)}, bf16[256,256]{1,0:...) async-done(((bf16[256,5632]{0,1:T(8,128)(2,1)}, bf16[256,5632]{0,1:T(8,128)(2,1)}, bf16[256,2048]{1,0:T(8,128)(2,1)}, ...) | async-done | bytes 11010064 | tf_op jit(solution)/shard_map/psum | solution.py:431
  (329 shorter events, 436.3 us)
Async XLA Ops:
  7.2 123.9 %copy-start = (bf16[704,2048]{1,0:T(8,128)(2,1)S(1)}, bf16[704,2048]{1,0:T(8,128)(2,1)}, u32[]{:S(2)}) copy-start(bf16[704,2048]{1,0:T(8,128)(2,1)} %param.25) | copy-start | bytes 8650756
  7.2 28.9 %all-gather.15.cloned.1.call-start = ((), (), s32[]{:S(2)}) async-start(), calls=%async_computation.17 | async-start | bytes 1179648 | tf_op jit(solution)/shard_map/all_gather | solution.py:110
  7.9 53.6 %all-gather.17.cloned.1.call-start = ((), (), s32[]{:S(2)}) async-start(), calls=%async_computation.18 | async-start | bytes 1179648 | tf_op jit(solution)/shard_map/all_gather | solution.py:111
  8.7 109.2 %all-gather.13.cloned.1.call-start = ((), (), s32[]{:S(2)}) async-start(), calls=%async_computation.16 | async-start | bytes 9437184 | tf_op jit(solution)/shard_map/all_gather | solution.py:109
  9.4 149.4 %all-gather.19.cloned.1.call-start = ((), (), s32[]{:S(2)}) async-start(), calls=%async_computation.19 | async-start | bytes 1310720 | tf_op jit(solution)/shard_map/all_gather | solution.py:326
  20.5 97.4 %copy-start.27 = (f32[8,1,256]{2,1,0:T(1,128)}, f32[8,1,256]{2,1,0:T(1,128)S(1)}, u32[]{:S(2)}) copy-start(f32[8,1,256]{2,1,0:T(1,128)S(1)} %convert_element_type.297) | copy-start | bytes 24580
  22.7 95.2 %copy-start.29 = (f32[256]{0:T(256)}, f32[256]{0:T(256)S(1)}, u32[]{:S(2)}) copy-start(f32[256]{0:T(256)S(1)} %add_rsqrt_fusion.1) | copy-start | bytes 3076
  22.9 102.2 %copy-start.23 = (f32[256,32]{0,1:T(8,128)}, f32[256,32]{0,1:T(8,128)S(1)}, u32[]{:S(2)}) copy-start(f32[256,32]{0,1:T(8,128)S(1)} %get-tuple-element.522) | copy-start | bytes 98308
  22.9 102.2 %copy-start.25 = (f32[256,32]{0,1:T(8,128)}, f32[256,32]{0,1:T(8,128)S(1)}, u32[]{:S(2)}) copy-start(f32[256,32]{0,1:T(8,128)S(1)} %get-tuple-element.523) | copy-start | bytes 98308
  78.4 326.8 %all-gather.21.cloned.1.call-start = ((), (), s32[]{:S(2)}) async-start(), calls=%async_computation.20 | async-start | bytes 9437184 | tf_op jit(solution)/shard_map/all_gather | solution.py:179
  79.0 357.1 %all-gather.31.cloned.1.call-start = ((), (), s32[]{:S(2)}) async-start(), calls=%async_computation.26 | async-start | bytes 5242880 | tf_op jit(solution)/shard_map/all_gather | solution.py:345
  126.5 30.9 %all-to-all-start = ((bf16[256,4,512]{0,2,1:T(8,128)(2,1)}), bf16[256,4,512]{0,2,1:T(8,128)(2,1)}, u32[]{:S(2)}, u32[]{:S(2)}) async-start(bf16[256,4,512]{0,2,1:T(8,128)(2,1)} %bitcast.120), calls=%async_computation | async-start | bytes 2097152 | tf_op jit(solution)/shard_map/all_to_all | solution.py:323
  131.1 305.0 %all-gather.29.cloned.1.call-start = ((), (), s32[]{:S(2)}) async-start(), calls=%async_computation.24 | async-start | bytes 6488064 | tf_op jit(solution)/shard_map/all_gather | solution.py:179
  132.0 429.0 %all-gather.23.cloned.1.call-start = ((), (), s32[]{:S(2)}) async-start(), calls=%async_computation.21 | async-start | bytes 10485760 | tf_op jit(solution)/shard_map/all_gather | solution.py:338
  164.9 7.0 copy-start.2
  171.9 4.7 copy-start.3
  192.1 5.8 copy-start.2
  197.9 4.7 copy-start.3
  218.4 5.8 copy-start.2
  224.2 4.7 copy-start.3
  244.4 5.8 copy-start.2
  250.2 4.7 copy-start.3
  270.3 5.8 copy-start.2
  276.1 4.7 copy-start.3
  296.8 6.5 copy-start.2
  303.3 4.7 copy-start.3
  323.6 5.8 copy-start.2
  349.5 5.8 copy-start.2
  370.5 34.7 %copy-start.13 = (bf16[1024,512]{1,0:T(8,128)(2,1)}, bf16[1024,512]{1,0:T(8,128)(2,1)S(1)}, u32[]{:S(2)}) copy-start(bf16[1024,512]{1,0:T(8,128)(2,1)S(1)} %get-tuple-element.776) | copy-start | bytes 3145732
  370.5 34.7 %copy-start.14 = (s32[4096]{0:T(1024)}, s32[4096]{0:T(1024)S(1)}, u32[]{:S(2)}) copy-start(s32[4096]{0:T(1024)S(1)} %get-tuple-element.786) | copy-start | bytes 49156
  370.5 34.7 %copy-start.8 = (bf16[256,2048]{1,0:T(8,128)(2,1)S(1)}, bf16[256,2048]{1,0:T(8,128)(2,1)}, u32[]{:S(2)}) copy-start(bf16[256,2048]{1,0:T(8,128)(2,1)} %param.16) | copy-start | bytes 3145732
  411.4 359.7 %copy-start.6 = (f32[256,2048]{1,0:T(8,128)}, f32[256,2048]{1,0:T(8,128)S(1)}, u32[]{:S(2)}) copy-start(f32[256,2048]{1,0:T(8,128)S(1)} %get-tuple-element.525) | copy-start | bytes 6291460
  413.1 193.0 %all-gather.27.cloned.1.call-start = ((), (), s32[]{:S(2)}) async-start(), calls=%async_computation.23 | async-start | bytes 6488064 | tf_op jit(solution)/shard_map/all_gather | solution.py:158
  419.8 7.0 copy-start.34
  419.8 232.4 %all-gather.25.cloned.1.call-start = ((), (), s32[]{:S(2)}) async-start(), calls=%async_computation.22 | async-start | bytes 6488064 | tf_op jit(solution)/shard_map/all_gather | solution.py:157
  426.7 342.7 %reduce-scatter.13.cloned.1.call-start = ((), (), s32[]{:S(2)}) async-start(), calls=%async_computation.27 | async-start | bytes 5242880 | tf_op jit(solution)/shard_map/reduce_scatter | solution.py:183
  652.2 17.0 copy-start.33
  669.3 10.7 copy-start.32
  669.3 10.7 copy-start.38
  692.5 78.6 %copy-start.16 = (bf16[256,2048]{1,0:T(8,128)(2,1)S(1)}, bf16[256,2048]{1,0:T(8,128)(2,1)}, u32[]{:S(2)}) copy-start(bf16[256,2048]{1,0:T(8,128)(2,1)} %param.18) | copy-start | bytes 3145732
  772.9 6.5 copy-start.10
  779.4 32.8 %copy-start.4 = (bf16[4096,128]{1,0:T(8,128)(2,1)S(1)}, bf16[4096,128]{1,0:T(8,128)(2,1)}, u32[]{:S(2)}) copy-start(bf16[4096,128]{1,0:T(8,128)(2,1)} %get-tuple-element.770) | copy-start | bytes 3145732
  780.5 30.6 %all-to-all-start.3 = ((bf16[256,4,512]{2,0,1:T(8,128)(2,1)}), bf16[256,4,512]{2,0,1:T(8,128)(2,1)}, u32[]{:S(2)}, u32[]{:S(2)}) async-start(bf16[256,4,512]{2,0,1:T(8,128)(2,1)} %bitcast.105), calls=%async_computation.5 | async-start | bytes 2097152 | tf_op jit(solution)/shard_map/all_to_all | solution.py:362
  784.7 384.3 %reduce-scatter.15.cloned.1.call-start = ((), (), s32[]{:S(2)}) async-start(), calls=%async_computation.28 | async-start | bytes 1310720 | tf_op jit(solution)/shard_map/reduce_scatter | solution.py:366
  1132.6 112.2 %reduce-scatter.25.cloned.1.call-start = ((), (), s32[]{:S(2)}) async-start(), calls=%async_computation.33 | async-start | bytes 6488064 | tf_op jit(solution)/shard_map/reduce_scatter | solution.py:404
  1143.8 138.9 %reduce-scatter.27.cloned.1.call-start = ((), (), s32[]{:S(2)}) async-start(), calls=%async_computation.34 | async-start | bytes 6488064 | tf_op jit(solution)/shard_map/reduce_scatter | solution.py:407
  1156.5 189.2 %reduce-scatter.29.cloned.1.call-start = ((), (), s32[]{:S(2)}) async-start(), calls=%async_computation.35 | async-start | bytes 6488064 | tf_op jit(solution)/shard_map/reduce_scatter | solution.py:410
  1168.9 12.6 copy-start.24
  1168.9 12.6 copy-start.26
  1168.9 12.7 copy-start.9
  1168.9 12.7 copy-start.28
  1169.0 12.7 copy-start.30
  1169.0 216.1 %reduce-scatter.19.cloned.1.call-start = ((), (), s32[]{:S(2)}) async-start(), calls=%async_computation.30 | async-start | bytes 1179648 | tf_op jit(solution)/shard_map/reduce_scatter | solution.py:395
  1183.2 241.3 %reduce-scatter.21.cloned.1.call-start = ((), (), s32[]{:S(2)}) async-start(), calls=%async_computation.31 | async-start | bytes 1179648 | tf_op jit(solution)/shard_map/reduce_scatter | solution.py:398
  1185.1 314.4 %reduce-scatter.23.cloned.1.call-start = ((), (), s32[]{:S(2)}) async-start(), calls=%async_computation.32 | async-start | bytes 9437184 | tf_op jit(solution)/shard_map/reduce_scatter | solution.py:401
  1192.0 382.2 %reduce-scatter.17.cloned.1.call-start = ((), (), s32[]{:S(2)}) async-start(), calls=%async_computation.29 | async-start | bytes 9437184 | tf_op jit(solution)/shard_map/reduce_scatter | solution.py:392
  1232.7 420.6 %reduce-scatter.11.cloned.1.call-start = ((), (), s32[]{:S(2)}) async-start(), calls=%async_computation.25 | async-start | bytes 5242880 | tf_op jit(solution)/shard_map/reduce_scatter | solution.py:183
  1244.5 793.7 %all-reduce.11.cloned.1.call-start = ((), (), s32[]{:S(2)}) async-start(), calls=%async_computation.36 | async-start | bytes 22020096 | tf_op jit(solution)/shard_map/psum | solution.py:431
  1574.3 79.0 %copy-start.7 = (f32[256,2048]{1,0:T(8,128)S(1)}, f32[256,2048]{1,0:T(8,128)}, u32[]{:S(2)}) copy-start(f32[256,2048]{1,0:T(8,128)} %copy-done.6) | copy-start | bytes 6291460
  1655.9 5.9 copy-start.21
  1663.0 31.0 %copy-start.12 = (f32[256,2048]{1,0:T(8,128)S(1)}, f32[256,2048]{1,0:T(8,128)}, u32[]{:S(2)}) copy-start(f32[256,2048]{1,0:T(8,128)} %copy-done.10) | copy-start | bytes 6291460
  2038.1 6.1 copy-start.20
  2045.8 5.3 copy-start.19
  2054.7 5.3 copy-start.1
  (20 other events, 50.3 us)
Sparse Core Ops, SparseCore 0:
  9.9 26.1 all-gather.14
  38.0 23.4 all-gather.16
  63.4 54.3 all-gather.12
  119.8 16.7 all-gather.18
  138.3 54.3 all-gather.20
  194.2 80.7 all-gather.30
  277.4 41.8 all-gather.28
  413.2 147.7 all-gather.22
  563.5 42.5 all-gather.26
  607.8 44.3 all-gather.24
  692.6 76.7 reduce-scatter.12
  1132.7 23.6 reduce-scatter.14
  1160.3 59.0 reduce-scatter.24
  1223.7 58.9 reduce-scatter.26
  1286.6 59.0 reduce-scatter.28
  1349.1 36.0 reduce-scatter.18
  1388.5 36.0 reduce-scatter.20
  1428.2 71.2 reduce-scatter.22
  1503.0 71.2 reduce-scatter.16
  1576.5 76.7 reduce-scatter.10
  1657.9 380.2 all-reduce.10
where the time goes:
time: 2080 us; the launch traced here: 2070 us
  waiting for transfers between devices  1130 us (54%)
  matrix products  495 us (24%)
  other arithmetic  164 us (8%)
  blocking collectives  130 us (6%)
  local copies, waits for them, and re-layouts  123 us (6%)
    psum x1, waiting for transfers between devices, on_device(): lax.psum(gate_owned.astype(jnp.bfloat16), 'seq').astype(jnp.float32)  341 us
    dot_general x31, matrix products, inner_columns(): lax.dot_general(left, right, (((1,), (1,)), ((), ())), preferred_element_...  236 us
    dot_general x23, matrix products, product(): return jnp.dot(left, right, preferred_element_type=jnp.float32)  159 us
    reduce_scatter x2, waiting for transfers between devices, sum_shares(): lax.psum_scatter(shares.astype(jnp.bfloat16), 'seq', scatter_dimension=0,...  154 us
    all_gather x1, waiting for transfers between devices, on_device(): feed_normed = lax.all_gather(second_normed, 'seq', axis=0, tiled=True)  113 us
    dot_general x23, matrix products, inner_rows(): lax.dot_general(left, right, (((0,), (0,)), ((), ())), preferred_element_...  99.6 us
    reduce_scatter x1, waiting for transfers between devices, on_device(): lax.psum_scatter(output_gradient.astype(jnp.bfloat16), ('dp', 'ctx'), sca...  75 us
    reduce_scatter x1, waiting for transfers between devices, on_device(): lax.psum_scatter(query_gradient.astype(jnp.bfloat16), ('dp', 'ctx'), scat...  74.8 us
  transfers between devices with their start and end apart: 23, of which 17 were waited for; matrix products, arithmetic and copies ran while one was open for 16% of the time, Pallas kernels for 0%

commit v1 on v0

v1 whole, which is shorter than its diff:
```python
from functools import partial

import jax
import jax.numpy as jnp
from jax import lax
from jax.experimental import pallas as pl
from jax.experimental.pallas import tpu as pltpu
from jax.sharding import PartitionSpec as P

HEADS = 32
KV_HEADS = 4
HEAD_DIM = 64
BLOCK = 256

epsilon = 1e-05
rotary_base = 10000.0
log2_e = 1.4426950408889634
ln_2 = 0.6931471805599453
bf16, f32 = jnp.bfloat16, jnp.float32
PLANE = ("dp", "ctx")
GROUP = ("seq", "ctx")
NT = (((1,), (1,)), ((), ()))
NN = (((1,), (0,)), ((), ()))
TN = (((0,), (0,)), ((), ()))


def dot(left, right, dims=NN):
    return lax.dot_general(left, right, dims, preferred_element_type=f32)


def normalize(features):
    inverse_rms = lax.rsqrt(jnp.mean(features * features, axis=-1, keepdims=True) + epsilon)
    return (features * inverse_rms, inverse_rms)


def norm_backward(slopes, normed, inverse_rms):
    return inverse_rms * (slopes - normed * jnp.mean(slopes * normed, axis=-1, keepdims=True))


def angles_of(places):
    lane = jnp.arange(2 * HEAD_DIM)
    exponent = (lane % (HEAD_DIM // 2)).astype(f32) * (2.0 / HEAD_DIM)
    frequency = rotary_base ** (-exponent)
    angles = places[:, None] * frequency[None, :]
    sign = jnp.where(lane % HEAD_DIM < HEAD_DIM // 2, -1.0, 1.0)
    return jnp.cos(angles), jnp.sin(angles) * sign


def tie(*values):
    return lax.optimization_barrier(values)


def swap(values, mask, axes=PLANE):
    count = lax.axis_size(axes)
    return lax.ppermute(values, axes, [(i, i ^ mask) for i in range(count)])


def halves(count):
    return (slice(0, count // 2), slice(count // 2, count))


class ChipGather:
    def __init__(self, own):
        self.own = own

    def first(self):
        self.ends = {}
        r = 1
        while r < lax.axis_size(PLANE) // 2:
            self.ends[r] = swap(self.own, r << 1)
            r *= 2

    def second(self):
        top, bottom = halves(self.own.shape[0])
        parts = {r: (values[top], values[bottom]) for r, values in self.ends.items()}
        for r in range(1, lax.axis_size(PLANE) // 2):
            low, high = r & -r, 1 << (r.bit_length() - 1)
            if low != high:
                first = swap(parts[r ^ low][0], low << 1)
                parts[r] = (first, swap(parts[r ^ high][1], high << 1))
        self.rest = {r: both for r, both in parts.items() if r not in self.ends}

    def chunks(self):
        half = self.own.shape[0] // 2
        chunks = [(0, 0, self.own)]
        for r in range(1, lax.axis_size(PLANE) // 2):
            if r in self.ends:
                chunks.append((r, 0, self.ends[r]))
            else:
                chunks += [(r, 0, self.rest[r][0]), (r, half, self.rest[r][1])]
        return chunks

    def result(self):
        return jnp.concatenate([values for _, _, values in self.chunks()], axis=0)


def add(left, right):
    return (left.astype(f32) + right.astype(f32)).astype(bf16)


def to_chips(blocks):
    return [block if r == 0 else swap(block, r << 1) for r, block in enumerate(blocks)]


def add_all(values):
    total = values[0].astype(f32)
    for other in values[1:]:
        total = total + other.astype(f32)
    return total


def gather_plane(own):
    rows = own.shape[0]
    owner = lax.axis_index(PLANE)
    full = jnp.zeros((rows * lax.axis_size(PLANE), own.shape[1]), own.dtype)
    gather = ChipGather(own)
    gather.first()
    gather.second()
    for r, first, chunk in gather.chunks():
        other = swap(chunk, 1)
        full = lax.dynamic_update_slice_in_dim(full, chunk, (owner ^ (2 * r)) * rows + first, 0)
        full = lax.dynamic_update_slice_in_dim(full, other, (owner ^ (2 * r + 1)) * rows + first, 0)
    return full


class LaneSum:
    def __init__(self, values):
        owners = lax.axis_size(PLANE)
        owner = lax.axis_index(PLANE)
        rows = values.shape[0] // owners
        self.kept, self.came = [], []
        for r in range(owners // 2):
            away = lax.dynamic_slice_in_dim(values, (owner ^ (2 * r + 1)) * rows, rows, 0)
            self.kept.append(lax.dynamic_slice_in_dim(values, (owner ^ (2 * r)) * rows, rows, 0))
            self.came.append(swap(away, 1))

    def blocks(self):
        return [add(kept, came) for kept, came in zip(self.kept, self.came)]


class LineSum:
    def __init__(self, share):
        self.share = share
        self.moving = lax.ppermute(self.share, "seq", [(0, 1), (3, 2)])

    def across(self):
        self.share = add(self.share, self.moving)
        self.moving = lax.ppermute(self.share, "seq", [(1, 2), (2, 1)])

    def outwards(self):
        self.share = add(self.share, self.moving)
        self.moving = lax.ppermute(self.share, "seq", [(1, 0), (2, 3)])

    def result(self):
        place = lax.axis_index("seq")
        inner = (place == 1) | (place == 2)
        return jnp.where(inner, self.share, self.moving).astype(f32)


def gather_group(line):
    rows = []
    for piece in line:
        rows += [piece, swap(piece, 2, "ctx")]
    pairs = [jnp.concatenate(rows[2 * i : 2 * i + 2], axis=0) for i in range(4)]
    others = [swap(pair, 1, "ctx") for pair in pairs]
    return jnp.concatenate([half for both in zip(pairs, others) for half in both], axis=0)


class GroupSum:
    def __init__(self, values):
        shaped = values.reshape(4, 2, 2, -1, values.shape[1])
        self.kept, self.came = shaped[:, 0], swap(shaped[:, 1], 1, "ctx")

    def along_x(self):
        pair = add(self.kept, self.came)
        self.kept, self.came = pair[:, 0], swap(pair[:, 1], 2, "ctx")

    def along_seq(self):
        line = add(self.kept, self.came)
        self.kept, self.came = line[0], [swap(line[m], m, "seq") for m in (1, 2, 3)]

    def result(self):
        total = self.kept.astype(f32)
        for values in self.came:
            total = total + values.astype(f32)
        return total


def spread(rows):
    count = lax.axis_size(GROUP)
    shaped = rows.reshape(count, -1, rows.shape[1])
    return lax.all_to_all(shaped, GROUP, 0, 0, tiled=True).reshape(rows.shape)


def place_body(at_ref, values_ref, gate_ref, up_ref):
    count = gate_ref.shape[1]
    gate_ref[...] = values_ref[0, :, :count].astype(f32)
    up_ref[...] = values_ref[0, :, count:].astype(f32)


def place_columns(values, at):
    chips, rows, both = values.shape
    count = both // 2
    if count % 128:
        gate = jnp.zeros((rows, chips * count), f32)
        up = jnp.zeros((rows, chips * count), f32)
        for r in range(chips):
            block, start = values[r].astype(f32), (at ^ r) * count
            gate = lax.dynamic_update_slice_in_dim(gate, block[:, :count], start, 1)
            up = lax.dynamic_update_slice_in_dim(up, block[:, count:], start, 1)
        return gate, up
    shape = jax.ShapeDtypeStruct((rows, chips * count), f32)
    return pl.pallas_call(
        place_body,
        grid_spec=pltpu.PrefetchScalarGridSpec(
            num_scalar_prefetch=1,
            grid=(chips,),
            in_specs=[pl.BlockSpec((1, rows, both), lambda t, at_ref: (at_ref[0] ^ t, 0, 0))],
            out_specs=[pl.BlockSpec((rows, count), lambda t, at_ref: (0, t))] * 2,
        ),
        out_shape=(shape, shape),
        cost_estimate=pl.CostEstimate(
            flops=0, bytes_accessed=10 * chips * rows * both // 2, transcendentals=0
        ),
        compiler_params=pltpu.CompilerParams(vmem_limit_bytes=24 * 1024 * 1024),
        name="place_columns",
    )(at.astype(jnp.int32)[None], values)


def stack_heads(block, heads, rows, first):
    return jnp.concatenate(
        [
            block[b * rows : (b + 1) * rows, (first + h) * HEAD_DIM : (first + h + 1) * HEAD_DIM]
            for b in range(2)
            for h in range(heads)
        ],
        axis=0,
    )


def spread_heads(stacked, heads, rows, b):
    return jnp.concatenate(
        [stacked[(b * heads + h) * rows : (b * heads + h + 1) * rows] for h in range(heads)], axis=1
    )


def forward_body(
    q_ref, kv_ref, o_ref, ot_ref, lse_ref, kvt, qs, m_s, l_s, *, groups, heads, rows, blocks
):
    c = pl.program_id(0)
    keys = kv_ref.shape[0] * rows
    width = 2 * heads * rows
    half = heads * rows

    @pl.when(c == 0)
    def _():
        def one(kt, carry):
            for g in range(groups):
                tile = kv_ref[:, kt, :, g * 128 : (g + 1) * 128].reshape(keys, 128)
                kvt[g, kt] = tile.astype(f32).T.astype(bf16)[HEAD_DIM:]
            return carry

        lax.fori_loop(0, blocks, one, 0)

    for g in range(groups):
        q = stack_heads(q_ref[...], heads, rows, g * heads)
        qs[g] = jnp.concatenate([q, jnp.zeros((width, HEAD_DIM), bf16)], axis=1)

    def tiles(kt, lo, first):
        scores = []
        for g in range(groups):
            kv = kv_ref[:, kt, :, g * 128 : (g + 1) * 128].reshape(keys, 128)
            scores.append(dot(kv, qs[g, lo:], NT))
        for g in range(groups):
            st = scores[g]
            peak = jnp.max(st, axis=0, keepdims=True)
            if not first:
                m_old = m_s[g, :, lo:]
                peak = jnp.maximum(m_old, peak)
            p = jnp.exp2(st - peak)
            total = jnp.sum(p, axis=0, keepdims=True)
            pv = dot(kvt[g, kt], p.astype(bf16))
            if first:
                l_s[g, :, lo:] = total
                ot_ref[0, g, :, lo:] = pv
            else:
                shrink = jnp.exp2(m_old - peak)
                l_s[g, :, lo:] = l_s[g, :, lo:] * shrink + total
                ot_ref[0, g, :, lo:] = ot_ref[0, g, :, lo:] * shrink + pv
            m_s[g, :, lo:] = peak

    def step(kt, carry):
        tiles(kt, 0, False)
        return carry

    tiles(0, 0, True)
    lax.fori_loop(1, 2 * c + 1, step, 0)
    tiles(2 * c + 1, half, False)
    for g in range(groups):
        total = l_s[g]
        o = ot_ref[0, g] / total
        ot_ref[0, g] = o
        lse_ref[0, g : g + 1, :] = m_s[g] + jnp.log2(total)
        stacked = o.T.astype(bf16)
        for b in range(2):
            o_ref[b * rows : (b + 1) * rows, g * heads * HEAD_DIM : (g + 1) * heads * HEAD_DIM] = (
                spread_heads(stacked, heads, rows, b)
            )


def attend_forward(q, kv, first, groups):
    devices, blocks, rows, kv_width = kv.shape
    heads = q.shape[1] * 128 // HEAD_DIM // kv_width
    wide = heads * HEAD_DIM * groups
    width = 2 * heads * rows
    pairs = blocks // 2
    keys = devices * rows
    tiles = groups * blocks * (blocks + 1) // 2
    at = first // groups
    return pl.pallas_call(
        partial(forward_body, groups=groups, heads=heads, rows=rows, blocks=blocks),
        grid=(pairs,),
        out_shape=(
            jax.ShapeDtypeStruct((q.shape[0], wide), bf16),
            jax.ShapeDtypeStruct((pairs, groups, HEAD_DIM, width), f32),
            jax.ShapeDtypeStruct((pairs, groups, width), f32),
        ),
        in_specs=[
            pl.BlockSpec((2 * rows, wide), lambda c: (c, at)),
            pl.BlockSpec((devices, blocks, rows, groups * 128), lambda c: (0, 0, 0, at)),
        ],
        out_specs=(
            pl.BlockSpec((2 * rows, wide), lambda c: (c, 0)),
            pl.BlockSpec((1, groups, HEAD_DIM, width), lambda c: (c, 0, 0, 0)),
            pl.BlockSpec((1, groups, width), lambda c: (c, 0, 0)),
        ),
        scratch_shapes=[
            pltpu.VMEM((groups, blocks, HEAD_DIM, keys), bf16),
            pltpu.VMEM((groups, width, 128), bf16),
            pltpu.VMEM((groups, 1, width), f32),
            pltpu.VMEM((groups, 1, width), f32),
        ],
        compiler_params=pltpu.CompilerParams(vmem_limit_bytes=40 * 1024 * 1024),
        cost_estimate=pl.CostEstimate(
            flops=tiles * keys * width * 128 * 8,
            bytes_accessed=6 * 1024 * 1024,
            transcendentals=tiles * keys * width // 2,
        ),
        name="attend_forward",
    )(q, kv)


def backward_body(
    q_ref,
    do_ref,
    kv_ref,
    ot_ref,
    lse_ref,
    dq_ref,
    dkv_ref,
    kt_s,
    qs,
    dos,
    d_s,
    dqt,
    acc,
    *,
    groups,
    heads,
    rows,
    blocks,
    start,
):
    c = pl.program_id(0) + start
    devices = kv_ref.shape[0]
    keys = devices * rows
    width = 2 * heads * rows
    half = heads * rows

    @pl.when(c == start)
    def _():
        def one(kt, carry):
            for g in range(groups):
                tile = kv_ref[:, kt, :, g * 128 : (g + 1) * 128].reshape(keys, 128)
                kt_s[g, kt] = tile.astype(f32).T.astype(bf16)[:HEAD_DIM]
                acc[g, kt] = jnp.zeros((keys, 128), f32)
            return carry

        lax.fori_loop(0, blocks, one, 0)

    zero = jnp.zeros((width, HEAD_DIM), bf16)
    for g in range(groups):
        q = stack_heads(q_ref[...], heads, rows, g * heads)
        do = stack_heads(do_ref[...], heads, rows, g * heads)
        qs[g] = jnp.concatenate([q, zero], axis=1)
        dos[g] = jnp.concatenate([zero, do], axis=1)
        d_s[g] = jnp.sum(do.astype(f32).T * ot_ref[0, g], axis=0, keepdims=True)
        dqt[g] = jnp.zeros((HEAD_DIM, width), f32)

    def tiles(kt, lo):
        kvs = [
            kv_ref[:, kt, :, g * 128 : (g + 1) * 128].reshape(keys, 128) for g in range(groups)
        ]
        sts = [dot(kvs[g], qs[g, lo:], NT) for g in range(groups)]
        dpts = [dot(kvs[g], dos[g, lo:], NT) for g in range(groups)]
        ps = [jnp.exp2(sts[g] - lse_ref[0, g : g + 1, lo:]) for g in range(groups)]
        dss = [(ps[g] * (dpts[g] - d_s[g, :, lo:])).astype(bf16) for g in range(groups)]
        for g in range(groups):
            dqt[g, :, lo:] += dot(kt_s[g, kt], dss[g])
        for g in range(groups):
            acc[g, kt] += dot(dss[g], qs[g, lo:]) + dot(ps[g].astype(bf16), dos[g, lo:])

    def step(kt, carry):
        tiles(kt, 0)
        return carry

    lax.fori_loop(0, 2 * c + 1, step, 0)
    tiles(2 * c + 1, half)
    for g in range(groups):
        dq = (dqt[g] * (HEAD_DIM**-0.5)).T.astype(bf16)
        for b in range(2):
            dq_ref[b * rows : (b + 1) * rows, g * heads * HEAD_DIM : (g + 1) * heads * HEAD_DIM] = (
                spread_heads(dq, heads, rows, b)
            )

    @pl.when(c == start + pl.num_programs(0) - 1)
    def _():
        column = lax.broadcasted_iota(jnp.int32, (1, 128), 1)
        factor = jnp.where(column < HEAD_DIM, ln_2, 1.0)

        def one(kt, carry):
            for g in range(groups):
                dkv_ref[:, kt, :, g * 128 : (g + 1) * 128] = (
                    (acc[g, kt] * factor).astype(bf16).reshape(devices, rows, 128)
                )
            return carry

        lax.fori_loop(0, blocks, one, 0)


def attend_backward(q, do, kv, ot, lse, start, count):
    groups = KV_HEADS
    devices, blocks, rows, kv_width = kv.shape
    heads = q.shape[1] * 128 // HEAD_DIM // kv_width
    wide = heads * HEAD_DIM * groups
    width = 2 * heads * rows
    keys = devices * rows
    tiles = groups * sum(4 * c + 3 for c in range(start, start + count))
    kv_shape = (devices, blocks, rows, groups * 128)
    return pl.pallas_call(
        partial(backward_body, groups=groups, heads=heads, rows=rows, blocks=blocks, start=start),
        grid=(count,),
        out_shape=(
            jax.ShapeDtypeStruct((2 * rows * count, wide), bf16),
            jax.ShapeDtypeStruct(kv_shape, bf16),
        ),
        in_specs=[
            pl.BlockSpec((2 * rows, wide), lambda c: (c + start, 0)),
            pl.BlockSpec((2 * rows, wide), lambda c: (c + start, 0)),
            pl.BlockSpec(kv_shape, lambda c: (0, 0, 0, 0)),
            pl.BlockSpec((1, groups, HEAD_DIM, width), lambda c: (c + start, 0, 0, 0)),
            pl.BlockSpec((1, groups, width), lambda c: (c + start, 0, 0)),
        ],
        out_specs=(
            pl.BlockSpec((2 * rows, wide), lambda c: (c, 0)),
            pl.BlockSpec(kv_shape, lambda c: (0, 0, 0, 0)),
        ),
        scratch_shapes=[
            pltpu.VMEM((groups, blocks, HEAD_DIM, keys), bf16),
            pltpu.VMEM((groups, width, 128), bf16),
            pltpu.VMEM((groups, width, 128), bf16),
            pltpu.VMEM((groups, 1, width), f32),
            pltpu.VMEM((groups, HEAD_DIM, width), f32),
            pltpu.VMEM((groups, blocks, keys, 128), f32),
        ],
        compiler_params=pltpu.CompilerParams(vmem_limit_bytes=40 * 1024 * 1024),
        cost_estimate=pl.CostEstimate(
            flops=tiles * keys * width * 128 * 10,
            bytes_accessed=8 * 1024 * 1024,
            transcendentals=tiles * keys * width // 2,
        ),
        name="attend_backward",
    )(q, do, kv, ot, lse)


def turn_lanes(values, cosine, sine):
    count, width = values.shape
    lane = lax.broadcasted_iota(jnp.int32, (count, width), 1) % HEAD_DIM
    half_width = HEAD_DIM // 2
    other = jnp.where(
        lane < half_width,
        pltpu.roll(values, width - half_width, 1),
        pltpu.roll(values, half_width, 1),
    )
    times = width // cosine.shape[1]
    return values * jnp.tile(cosine, (1, times)) + other * jnp.tile(sine, (1, times))


def project_body(x_ref, w_ref, cosine_ref, sine_ref, out_ref, *, scale):
    values = dot(x_ref[...], w_ref[...])
    out_ref[...] = (turn_lanes(values, cosine_ref[...], sine_ref[...]) * scale).astype(bf16)


def project(x, weight, cosine, sine, scale, width):
    count, depth = x.shape
    tile = min(width, 512)
    return pl.pallas_call(
        partial(project_body, scale=scale),
        grid=(width // tile,),
        out_shape=jax.ShapeDtypeStruct((count, width), bf16),
        in_specs=[
            pl.BlockSpec((count, depth), lambda i: (0, 0)),
            pl.BlockSpec((depth, tile), lambda i: (0, i)),
            pl.BlockSpec(cosine.shape, lambda i: (0, 0)),
            pl.BlockSpec(sine.shape, lambda i: (0, 0)),
        ],
        out_specs=pl.BlockSpec((count, tile), lambda i: (0, i)),
        compiler_params=pltpu.CompilerParams(vmem_limit_bytes=24 * 1024 * 1024),
        cost_estimate=pl.CostEstimate(
            flops=2 * count * depth * width,
            bytes_accessed=2 * (count * depth + depth * width + count * width),
            transcendentals=0,
        ),
        name="project",
    )(x, weight, cosine, sine)


def turn_body(x_ref, cosine_ref, sine_ref, out_ref):
    values = x_ref[...].astype(f32)
    out_ref[...] = turn_lanes(values, cosine_ref[...], sine_ref[...]).astype(bf16)


def turn_back(x, cosine, sine):
    count, width = x.shape
    tile = min(width, 512)
    return pl.pallas_call(
        turn_body,
        grid=(width // tile,),
        out_shape=jax.ShapeDtypeStruct(x.shape, bf16),
        in_specs=[
            pl.BlockSpec((count, tile), lambda i: (0, i)),
            pl.BlockSpec(cosine.shape, lambda i: (0, 0)),
            pl.BlockSpec(sine.shape, lambda i: (0, 0)),
        ],
        out_specs=pl.BlockSpec((count, tile), lambda i: (0, i)),
        cost_estimate=pl.CostEstimate(
            flops=6 * count * width, bytes_accessed=4 * count * width, transcendentals=0
        ),
        name="turn_back",
    )(x, cosine, -sine)


def on_device(
    tokens,
    positions,
    cotangent,
    query_weight,
    key_weight,
    value_weight,
    output_weight,
    gate_weight,
    up_weight,
    down_weight,
    first_gain,
    second_gain,
):
    token_count, width = tokens.shape
    group = lax.axis_size(GROUP)
    owners = lax.axis_size(PLANE)
    owner = lax.axis_index(PLANE)
    lane = owner % 2
    chip = owner // 2
    chips = owners // 2
    rows = token_count // group
    own_rows = query_weight.shape[0]
    hidden_part = gate_weight.shape[1] // chips
    down_rows = down_weight.shape[0]
    kv_width = key_weight.shape[1]
    line = lax.axis_size("seq")
    line_place = lax.axis_index("seq")
    direct = [r for r in range(1, chips) if r & (r - 1) == 0]
    indirect = [r for r in range(1, chips) if r & (r - 1)]

    digits = jnp.stack([positions // 256, positions % 256], axis=1).astype(bf16)
    moved = spread(jnp.concatenate([tokens, jnp.pad(digits, ((0, 0), (0, 126)))], axis=1))
    by_head = (own_rows, KV_HEADS, 1, HEAD_DIM)
    gains = jnp.pad(jnp.stack([first_gain, second_gain], axis=1), ((0, 0), (0, 126)))
    pair_own = jnp.concatenate([key_weight.reshape(by_head), value_weight.reshape(by_head)], 2)
    pair_own = jnp.concatenate([pair_own.reshape(own_rows, 2 * kv_width), gains], axis=1)
    pair_weight = gather_plane(pair_own)
    query_full = lax.all_gather(query_weight, PLANE, axis=0, tiled=True)
    output_full = lax.all_gather(output_weight, PLANE, axis=0, tiled=True)
    scales = pair_weight[:, 2 * kv_width : 2 * kv_width + 2].astype(f32).T
    first_scale, second_scale = scales[0:1], scales[1:2]

    def columns(r, first, count):
        start = (chip ^ r) * hidden_part
        parts = []
        for weight in (gate_weight, up_weight):
            some = lax.dynamic_slice_in_dim(weight, first, count, 0)
            parts.append(lax.dynamic_slice_in_dim(some, start, hidden_part, 1))
        return jnp.concatenate(parts, axis=1)

    blocks = [columns(r, 0, own_rows) for r in range(chips)]

    places = moved[:, width].astype(f32) * 256.0 + moved[:, width + 1].astype(f32)
    cosine, sine = angles_of(places)
    is_key = jnp.arange(2 * HEAD_DIM) < HEAD_DIM
    pair_cosine, pair_sine = jnp.where(is_key, cosine, 1.0), jnp.where(is_key, sine, 0.0)
    inputs = moved[:, :width].astype(f32)
    first_normed, first_inverse = normalize(inputs)
    first_input = (first_normed * first_scale).astype(bf16)
    paired = project(first_input, pair_weight, pair_cosine, pair_sine, 1.0, 2 * kv_width)

    line_pairs = [paired] + [swap(paired, m, "seq") for m in (1, 2, 3)]
    both_full = jnp.broadcast_to(moved[0, 0] * 0.0, (own_rows * owners, 2 * hidden_part))
    line_pairs[0], both_full = tie(line_pairs[0], both_full)
    all_pairs = gather_group(line_pairs).reshape(group, group, rows, -1)
    query_scale = HEAD_DIM**-0.5 * log2_e
    queries = project(first_input, query_full, cosine, sine, query_scale, width)

    queries, all_pairs, blocks, cotangent, down_weight = tie(
        queries, all_pairs, blocks, cotangent, down_weight
    )
    blocks = to_chips(blocks)
    slopes = spread(cotangent)
    down_other = swap(down_weight, 1)
    own_other = swap(blocks[0], 1)
    attended, raw_outputs, log_sums = attend_forward(queries, all_pairs, 0, KV_HEADS)
    attended, down_other, own_other = tie(attended, down_other, own_other)

    middle = inputs + dot(attended, output_full)
    second_normed, second_inverse = normalize(middle)
    second_input = (second_normed * second_scale).astype(bf16)
    second_input, slopes = tie(second_input, slopes)
    feed_input = ChipGather(second_input)
    feed_input.first()
    both_full = lax.dynamic_update_slice_in_dim(both_full, blocks[0], owner * own_rows, 0)
    both_full = lax.dynamic_update_slice_in_dim(both_full, own_other, (owner ^ 1) * own_rows, 0)
    down_full = jnp.where(
        lane == 0,
        jnp.concatenate([down_weight, down_other], axis=0),
        jnp.concatenate([down_other, down_weight], axis=0),
    )
    feed_input.ends, blocks, both_full, down_full, slopes = tie(
        feed_input.ends, blocks, both_full, down_full, slopes
    )
    feed_input.second()
    feed_slope = ChipGather(slopes)
    feed_slope.first()
    for r in range(1, chips):
        other = swap(blocks[r], 1)
        both_full = lax.dynamic_update_slice_in_dim(
            both_full, blocks[r], (owner ^ (2 * r)) * own_rows, 0
        )
        both_full = lax.dynamic_update_slice_in_dim(
            both_full, other, (owner ^ (2 * r + 1)) * own_rows, 0
        )
    feed_slope.ends, feed_input.rest = tie(feed_slope.ends, feed_input.rest)
    feed_slope.second()
    feed_input = feed_input.result()

    gate_values = dot(feed_input, both_full[:, :hidden_part])
    up_values = dot(feed_input, both_full[:, hidden_part:])
    feed_slope.rest, up_values, gate_values = tie(feed_slope.rest, up_values, gate_values)
    feed_slope = feed_slope.result()
    hidden_slope = dot(feed_slope, down_full, NT)
    gate_sigmoid = jax.nn.sigmoid(gate_values)
    hidden = (gate_values * gate_sigmoid * up_values).astype(bf16)
    gate_slope = (
        hidden_slope * up_values * gate_sigmoid * (1.0 + gate_values * (1.0 - gate_sigmoid))
    ).astype(bf16)
    up_slope = (hidden_slope * gate_values * gate_sigmoid).astype(bf16)
    both_slope = jnp.concatenate([gate_slope, up_slope], axis=1)

    def by_chip(share):
        return [share[r * token_count : (r + 1) * token_count] for r in range(chips)]

    def for_chips(features):
        count = 2 * own_rows
        return [
            lax.dynamic_slice_in_dim(features, (chip ^ r) * count, count, 1) for r in range(chips)
        ]

    def swap_rows(share):
        count = share.shape[0] // 2
        kept = lax.dynamic_slice_in_dim(share, lane * count, count, 0)
        return kept, swap(lax.dynamic_slice_in_dim(share, (1 - lane) * count, count, 0), 1)

    feed_share = dot(both_slope, both_full, NT).astype(bf16)
    feed_share, both_slope, hidden = tie(feed_share, both_slope, hidden)
    second_parts = to_chips(by_chip(feed_share))
    down_rows_two = swap_rows(dot(hidden, feed_slope, TN).astype(bf16))
    both_slope, down_rows_two = tie(both_slope, down_rows_two)
    down_part = lax.psum_scatter(add(*down_rows_two), "seq", scatter_dimension=0, tiled=True)
    both_lanes = LaneSum(dot(feed_input, both_slope, TN).astype(bf16))
    both_stack = jnp.stack(both_lanes.blocks())
    second_parts, both_stack = tie(second_parts, both_stack)
    both_part = lax.psum_scatter(both_stack, "seq", scatter_dimension=1, tiled=True)
    second_slope = add_all(second_parts)
    second_gain_share = jnp.sum(second_slope * second_normed, axis=0)
    middle_slope = slopes.astype(f32) + norm_backward(
        second_slope * second_scale, second_normed, second_inverse
    )
    attention_slope = middle_slope.astype(bf16)
    attended_slope = dot(attention_slope, output_full, NT).astype(bf16)

    attended_slope, attention_slope, first_input, attended = tie(
        attended_slope, attention_slope, first_input, attended
    )
    slope_chunks = to_chips([attention_slope] * chips)
    attended_columns = to_chips(for_chips(attended))
    first_columns = to_chips(for_chips(first_input))
    query_turned, pair_terms = attend_backward(
        queries, attended_slope, all_pairs, raw_outputs, log_sums, 0, group // 2
    )
    query_turned, pair_terms, slope_chunks, attended_columns, first_columns, down_part = tie(
        query_turned, pair_terms, slope_chunks, attended_columns, first_columns, down_part
    )

    pair_slope = GroupSum(pair_terms.reshape(token_count * group, -1))
    down_sum = lax.all_gather(down_part, "seq", axis=0, tiled=True)
    query_slope = turn_back(query_turned, cosine, sine)
    query_side = dot(query_slope, query_full, NT)
    pair_slope.came, query_slope, query_side, both_part, hidden, slope_chunks = tie(
        pair_slope.came, query_slope, query_side, both_part, hidden, slope_chunks
    )
    pair_slope.along_x()
    both_part = to_chips([both_part[r] for r in range(chips)])
    out_share = dot(hidden, down_full).astype(bf16)
    output_share = dot(
        jnp.concatenate(attended_columns), jnp.concatenate(slope_chunks), TN
    ).astype(bf16)
    pair_slope.came, both_part, out_share, output_share, query_slope = tie(
        pair_slope.came, both_part, out_share, output_share, query_slope
    )
    pair_slope.along_seq()
    both_stack = jnp.stack(both_part)
    query_chunks = to_chips([query_slope] * chips)
    output_own = add(*swap_rows(output_share))
    pair_slope.came, output_own, both_stack, down_sum = tie(
        pair_slope.came, output_own, both_stack, down_sum
    )
    both_sums = lax.all_gather(both_stack, "seq", axis=1, tiled=True)
    outputs = LineSum(output_own)
    kv_slope = turn_back(pair_slope.result().astype(bf16), pair_cosine, pair_sine)
    first_slope = query_side + dot(kv_slope, pair_weight[:, : 2 * kv_width], NT)
    input_gradient = middle_slope + norm_backward(
        first_slope * first_scale, first_normed, first_inverse
    )
    gain_shares = jnp.stack([jnp.sum(first_slope * first_normed, axis=0), second_gain_share])
    input_gradient, kv_slope, gain_shares, query_chunks, outputs.moving = tie(
        input_gradient.astype(bf16),
        kv_slope,
        gain_shares.astype(bf16),
        query_chunks,
        outputs.moving,
    )
    kv_chunks = to_chips([kv_slope] * chips)
    gain_parts = to_chips(for_chips(gain_shares))
    outputs.across()
    first_columns = jnp.concatenate(first_columns)
    query_share = dot(first_columns, jnp.concatenate(query_chunks), TN).astype(bf16)
    query_own = add(*swap_rows(query_share))
    query_own, kv_chunks, gain_parts, outputs.moving, input_gradient, out_share = tie(
        query_own, kv_chunks, gain_parts, outputs.moving, input_gradient, out_share
    )
    outputs.outwards()
    squares = LineSum(query_own)
    input_gradient = spread(input_gradient)
    out_parts = to_chips(by_chip(out_share))
    kv_share = dot(first_columns, jnp.concatenate(kv_chunks), TN).astype(bf16)
    gain_two = swap_rows(add_all(gain_parts).T.astype(bf16))
    pairs = jnp.concatenate(
        [add(*swap_rows(kv_share)), jnp.pad(add(*gain_two), ((0, 0), (0, 126)))], axis=1
    )
    squares.moving, pairs, outputs.moving, input_gradient = tie(
        squares.moving, pairs, outputs.moving, input_gradient
    )
    squares.across()
    pairs = LineSum(pairs)
    squares.moving, pairs.moving, out_parts = tie(squares.moving, pairs.moving, out_parts)
    squares.outwards()
    pairs.across()
    layer_output = spread((middle + add_all(out_parts)).astype(bf16))
    squares.moving, pairs.moving = tie(squares.moving, pairs.moving)
    pairs.outwards()
    pairs.moving, both_sums, layer_output = tie(pairs.moving, both_sums, layer_output)

    input_gradient = input_gradient.astype(f32)
    down_gradient = down_sum.astype(f32)
    query_gradient, output_gradient = squares.result(), outputs.result()
    pairs = pairs.result()
    gain_gradients = pairs[:, 2 * kv_width : 2 * kv_width + 2].T
    pairs = pairs[:, : 2 * kv_width].reshape(own_rows, KV_HEADS, 2, HEAD_DIM)
    gate_gradient, up_gradient = place_columns(both_sums, chip)
    return (
        layer_output,
        input_gradient,
        query_gradient,
        pairs[:, :, 0].reshape(own_rows, kv_width),
        pairs[:, :, 1].reshape(own_rows, kv_width),
        output_gradient,
        gate_gradient,
        up_gradient,
        down_gradient,
        gain_gradients[0],
        gain_gradients[1],
    )


def solution(mesh):
    tokens = P(("dp", "seq", "ctx"), None)
    rows = P(PLANE, None)
    return jax.shard_map(
        on_device,
        mesh=mesh,
        in_specs=(tokens, P(("dp", "seq", "ctx")), tokens) + (rows,) * 7 + (P(PLANE),) * 2,
        out_specs=(tokens,) * 2 + (rows,) * 7 + (P(PLANE),) * 2,
        check_vma=False,
    )
```

time: 2080 us -> 944 us (0.45)
  waiting for transfers between devices: 1130 us -> 319 us
  matrix products: 495 us -> 114 us
  starting transfers between devices: 10.2 us -> 183 us
  Pallas kernels: 0 us -> 132 us
  blocking collectives: 130 us -> 0 us
  other arithmetic: 164 us -> 87.4 us
  local copies, waits for them, and re-layouts: 123 us -> 82.2 us
    reduce_scatter x10 -> x2, waiting for transfers between devices: 471 us -> 0.01 us  [the longest x1 0.01 us: on_device(): lax.psum_scatter(add(*down_rows_two), 'seq', scatter_dimension=0, tiled=T...]
    dot_general x77 -> x14, matrix products: 495 us -> 114 us  [dot(): return lax.dot_general(left, right, dims, preferred_element_type=f32)]
    psum x1 -> x0, waiting for transfers between devices: 341 us -> none  [on_device(): lax.psum(gate_owned.astype(jnp.bfloat16), 'seq').astype(jnp.float32)]
    ppermute x0 -> x86, waiting for transfers between devices: none -> 318 us  [the longest x77 226 us: swap(): return lax.ppermute(values, axes, [(i, i ^ mask) for i in range(count)])]
    all_gather x10 -> x4, waiting for transfers between devices: 261 us -> 0.02 us  [the longest x1 0.01 us: on_device(): output_full = lax.all_gather(output_weight, PLANE, axis=0, tiled=True)]
    pallas_call x0 -> x7, Pallas kernels: none -> 132 us  [the longest x1 70.2 us: attend_backward(): pl.pallas_call(partial(backward_body, groups=groups, heads=heads, rows=ro...]
    ppermute x0 -> x86, starting transfers between devices: none -> 92.4 us  [the longest x77 68.3 us: swap(): return lax.ppermute(values, axes, [(i, i ^ mask) for i in range(count)])]
    all_to_all x4 -> x0, blocking collectives: 83.5 us -> none  [the longest x1 29.7 us: on_device(): lax.all_to_all(head_outputs, 'seq', split_axis=0, concat_axis=1, tiled=True)]
  transfers between devices with their start and end apart: 23 -> 96, of which waited for: 17 -> 37; matrix products, arithmetic and copies ran while one was open for 16% -> 22% of each run, Pallas kernels for 0% -> 14%
where the time goes in v1:
time: 944 us; the launch traced here: 935 us
  waiting for transfers between devices  319 us (34%)
  starting transfers between devices  183 us (19%)
  Pallas kernels  132 us (14%)
  matrix products  114 us (12%)
  other arithmetic  87.4 us (9%)
  local copies, waits for them, and re-layouts  82.2 us (9%)
  between operations  16.8 us (2%)
    ppermute x77, waiting for transfers between devices, swap(): return lax.ppermute(values, axes, [(i, i ^ mask) for i in range(count)])  226 us
    dot_general x14, matrix products, dot(): return lax.dot_general(left, right, dims, preferred_element_type=f32)  114 us
    all_to_all x4, starting transfers between devices, spread(): return lax.all_to_all(shaped, GROUP, 0, 0, tiled=True).reshape(rows.shape)  90.2 us
    pallas_call x1, Pallas kernels, attend_backward(): pl.pallas_call(partial(backward_body, groups=groups, heads=heads, rows=ro...  70.2 us
    ppermute x77, starting transfers between devices, swap(): return lax.ppermute(values, axes, [(i, i ^ mask) for i in range(count)])  68.3 us
    ppermute x3, waiting for transfers between devices, outwards(): self.moving = lax.ppermute(self.share, 'seq', [(1, 0), (2, 3)])  62.5 us
    pallas_call x1, Pallas kernels, attend_forward(): pl.pallas_call(partial(forward_body, groups=groups, heads=heads, rows=row...  45.4 us
    unnamed x175, local copies, waits for them, and re-layouts  39.4 us
  transfers between devices with their start and end apart: 96, of which 37 were waited for; matrix products, arithmetic and copies ran while one was open for 22% of the time, Pallas kernels for 14%

profile of v1, /device:TPU:0, one launch (start us, length us, event | category | flops | bytes accessed | tf_op | source)
XLA Modules:
  0.0 935.4 jit_solution(10148098414049047787)
XLA Ops:
  19.1 5.0 all-to-all-start
  24.2 4.2 constant_dynamic-slice_fusion.23
  35.8 13.7 %collective-permute-done.5 = bf16[128,640]{1,0:T(8,128)(2,1)S(1)} collective-permute-done((bf16[128,640]{1,0:T(8,128)(2,1)S(1)}, bf16[128,640]{1,0:T(8,128)(2,1)S(1)}, u32[]{:S(2)}, u32[]{:S(2)}) %collective-permute-start.5) | collective-permute-done | bytes 163872 | tf_op jit(solution)/shard_map/ppermute | solution.py:55
  62.5 3.3 collective-permute-start.14
  67.0 5.0 broadcast_in_dim.44
  75.9 10.9 %collective-permute-done.9 = bf16[256,512]{1,0:T(8,128)(2,1)S(1)} collective-permute-done((bf16[256,512]{1,0:T(8,128)(2,1)S(1)}, bf16[256,512]{1,0:T(8,128)(2,1)S(1)}, u32[]{:S(2)}, u32[]{:S(2)}) %collective-permute-start.9) | collective-permute-done | bytes 262176 | tf_op jit(solution)/shard_map/ppermute | solution.py:55
  89.2 4.6 collective-permute-done.12
  93.9 5.5 collective-permute-done.15
  99.5 5.0 collective-permute-done.18
  108.6 3.4 copy-done.3
  112.0 4.7 project.2.q_ref
  118.1 4.7 all-to-all-start.1
  130.1 45.4 %attend_forward.1 = (bf16[256,2048]{1,0:T(8,128)(2,1)S(1)}, f32[8,4,64,256]{3,2,1,0:T(8,128)S(1)}, f32[8,4,256]{2,1,0:T(4,128)S(1)}) custom-call(bf16[256,2048]{1,0:T(8,128)(2,1)S(1)} %copy-done.10, bf16[16,16,16,512]{3,2,1,0:T(8,128)(2,1)S(1)} %bitcast.101), custom_call_target="tpu_custom_call" | custom-call | flops 36507222016 | bytes 6291456 | tf_op jit(solution)/shard_map/attend_forward/pallas_call | solution.py:320
  179.4 6.1 multiply_reduce_fusion.2
  194.1 5.8 maximum_select_fusion
  199.9 21.2 %collective-permute-done.26 = bf16[256,2816]{1,0:T(8,128)(2,1)} collective-permute-done((bf16[256,2816]{1,0:T(8,128)(2,1)}, bf16[256,2816]{1,0:T(8,128)(2,1)}, u32[]{:S(2)}, u32[]{:S(2)}) %collective-permute-start.26) | collective-permute-done | bytes 1441824 | tf_op jit(solution)/shard_map/ppermute | solution.py:55
  221.0 21.2 %collective-permute-done.22 = bf16[256,2048]{1,0:T(8,128)(2,1)S(1)} collective-permute-done((bf16[256,2048]{1,0:T(8,128)(2,1)}, bf16[256,2048]{1,0:T(8,128)(2,1)S(1)}, u32[]{:S(2)}, u32[]{:S(2)}) %collective-permute-start.22) | collective-permute-done | bytes 1048608 | tf_op jit(solution)/shard_map/ppermute | solution.py:55
  250.3 29.2 %collective-permute-done.29 = bf16[128,2048]{1,0:T(8,128)(2,1)S(1)} collective-permute-done((bf16[128,2048]{1,0:T(8,128)(2,1)S(1)}, bf16[128,2048]{1,0:T(8,128)(2,1)S(1)}, u32[]{:S(2)}, u32[]{:S(2)}) %collective-permute-start.29) | collective-permute-done | bytes 524320 | tf_op jit(solution)/shard_map/ppermute | solution.py:55
  291.6 9.2 fusion
  300.8 9.4 %fusion.2 = f32[1024,1408]{1,0:T(8,128)S(1)} fusion(bf16[1024,2048]{1,0:T(8,128)(2,1)S(1)} %constant_dynamic-update-slice_fusion.12, bf16[2048,2816]{1,0:T(8,128)(2,1)} %constant_dynamic-update-slice_fusion.26), kind=kOutput, calls=%fused_computation.4 | convolution fusion | flops 5905580032 | bytes 15728640 | tf_op jit(solution)/shard_map/dot_general | solution.py:28
  312.3 8.5 fusion.89
  320.8 6.4 multiply_convert_fusion
  330.1 16.3 %convolution_convert_fusion.2 = bf16[1024,2048]{1,0:T(8,128)(2,1)} fusion(bf16[2048,2816]{1,0:T(8,128)(2,1)} %constant_dynamic-update-slice_fusion.26, bf16[1024,1408]{1,0:T(8,128)(2,1)S(1)} %get-tuple-element.303, bf16[1024,1408]{1,0:T(8,128)(2,1)S(1)} %get-tuple-element.302), kind=kOutput, calls=%fused_computation.32 | convolution fusion | flops 11824791552 | bytes 21495808 | tf_op jit(solution)/shard_map/dot_general | solution.py:28
  346.5 9.3 convolution_convert_fusion.1
  356.8 5.3 collective-permute-done.39
  365.0 15.8 %convolution_convert_fusion = bf16[2048,2816]{1,0:T(8,128)(2,1)S(1)} fusion(bf16[1024,2048]{1,0:T(8,128)(2,1)} %copy-done.45, bf16[1024,2816]{1,0:T(8,128)(2,1)} %pad_maximum_fusion), kind=kOutput, calls=%fused_computation | convolution fusion | flops 11816927232 | bytes 21495808 | tf_op jit(solution)/shard_map/dot_general | solution.py:28
  391.8 5.3 fusion.42
  397.1 4.2 pad_maximum_fusion.1
  401.3 10.1 %collective-permute-done.36 = bf16[256,2048]{1,0:T(8,128)(2,1)} collective-permute-done((bf16[256,2048]{1,0:T(8,128)(2,1)}, bf16[256,2048]{1,0:T(8,128)(2,1)}, u32[]{:S(2)}, u32[]{:S(2)}) %collective-permute-start.36) | collective-permute-done | bytes 1048608 | tf_op jit(solution)/shard_map/ppermute | solution.py:55
  411.4 21.3 %collective-permute-done.37 = bf16[256,2048]{1,0:T(8,128)(2,1)} collective-permute-done((bf16[256,2048]{1,0:T(8,128)(2,1)}, bf16[256,2048]{1,0:T(8,128)(2,1)}, u32[]{:S(2)}, u32[]{:S(2)}) %collective-permute-start.37) | collective-permute-done | bytes 1048608 | tf_op jit(solution)/shard_map/ppermute | solution.py:55
  434.3 3.9 multiply_reduce_fusion
  438.3 4.6 fusion.83
  442.9 6.2 convolution_convert_fusion.4.do_ref
  455.0 3.6 collective-permute-done.47
  459.5 3.5 collective-permute-done.48
  466.5 3.3 collective-permute-done.50
  471.6 70.2 %attend_backward.1 = (bf16[256,2048]{1,0:T(8,128)(2,1)S(1)}, bf16[16,16,16,512]{3,2,1,0:T(8,128)(2,1)S(1)}) custom-call(bf16[256,2048]{1,0:T(8,128)(2,1)S(1)} %copy-done.11, bf16[256,2048]{1,0:T(8,128)(2,1)S(1)} %convolution_convert_fusion.4.do_ref, bf16[16,16,16,512]{3,2,1,0:T(8,128)(2,1)S(1)} %bitcast.102, f32[8,4,64,256]{3,2,1,0:T(8,128)S(1)} %copy-done.16, ...), custom_call_target="tpu_custom_call" | custom-call | flops 45634027520 | bytes 8388608 | tf_op jit(solution)/shard_map/attend_backward/pallas_call | solution.py:450
  551.3 4.1 turn_back.2
  557.6 7.9 fusion.90
  568.8 10.9 %convolution_convert_fusion.3 = bf16[1024,2048]{1,0:T(8,128)(2,1)} fusion(bf16[1024,1408]{1,0:T(8,128)(2,1)S(1)} %copy-done.28, bf16[1408,2048]{1,0:T(8,128)(2,1)} %copy-done.21), kind=kOutput, calls=%fused_computation.33 | convolution fusion | flops 5907677184 | bytes 12845056 | tf_op jit(solution)/shard_map/dot_general | solution.py:28
  583.5 3.6 fusion.28
  587.1 14.5 %collective-permute-done.55 = bf16[64,2816]{1,0:T(8,128)(2,1)S(1)} collective-permute-done((bf16[64,2816]{1,0:T(8,128)(2,1)S(1)}, bf16[64,2816]{1,0:T(8,128)(2,1)S(1)}, u32[]{:S(2)}, u32[]{:S(2)}) %collective-permute-start.55) | collective-permute-done | bytes 360480 | tf_op jit(solution)/shard_map/ppermute | solution.py:55
  601.7 7.4 collective-permute-done.57
  620.2 3.1 add_convert_fusion.11
  623.3 4.3 collective-permute-done.58
  628.9 8.6 collective-permute-done.59
  641.4 4.2 fusion.38
  645.5 7.1 collective-permute-start.65
  652.7 4.1 fusion.37
  656.8 3.4 collective-permute-done.63
  660.2 29.2 %collective-permute-done.65 = bf16[256,2048]{1,0:T(8,128)(2,1)S(1)} collective-permute-done((bf16[256,2048]{1,0:T(8,128)(2,1)}, bf16[256,2048]{1,0:T(8,128)(2,1)S(1)}, u32[]{:S(2)}, u32[]{:S(2)}) %collective-permute-start.65) | collective-permute-done | bytes 1048608 | tf_op jit(solution)/shard_map/ppermute | solution.py:144
  689.3 4.9 fusion.25
  705.3 7.5 collective-permute-done.72
  714.9 67.5 %all-to-all-start.2 = ((bf16[16,16,2048]{2,1,0:T(8,128)(2,1)}), bf16[16,16,2048]{2,1,0:T(8,128)(2,1)}, u32[]{:S(2)}, u32[]{:S(2)}) async-start(bf16[16,16,2048]{2,1,0:T(8,128)(2,1)} %bitcast.33), calls=%async_computation.4 | async-start | bytes 2097152 | tf_op jit(solution)/shard_map/all_to_all | solution.py:192
  787.1 5.6 collective-permute-start.74
  798.6 26.4 %collective-permute-done.77 = bf16[256,2048]{1,0:T(8,128)(2,1)S(1)} collective-permute-done((bf16[256,2048]{1,0:T(8,128)(2,1)S(1)}, bf16[256,2048]{1,0:T(8,128)(2,1)S(1)}, u32[]{:S(2)}, u32[]{:S(2)}) %collective-permute-start.77) | collective-permute-done | bytes 1048608 | tf_op jit(solution)/shard_map/ppermute | solution.py:152
  829.7 5.1 collective-permute-start.79
  834.8 10.8 %collective-permute-done.82 = bf16[256,2048]{1,0:T(8,128)(2,1)} collective-permute-done((bf16[256,2048]{1,0:T(8,128)(2,1)}, bf16[256,2048]{1,0:T(8,128)(2,1)}, u32[]{:S(2)}, u32[]{:S(2)}) %collective-permute-start.82) | collective-permute-done | bytes 1048608 | tf_op jit(solution)/shard_map/ppermute | solution.py:55
  847.3 3.6 add_convert_fusion.5
  851.0 12.9 %all-to-all-start.3 = ((bf16[16,16,2048]{2,1,0:T(8,128)(2,1)}), bf16[16,16,2048]{2,1,0:T(8,128)(2,1)S(1)}, u32[]{:S(2)}, u32[]{:S(2)}) async-start(bf16[16,16,2048]{2,1,0:T(8,128)(2,1)} %bitcast.108), calls=%async_computation.5 | async-start | bytes 2097152 | tf_op jit(solution)/shard_map/all_to_all | solution.py:192
  867.1 5.1 convert_element_type.409
  877.4 29.0 %collective-permute-done.83 = bf16[256,2048]{1,0:T(8,128)(2,1)} collective-permute-done((bf16[256,2048]{1,0:T(8,128)(2,1)S(1)}, bf16[256,2048]{1,0:T(8,128)(2,1)}, u32[]{:S(2)}, u32[]{:S(2)}) %collective-permute-start.83) | collective-permute-done | bytes 1048608 | tf_op jit(solution)/shard_map/ppermute | solution.py:152
  910.5 7.2 collective-permute-done.85
  922.7 4.4 place_columns.1
  (448 shorter events, 200.9 us)
Async XLA Ops:
  7.2 101.4 %all-gather.5.cloned.1.call-start = ((), (), s32[]{:S(2)}) async-start(), calls=%async_computation.6 | async-start | bytes 9437184 | tf_op jit(solution)/shard_map/all_gather | solution.py:591
  7.9 171.4 %all-gather.7.cloned.1.call-start = ((), (), s32[]{:S(2)}) async-start(), calls=%async_computation.7 | async-start | bytes 9437184 | tf_op jit(solution)/shard_map/all_gather | solution.py:592
  12.1 22.6 %collective-permute-start = (bf16[256,640]{1,0:T(8,128)(2,1)}, bf16[256,640]{1,0:T(8,128)(2,1)}, u32[]{:S(2)}, u32[]{:S(2)}) collective-permute-start(bf16[256,640]{1,0:T(8,128)(2,1)} %get-tuple-element.341), channel_id=1, source_target_pairs={{0,1},{1,0},{2,3},{3,2},{16,17},{17,16},{18,19},{19,18},{4,5},{5,4... | collective-permute-start | bytes 983048 | tf_op jit(solution)/shard_map/ppermute | solution.py:55
  12.6 19.4 %collective-permute-start.1 = (bf16[256,640]{1,0:T(8,128)(2,1)}, bf16[256,640]{1,0:T(8,128)(2,1)S(1)}, u32[]{:S(2)}, u32[]{:S(2)}) collective-permute-start(bf16[256,640]{1,0:T(8,128)(2,1)} %get-tuple-element.341), channel_id=1, source_target_pairs={{0,2},{1,3},{2,0},{3,1},{16,18},{17,19},{18,16},{19,17},{4,6},{5,7... | collective-permute-start | bytes 983048 | tf_op jit(solution)/shard_map/ppermute | solution.py:55
  15.1 17.3 %collective-permute-start.3 = (bf16[256,640]{1,0:T(8,128)(2,1)}, bf16[256,640]{1,0:T(8,128)(2,1)S(1)}, u32[]{:S(2)}, u32[]{:S(2)}) collective-permute-start(bf16[256,640]{1,0:T(8,128)(2,1)} %get-tuple-element.341), channel_id=1, source_target_pairs={{0,16},{1,17},{2,18},{3,19},{16,0},{17,1},{18,2},{19,3},{4,20},{5,... | collective-permute-start | bytes 983048 | tf_op jit(solution)/shard_map/ppermute | solution.py:55
  19.1 33.0 %all-to-all-start = ((bf16[16,16,2176]{2,1,0:T(8,128)(2,1)}), bf16[16,16,2176]{2,1,0:T(8,128)(2,1)}, u32[]{:S(2)}, u32[]{:S(2)}) async-start(bf16[16,16,2176]{2,1,0:T(8,128)(2,1)} %bitcast.107), calls=%async_computation | async-start | bytes 2228224 | tf_op jit(solution)/shard_map/all_to_all | solution.py:192
  32.0 18.0 %collective-permute-start.2 = (bf16[256,640]{1,0:T(8,128)(2,1)S(1)}, bf16[256,640]{1,0:T(8,128)(2,1)S(1)}, u32[]{:S(2)}, u32[]{:S(2)}) collective-permute-start(bf16[256,640]{1,0:T(8,128)(2,1)S(1)} %collective-permute-done.1), channel_id=1, source_target_pairs={{0,1},{1,0},{2,3},{3,2},{16,17},{17,16},{18,19},{19,18},{4,5},{5,4... | collective-permute-start | bytes 983048 | tf_op jit(solution)/shard_map/ppermute | solution.py:55
  32.4 17.1 %collective-permute-start.5 = (bf16[128,640]{1,0:T(8,128)(2,1)S(1)}, bf16[128,640]{1,0:T(8,128)(2,1)S(1)}, u32[]{:S(2)}, u32[]{:S(2)}) collective-permute-start(bf16[128,640]{1,0:T(8,128)(2,1)S(1)} %slice.169), channel_id=1, source_target_pairs={{0,2},{1,3},{2,0},{3,1},{16,18},{17,19},{18,16},{19,17},{4,6},{5,7... | collective-permute-start | bytes 491528 | tf_op jit(solution)/shard_map/ppermute | solution.py:55
  34.8 15.3 %collective-permute-start.4 = (bf16[256,640]{1,0:T(8,128)(2,1)S(1)}, bf16[256,640]{1,0:T(8,128)(2,1)S(1)}, u32[]{:S(2)}, u32[]{:S(2)}) collective-permute-start(bf16[256,640]{1,0:T(8,128)(2,1)S(1)} %collective-permute-done.3), channel_id=1, source_target_pairs={{0,1},{1,0},{2,3},{3,2},{16,17},{17,16},{18,19},{19,18},{4,5},{5,4... | collective-permute-start | bytes 983048 | tf_op jit(solution)/shard_map/ppermute | solution.py:55
  62.5 24.5 %collective-permute-start.14 = (bf16[256,512]{1,0:T(8,128)(2,1)S(1)}, bf16[256,512]{1,0:T(8,128)(2,1)S(1)}, u32[]{:S(2)}, u32[]{:S(2)}) collective-permute-start(bf16[256,512]{1,0:T(8,128)(2,1)S(1)} %project.3), channel_id=1, source_target_pairs={{0,8},{4,12},{8,0},{12,4},{1,9},{5,13},{9,1},{13,5},{2,10},{6,14},... | collective-permute-start | bytes 786440 | tf_op jit(solution)/shard_map/ppermute | solution.py:55
  65.8 21.5 %collective-permute-start.17 = (bf16[256,512]{1,0:T(8,128)(2,1)S(1)}, bf16[256,512]{1,0:T(8,128)(2,1)S(1)}, u32[]{:S(2)}, u32[]{:S(2)}) collective-permute-start(bf16[256,512]{1,0:T(8,128)(2,1)S(1)} %project.3), channel_id=1, source_target_pairs={{0,12},{4,8},{8,4},{12,0},{1,13},{5,9},{9,5},{13,1},{2,14},{6,10},... | collective-permute-start | bytes 786440 | tf_op jit(solution)/shard_map/ppermute | solution.py:55
  75.6 18.1 %collective-permute-start.12 = (bf16[256,512]{1,0:T(8,128)(2,1)S(1)}, bf16[256,512]{1,0:T(8,128)(2,1)S(1)}, u32[]{:S(2)}, u32[]{:S(2)}) collective-permute-start(bf16[256,512]{1,0:T(8,128)(2,1)S(1)} %collective-permute-done.11), channel_id=1, source_target_pairs={{0,2},{1,3},{2,0},{3,1},{4,6},{5,7},{6,4},{7,5},{8,10},{9,11},{10,... | collective-permute-start | bytes 786440 | tf_op jit(solution)/shard_map/ppermute | solution.py:55
  86.9 17.8 %collective-permute-start.10 = (bf16[512,512]{1,0:T(8,128)(2,1)S(1)}, bf16[512,512]{1,0:T(8,128)(2,1)S(1)}, u32[]{:S(2)}, u32[]{:S(2)}) collective-permute-start(bf16[512,512]{1,0:T(8,128)(2,1)S(1)} %pad_maximum_fusion.7), channel_id=1, source_target_pairs={{0,1},{1,0},{2,3},{3,2},{4,5},{5,4},{6,7},{7,6},{8,9},{9,8},{10,11... | collective-permute-start | bytes 1572872 | tf_op jit(solution)/shard_map/ppermute | solution.py:55
  87.3 17.2 %collective-permute-start.18 = (bf16[256,512]{1,0:T(8,128)(2,1)S(1)}, bf16[256,512]{1,0:T(8,128)(2,1)S(1)}, u32[]{:S(2)}, u32[]{:S(2)}) collective-permute-start(bf16[256,512]{1,0:T(8,128)(2,1)S(1)} %collective-permute-done.17), channel_id=1, source_target_pairs={{0,2},{1,3},{2,0},{3,1},{4,6},{5,7},{6,4},{7,5},{8,10},{9,11},{10,... | collective-permute-start | bytes 786440 | tf_op jit(solution)/shard_map/ppermute | solution.py:55
  117.6 61.7 %collective-permute-start.20 = (bf16[704,2048]{1,0:T(8,128)(2,1)}, bf16[704,2048]{1,0:T(8,128)(2,1)}, u32[]{:S(2)}, u32[]{:S(2)}) collective-permute-start(bf16[704,2048]{1,0:T(8,128)(2,1)} %param.21), channel_id=1, source_target_pairs={{0,1},{1,0},{2,3},{3,2},{16,17},{17,16},{18,19},{19,18},{4,5},{5,4... | collective-permute-start | bytes 8650760 | tf_op jit(solution)/shard_map/ppermute | solution.py:55
  117.8 61.6 %collective-permute-start.21 = (bf16[256,2816]{1,0:T(8,128)(2,1)}, bf16[256,2816]{1,0:T(8,128)(2,1)}, u32[]{:S(2)}, u32[]{:S(2)}) collective-permute-start(bf16[256,2816]{1,0:T(8,128)(2,1)} %pad_maximum_fusion.2), channel_id=1, source_target_pairs={{0,1},{1,0},{2,3},{3,2},{16,17},{17,16},{18,19},{19,18},{4,5},{5,4... | collective-permute-start | bytes 4325384 | tf_op jit(solution)/shard_map/ppermute | solution.py:55
  118.1 69.8 %all-to-all-start.1 = ((bf16[16,16,2048]{2,1,0:T(8,128)(2,1)}), bf16[16,16,2048]{2,1,0:T(8,128)(2,1)S(1)}, u32[]{:S(2)}, u32[]{:S(2)}) async-start(bf16[16,16,2048]{2,1,0:T(8,128)(2,1)} %bitcast.112), calls=%async_computation.1 | async-start | bytes 2097152 | tf_op jit(solution)/shard_map/all_to_all | solution.py:192
  122.9 424.1 %reduce-scatter.3.cloned.1.call-start = ((), (), s32[]{:S(2)}) async-start(), calls=%async_computation.8 | async-start | bytes 3604480 | tf_op jit(solution)/shard_map/reduce_scatter | solution.py:695
  123.1 76.8 %collective-permute-start.24 = (bf16[256,2816]{1,0:T(8,128)(2,1)}, bf16[256,2816]{1,0:T(8,128)(2,1)}, u32[]{:S(2)}, u32[]{:S(2)}) collective-permute-start(bf16[256,2816]{1,0:T(8,128)(2,1)} %pad_maximum_fusion.3), channel_id=1, source_target_pairs={{0,2},{1,3},{2,0},{3,1},{16,18},{17,19},{18,16},{19,17},{4,6},{5,7... | collective-permute-start | bytes 4325384 | tf_op jit(solution)/shard_map/ppermute | solution.py:55
  125.1 74.8 %collective-permute-start.25 = (bf16[256,2816]{1,0:T(8,128)(2,1)}, bf16[256,2816]{1,0:T(8,128)(2,1)}, u32[]{:S(2)}, u32[]{:S(2)}) collective-permute-start(bf16[256,2816]{1,0:T(8,128)(2,1)} %pad_maximum_fusion.4), channel_id=1, source_target_pairs={{0,16},{1,17},{2,18},{3,19},{16,0},{17,1},{18,2},{19,3},{4,20},{5,... | collective-permute-start | bytes 4325384 | tf_op jit(solution)/shard_map/ppermute | solution.py:55
  126.5 94.5 %collective-permute-start.26 = (bf16[256,2816]{1,0:T(8,128)(2,1)}, bf16[256,2816]{1,0:T(8,128)(2,1)}, u32[]{:S(2)}, u32[]{:S(2)}) collective-permute-start(bf16[256,2816]{1,0:T(8,128)(2,1)} %pad_maximum_fusion.5), channel_id=1, source_target_pairs={{0,18},{1,19},{2,16},{3,17},{16,2},{17,3},{18,0},{19,1},{4,22},{5,... | collective-permute-start | bytes 4325384 | tf_op jit(solution)/shard_map/ppermute | solution.py:55
  188.0 54.3 %collective-permute-start.22 = (bf16[256,2048]{1,0:T(8,128)(2,1)}, bf16[256,2048]{1,0:T(8,128)(2,1)S(1)}, u32[]{:S(2)}, u32[]{:S(2)}) collective-permute-start(bf16[256,2048]{1,0:T(8,128)(2,1)} %multiply_convert_fusion.3), channel_id=1, source_target_pairs={{0,2},{1,3},{2,0},{3,1},{16,18},{17,19},{18,16},{19,17},{4,6},{5,7... | collective-permute-start | bytes 3145736 | tf_op jit(solution)/shard_map/ppermute | solution.py:55
  189.9 53.2 %collective-permute-start.23 = (bf16[256,2048]{1,0:T(8,128)(2,1)}, bf16[256,2048]{1,0:T(8,128)(2,1)S(1)}, u32[]{:S(2)}, u32[]{:S(2)}) collective-permute-start(bf16[256,2048]{1,0:T(8,128)(2,1)} %multiply_convert_fusion.3), channel_id=1, source_target_pairs={{0,16},{1,17},{2,18},{3,19},{16,0},{17,1},{18,2},{19,3},{4,20},{5,... | collective-permute-start | bytes 3145736 | tf_op jit(solution)/shard_map/ppermute | solution.py:55
  243.2 36.8 %collective-permute-start.27 = (bf16[256,2048]{1,0:T(8,128)(2,1)S(1)}, bf16[256,2048]{1,0:T(8,128)(2,1)S(1)}, u32[]{:S(2)}, u32[]{:S(2)}) collective-permute-start(bf16[256,2048]{1,0:T(8,128)(2,1)S(1)} %bitcast.103), channel_id=1, source_target_pairs={{0,2},{1,3},{2,0},{3,1},{16,18},{17,19},{18,16},{19,17},{4,6},{5,7... | collective-permute-start | bytes 3145736 | tf_op jit(solution)/shard_map/ppermute | solution.py:55
  243.7 36.3 %collective-permute-start.28 = (bf16[256,2048]{1,0:T(8,128)(2,1)S(1)}, bf16[256,2048]{1,0:T(8,128)(2,1)S(1)}, u32[]{:S(2)}, u32[]{:S(2)}) collective-permute-start(bf16[256,2048]{1,0:T(8,128)(2,1)S(1)} %bitcast.104), channel_id=1, source_target_pairs={{0,16},{1,17},{2,18},{3,19},{16,0},{17,1},{18,2},{19,3},{4,20},{5,... | collective-permute-start | bytes 3145736 | tf_op jit(solution)/shard_map/ppermute | solution.py:55
  244.4 35.1 %collective-permute-start.29 = (bf16[128,2048]{1,0:T(8,128)(2,1)S(1)}, bf16[128,2048]{1,0:T(8,128)(2,1)S(1)}, u32[]{:S(2)}, u32[]{:S(2)}) collective-permute-start(bf16[128,2048]{1,0:T(8,128)(2,1)S(1)} %slice.135), channel_id=1, source_target_pairs={{0,2},{1,3},{2,0},{3,1},{16,18},{17,19},{18,16},{19,17},{4,6},{5,7... | collective-permute-start | bytes 1572872 | tf_op jit(solution)/shard_map/ppermute | solution.py:55
  245.9 33.8 %collective-permute-start.30 = (bf16[128,2048]{1,0:T(8,128)(2,1)S(1)}, bf16[128,2048]{1,0:T(8,128)(2,1)S(1)}, u32[]{:S(2)}, u32[]{:S(2)}) collective-permute-start(bf16[128,2048]{1,0:T(8,128)(2,1)S(1)} %slice.136), channel_id=1, source_target_pairs={{0,16},{1,17},{2,18},{3,19},{16,0},{17,1},{18,2},{19,3},{4,20},{5,... | collective-permute-start | bytes 1572872 | tf_op jit(solution)/shard_map/ppermute | solution.py:55
  247.4 34.8 %collective-permute-start.33 = (bf16[256,2816]{1,0:T(8,128)(2,1)}, bf16[256,2816]{1,0:T(8,128)(2,1)S(1)}, u32[]{:S(2)}, u32[]{:S(2)}) collective-permute-start(bf16[256,2816]{1,0:T(8,128)(2,1)} %collective-permute-done.24), channel_id=1, source_target_pairs={{0,1},{1,0},{2,3},{3,2},{16,17},{17,16},{18,19},{19,18},{4,5},{5,4... | collective-permute-start | bytes 4325384 | tf_op jit(solution)/shard_map/ppermute | solution.py:55
  280.0 30.2 %collective-permute-start.31 = (bf16[128,2048]{1,0:T(8,128)(2,1)S(1)}, bf16[128,2048]{1,0:T(8,128)(2,1)S(1)}, u32[]{:S(2)}, u32[]{:S(2)}) collective-permute-start(bf16[128,2048]{1,0:T(8,128)(2,1)S(1)} %slice.137), channel_id=1, source_target_pairs={{0,2},{1,3},{2,0},{3,1},{16,18},{17,19},{18,16},{19,17},{4,6},{5,7... | collective-permute-start | bytes 1572872 | tf_op jit(solution)/shard_map/ppermute | solution.py:55
  281.4 28.8 %collective-permute-start.32 = (bf16[128,2048]{1,0:T(8,128)(2,1)S(1)}, bf16[128,2048]{1,0:T(8,128)(2,1)S(1)}, u32[]{:S(2)}, u32[]{:S(2)}) collective-permute-start(bf16[128,2048]{1,0:T(8,128)(2,1)S(1)} %slice.138), channel_id=1, source_target_pairs={{0,16},{1,17},{2,18},{3,19},{16,0},{17,1},{18,2},{19,3},{4,20},{5,... | collective-permute-start | bytes 1572872 | tf_op jit(solution)/shard_map/ppermute | solution.py:55
  364.9 200.6 %reduce-scatter.5.cloned.1.call-start = ((), (), s32[]{:S(2)}) async-start(), calls=%async_computation.9 | async-start | bytes 7208960 | tf_op jit(solution)/shard_map/reduce_scatter | solution.py:699
  385.0 26.3 %collective-permute-start.36 = (bf16[256,2048]{1,0:T(8,128)(2,1)}, bf16[256,2048]{1,0:T(8,128)(2,1)}, u32[]{:S(2)}, u32[]{:S(2)}) collective-permute-start(bf16[256,2048]{1,0:T(8,128)(2,1)} %get-tuple-element.314), channel_id=1, source_target_pairs={{0,2},{1,3},{2,0},{3,1},{16,18},{17,19},{18,16},{19,17},{4,6},{5,7... | collective-permute-start | bytes 3145736 | tf_op jit(solution)/shard_map/ppermute | solution.py:55
  385.8 46.8 %collective-permute-start.37 = (bf16[256,2048]{1,0:T(8,128)(2,1)}, bf16[256,2048]{1,0:T(8,128)(2,1)}, u32[]{:S(2)}, u32[]{:S(2)}) collective-permute-start(bf16[256,2048]{1,0:T(8,128)(2,1)} %get-tuple-element.313), channel_id=1, source_target_pairs={{0,16},{1,17},{2,18},{3,19},{16,0},{17,1},{18,2},{19,3},{4,20},{5,... | collective-permute-start | bytes 3145736 | tf_op jit(solution)/shard_map/ppermute | solution.py:55
  388.6 45.5 %collective-permute-start.38 = (bf16[256,2048]{1,0:T(8,128)(2,1)}, bf16[256,2048]{1,0:T(8,128)(2,1)}, u32[]{:S(2)}, u32[]{:S(2)}) collective-permute-start(bf16[256,2048]{1,0:T(8,128)(2,1)} %get-tuple-element.312), channel_id=1, source_target_pairs={{0,18},{1,19},{2,16},{3,17},{16,2},{17,3},{18,0},{19,1},{4,22},{5,... | collective-permute-start | bytes 3145736 | tf_op jit(solution)/shard_map/ppermute | solution.py:55
  434.1 194.8 %all-gather.9.cloned.1.call-start = ((), (), s32[]{:S(2)}) async-start(), calls=%async_computation.10 | async-start | bytes 3604480 | tf_op jit(solution)/shard_map/all_gather | solution.py:722
  452.9 16.9 %collective-permute-start.50 = (bf16[256,512]{1,0:T(8,128)(2,1)S(1)}, bf16[256,512]{1,0:T(8,128)(2,1)S(1)}, u32[]{:S(2)}, u32[]{:S(2)}) collective-permute-start(bf16[256,512]{1,0:T(8,128)(2,1)S(1)} %get-tuple-element.333), channel_id=1, source_target_pairs={{0,2},{1,3},{2,0},{3,1},{16,18},{17,19},{18,16},{19,17},{4,6},{5,7... | collective-permute-start | bytes 786440 | tf_op jit(solution)/shard_map/ppermute | solution.py:55
  453.7 91.1 %collective-permute-start.44 = (bf16[256,2048]{1,0:T(8,128)(2,1)S(1)}, bf16[256,2048]{1,0:T(8,128)(2,1)S(1)}, u32[]{:S(2)}, u32[]{:S(2)}) collective-permute-start(bf16[256,2048]{1,0:T(8,128)(2,1)S(1)} %get-tuple-element.206), channel_id=1, source_target_pairs={{0,2},{1,3},{2,0},{3,1},{16,18},{17,19},{18,16},{19,17},{4,6},{5,7... | collective-permute-start | bytes 3145736 | tf_op jit(solution)/shard_map/ppermute | solution.py:55
  458.5 86.3 %collective-permute-start.45 = (bf16[256,2048]{1,0:T(8,128)(2,1)S(1)}, bf16[256,2048]{1,0:T(8,128)(2,1)S(1)}, u32[]{:S(2)}, u32[]{:S(2)}) collective-permute-start(bf16[256,2048]{1,0:T(8,128)(2,1)S(1)} %get-tuple-element.206), channel_id=1, source_target_pairs={{0,16},{1,17},{2,18},{3,19},{16,0},{17,1},{18,2},{19,3},{4,20},{5,... | collective-permute-start | bytes 3145736 | tf_op jit(solution)/shard_map/ppermute | solution.py:55
  463.1 83.9 %collective-permute-start.46 = (bf16[256,2048]{1,0:T(8,128)(2,1)S(1)}, bf16[256,2048]{1,0:T(8,128)(2,1)}, u32[]{:S(2)}, u32[]{:S(2)}) collective-permute-start(bf16[256,2048]{1,0:T(8,128)(2,1)S(1)} %get-tuple-element.206), channel_id=1, source_target_pairs={{0,18},{1,19},{2,16},{3,17},{16,2},{17,3},{18,0},{19,1},{4,22},{5,... | collective-permute-start | bytes 3145736 | tf_op jit(solution)/shard_map/ppermute | solution.py:55
  464.7 80.2 %collective-permute-start.51 = (bf16[256,512]{1,0:T(8,128)(2,1)S(1)}, bf16[256,512]{1,0:T(8,128)(2,1)S(1)}, u32[]{:S(2)}, u32[]{:S(2)}) collective-permute-start(bf16[256,512]{1,0:T(8,128)(2,1)S(1)} %get-tuple-element.332), channel_id=1, source_target_pairs={{0,16},{1,17},{2,18},{3,19},{16,0},{17,1},{18,2},{19,3},{4,20},{5,... | collective-permute-start | bytes 786440 | tf_op jit(solution)/shard_map/ppermute | solution.py:55
  469.8 75.0 %collective-permute-start.52 = (bf16[256,512]{1,0:T(8,128)(2,1)S(1)}, bf16[256,512]{1,0:T(8,128)(2,1)S(1)}, u32[]{:S(2)}, u32[]{:S(2)}) collective-permute-start(bf16[256,512]{1,0:T(8,128)(2,1)S(1)} %get-tuple-element.331), channel_id=1, source_target_pairs={{0,18},{1,19},{2,16},{3,17},{16,2},{17,3},{18,0},{19,1},{4,22},{5,... | collective-permute-start | bytes 786440 | tf_op jit(solution)/shard_map/ppermute | solution.py:55
  551.0 366.7 %all-gather.11.cloned.1.call-start = ((), (), s32[]{:S(2)}) async-start(), calls=%async_computation.11 | async-start | bytes 7208960 | tf_op jit(solution)/shard_map/all_gather | solution.py:744
  567.9 41.1 %collective-permute-start.54 = (bf16[4,256,512]{2,1,0:T(8,128)(2,1)S(1)}, bf16[4,256,512]{2,1,0:T(8,128)(2,1)S(1)}, u32[]{:S(2)}, u32[]{:S(2)}) collective-permute-start(bf16[4,256,512]{2,1,0:T(8,128)(2,1)S(1)} %slice_bitcast_fusion), channel_id=1, source_target_pairs={{0,2},{1,3},{2,0},{3,1},{4,6},{5,7},{6,4},{7,5},{8,10},{9,11},{10,... | collective-permute-start | bytes 3145736 | tf_op jit(solution)/shard_map/ppermute | solution.py:55
  579.9 21.8 %collective-permute-start.55 = (bf16[64,2816]{1,0:T(8,128)(2,1)S(1)}, bf16[64,2816]{1,0:T(8,128)(2,1)S(1)}, u32[]{:S(2)}, u32[]{:S(2)}) collective-permute-start(bf16[64,2816]{1,0:T(8,128)(2,1)S(1)} %get-tuple-element.326), channel_id=1, source_target_pairs={{0,2},{1,3},{2,0},{3,1},{16,18},{17,19},{18,16},{19,17},{4,6},{5,7... | collective-permute-start | bytes 1081352 | tf_op jit(solution)/shard_map/ppermute | solution.py:55
  581.1 20.5 %collective-permute-start.56 = (bf16[64,2816]{1,0:T(8,128)(2,1)S(1)}, bf16[64,2816]{1,0:T(8,128)(2,1)S(1)}, u32[]{:S(2)}, u32[]{:S(2)}) collective-permute-start(bf16[64,2816]{1,0:T(8,128)(2,1)S(1)} %get-tuple-element.325), channel_id=1, source_target_pairs={{0,16},{1,17},{2,18},{3,19},{16,0},{17,1},{18,2},{19,3},{4,20},{5,... | collective-permute-start | bytes 1081352 | tf_op jit(solution)/shard_map/ppermute | solution.py:55
  581.7 27.3 %collective-permute-start.57 = (bf16[64,2816]{1,0:T(8,128)(2,1)S(1)}, bf16[64,2816]{1,0:T(8,128)(2,1)S(1)}, u32[]{:S(2)}, u32[]{:S(2)}) collective-permute-start(bf16[64,2816]{1,0:T(8,128)(2,1)S(1)} %get-tuple-element.324), channel_id=1, source_target_pairs={{0,18},{1,19},{2,16},{3,17},{16,2},{17,3},{18,0},{19,1},{4,22},{5,... | collective-permute-start | bytes 1081352 | tf_op jit(solution)/shard_map/ppermute | solution.py:55
  610.8 45.9 %collective-permute-start.62 = (bf16[256,2048]{1,0:T(8,128)(2,1)}, bf16[256,2048]{1,0:T(8,128)(2,1)}, u32[]{:S(2)}, u32[]{:S(2)}) collective-permute-start(bf16[256,2048]{1,0:T(8,128)(2,1)} %turn_back.2), channel_id=1, source_target_pairs={{0,2},{1,3},{2,0},{3,1},{16,18},{17,19},{18,16},{19,17},{4,6},{5,7... | collective-permute-start | bytes 3145736 | tf_op jit(solution)/shard_map/ppermute | solution.py:55
  612.1 48.1 %collective-permute-start.63 = (bf16[256,2048]{1,0:T(8,128)(2,1)}, bf16[256,2048]{1,0:T(8,128)(2,1)}, u32[]{:S(2)}, u32[]{:S(2)}) collective-permute-start(bf16[256,2048]{1,0:T(8,128)(2,1)} %turn_back.2), channel_id=1, source_target_pairs={{0,16},{1,17},{2,18},{3,19},{16,0},{17,1},{18,2},{19,3},{4,20},{5,... | collective-permute-start | bytes 3145736 | tf_op jit(solution)/shard_map/ppermute | solution.py:55
  615.9 21.6 %collective-permute-start.59 = (bf16[256,512]{1,0:T(8,128)(2,1)}, bf16[256,512]{1,0:T(8,128)(2,1)S(1)}, u32[]{:S(2)}, u32[]{:S(2)}) collective-permute-start(bf16[256,512]{1,0:T(8,128)(2,1)} %get-tuple-element.329), channel_id=1, source_target_pairs={{0,8},{4,12},{8,0},{12,4},{1,9},{5,13},{9,1},{13,5},{2,10},{6,14},... | collective-permute-start | bytes 786440 | tf_op jit(solution)/shard_map/ppermute | solution.py:55
  619.7 17.8 %collective-permute-start.60 = (bf16[256,512]{1,0:T(8,128)(2,1)}, bf16[256,512]{1,0:T(8,128)(2,1)S(1)}, u32[]{:S(2)}, u32[]{:S(2)}) collective-permute-start(bf16[256,512]{1,0:T(8,128)(2,1)} %get-tuple-element.328), channel_id=1, source_target_pairs={{0,12},{4,8},{8,4},{12,0},{1,13},{5,9},{9,5},{13,1},{2,14},{6,10},... | collective-permute-start | bytes 786440 | tf_op jit(solution)/shard_map/ppermute | solution.py:55
  627.6 32.5 %collective-permute-start.64 = (bf16[256,2048]{1,0:T(8,128)(2,1)}, bf16[256,2048]{1,0:T(8,128)(2,1)}, u32[]{:S(2)}, u32[]{:S(2)}) collective-permute-start(bf16[256,2048]{1,0:T(8,128)(2,1)} %turn_back.2), channel_id=1, source_target_pairs={{0,18},{1,19},{2,16},{3,17},{16,2},{17,3},{18,0},{19,1},{4,22},{5,... | collective-permute-start | bytes 3145736 | tf_op jit(solution)/shard_map/ppermute | solution.py:55
  645.5 43.8 %collective-permute-start.65 = (bf16[256,2048]{1,0:T(8,128)(2,1)}, bf16[256,2048]{1,0:T(8,128)(2,1)S(1)}, u32[]{:S(2)}, u32[]{:S(2)}) collective-permute-start(bf16[256,2048]{1,0:T(8,128)(2,1)} %add_convert_fusion.11), channel_id=1, source_target_pairs={{0,4},{12,8},{1,5},{13,9},{2,6},{14,10},{3,7},{15,11},{16,20},{28,... | collective-permute-start | bytes 3145736 | tf_op jit(solution)/shard_map/ppermute | solution.py:144
  696.0 18.1 %collective-permute-start.73 = (bf16[256,2048]{1,0:T(8,128)(2,1)S(1)}, bf16[256,2048]{1,0:T(8,128)(2,1)S(1)}, u32[]{:S(2)}, u32[]{:S(2)}) collective-permute-start(bf16[256,2048]{1,0:T(8,128)(2,1)S(1)} %add_convert_fusion.9), channel_id=1, source_target_pairs={{4,8},{8,4},{5,9},{9,5},{6,10},{10,6},{7,11},{11,7},{20,24},{24,20... | collective-permute-start | bytes 3145736 | tf_op jit(solution)/shard_map/ppermute | solution.py:148
  697.4 15.4 %collective-permute-start.67 = (bf16[256,512]{1,0:T(8,128)(2,1)S(1)}, bf16[256,512]{1,0:T(8,128)(2,1)S(1)}, u32[]{:S(2)}, u32[]{:S(2)}) collective-permute-start(bf16[256,512]{1,0:T(8,128)(2,1)S(1)} %copy-done.43), channel_id=1, source_target_pairs={{0,2},{1,3},{2,0},{3,1},{16,18},{17,19},{18,16},{19,17},{4,6},{5,7... | collective-permute-start | bytes 786440 | tf_op jit(solution)/shard_map/ppermute | solution.py:55
  714.9 111.1 %all-to-all-start.2 = ((bf16[16,16,2048]{2,1,0:T(8,128)(2,1)}), bf16[16,16,2048]{2,1,0:T(8,128)(2,1)}, u32[]{:S(2)}, u32[]{:S(2)}) async-start(bf16[16,16,2048]{2,1,0:T(8,128)(2,1)} %bitcast.33), calls=%async_computation.4 | async-start | bytes 2097152 | tf_op jit(solution)/shard_map/all_to_all | solution.py:192
  782.8 42.1 %collective-permute-start.77 = (bf16[256,2048]{1,0:T(8,128)(2,1)S(1)}, bf16[256,2048]{1,0:T(8,128)(2,1)S(1)}, u32[]{:S(2)}, u32[]{:S(2)}) collective-permute-start(bf16[256,2048]{1,0:T(8,128)(2,1)S(1)} %add_convert_fusion.8), channel_id=1, source_target_pairs={{4,0},{8,12},{5,1},{9,13},{6,2},{10,14},{7,3},{11,15},{20,16},{24,... | collective-permute-start | bytes 3145736 | tf_op jit(solution)/shard_map/ppermute | solution.py:152
  787.1 38.9 %collective-permute-start.74 = (bf16[256,2048]{1,0:T(8,128)(2,1)}, bf16[256,2048]{1,0:T(8,128)(2,1)}, u32[]{:S(2)}, u32[]{:S(2)}) collective-permute-start(bf16[256,2048]{1,0:T(8,128)(2,1)} %add_convert_fusion.10), channel_id=1, source_target_pairs={{0,4},{12,8},{1,5},{13,9},{2,6},{14,10},{3,7},{15,11},{16,20},{28,... | collective-permute-start | bytes 3145736 | tf_op jit(solution)/shard_map/ppermute | solution.py:144
  794.9 39.9 %collective-permute-start.80 = (bf16[256,2048]{1,0:T(8,128)(2,1)}, bf16[256,2048]{1,0:T(8,128)(2,1)}, u32[]{:S(2)}, u32[]{:S(2)}) collective-permute-start(bf16[256,2048]{1,0:T(8,128)(2,1)} %get-tuple-element.308), channel_id=1, source_target_pairs={{0,2},{1,3},{2,0},{3,1},{16,18},{17,19},{18,16},{19,17},{4,6},{5,7... | collective-permute-start | bytes 3145736 | tf_op jit(solution)/shard_map/ppermute | solution.py:55
  796.8 38.0 %collective-permute-start.81 = (bf16[256,2048]{1,0:T(8,128)(2,1)}, bf16[256,2048]{1,0:T(8,128)(2,1)}, u32[]{:S(2)}, u32[]{:S(2)}) collective-permute-start(bf16[256,2048]{1,0:T(8,128)(2,1)} %get-tuple-element.307), channel_id=1, source_target_pairs={{0,16},{1,17},{2,18},{3,19},{16,0},{17,1},{18,2},{19,3},{4,20},{5,... | collective-permute-start | bytes 3145736 | tf_op jit(solution)/shard_map/ppermute | solution.py:55
  797.5 48.1 %collective-permute-start.82 = (bf16[256,2048]{1,0:T(8,128)(2,1)}, bf16[256,2048]{1,0:T(8,128)(2,1)}, u32[]{:S(2)}, u32[]{:S(2)}) collective-permute-start(bf16[256,2048]{1,0:T(8,128)(2,1)} %get-tuple-element.306), channel_id=1, source_target_pairs={{0,18},{1,19},{2,16},{3,17},{16,2},{17,3},{18,0},{19,1},{4,22},{5,... | collective-permute-start | bytes 3145736 | tf_op jit(solution)/shard_map/ppermute | solution.py:55
  829.0 16.6 %collective-permute-start.78 = (bf16[256,2048]{1,0:T(8,128)(2,1)S(1)}, bf16[256,2048]{1,0:T(8,128)(2,1)S(1)}, u32[]{:S(2)}, u32[]{:S(2)}) collective-permute-start(bf16[256,2048]{1,0:T(8,128)(2,1)S(1)} %add_convert_fusion.7), channel_id=1, source_target_pairs={{4,8},{8,4},{5,9},{9,5},{6,10},{10,6},{7,11},{11,7},{20,24},{24,20... | collective-permute-start | bytes 3145736 | tf_op jit(solution)/shard_map/ppermute | solution.py:148
  829.7 15.9 %collective-permute-start.79 = (bf16[256,640]{0,1:T(8,128)(2,1)S(1)}, bf16[256,640]{0,1:T(8,128)(2,1)S(1)}, u32[]{:S(2)}, u32[]{:S(2)}) collective-permute-start(bf16[256,640]{0,1:T(8,128)(2,1)S(1)} %fusion.66), channel_id=1, source_target_pairs={{0,4},{12,8},{1,5},{13,9},{2,6},{14,10},{3,7},{15,11},{16,20},{28,... | collective-permute-start | bytes 983048 | tf_op jit(solution)/shard_map/ppermute | solution.py:144
  851.0 66.7 %all-to-all-start.3 = ((bf16[16,16,2048]{2,1,0:T(8,128)(2,1)}), bf16[16,16,2048]{2,1,0:T(8,128)(2,1)S(1)}, u32[]{:S(2)}, u32[]{:S(2)}) async-start(bf16[16,16,2048]{2,1,0:T(8,128)(2,1)} %bitcast.108), calls=%async_computation.5 | async-start | bytes 2097152 | tf_op jit(solution)/shard_map/all_to_all | solution.py:192
  865.8 40.6 %collective-permute-start.83 = (bf16[256,2048]{1,0:T(8,128)(2,1)S(1)}, bf16[256,2048]{1,0:T(8,128)(2,1)}, u32[]{:S(2)}, u32[]{:S(2)}) collective-permute-start(bf16[256,2048]{1,0:T(8,128)(2,1)S(1)} %add_convert_fusion.6), channel_id=1, source_target_pairs={{4,0},{8,12},{5,1},{9,13},{6,2},{10,14},{7,3},{11,15},{20,16},{24,... | collective-permute-start | bytes 3145736 | tf_op jit(solution)/shard_map/ppermute | solution.py:152
  (105 other events, 946.8 us)
Sparse Core Ops, SparseCore 0:
  9.9 81.3 all-gather.4
  93.2 84.4 all-gather.6
  365.0 56.4 reduce-scatter.2
  434.2 102.4 reduce-scatter.4
  551.2 58.9 all-gather.8
  652.8 127.9 all-gather.10

commit v2 on v1

--- a/solution.py
+++ b/solution.py
@@ -96,6 +96,39 @@
 
 def add(left, right):
     return (left.astype(f32) + right.astype(f32)).astype(bf16)
+
+
+class ChipSum:
+    def __init__(self, blocks):
+        self.parts = [[block[half] for half in halves(block.shape[0])] for block in blocks]
+
+    def first(self):
+        chips = len(self.parts)
+        self.came = {}
+        for r in sorted(range(1, chips), key=lambda r: -bin(r).count("1")):
+            low, high = r & -r, 1 << (r.bit_length() - 1)
+            if low == high:
+                continue
+            if bin(r).count("1") < bin(chips - 1).count("1"):
+                self.settle(r)
+            self.came[r ^ low, 0, r] = swap(self.parts[r][0], low << 1)
+            self.came[r ^ high, 1, r] = swap(self.parts[r][1], high << 1)
+
+    def settle(self, only=None):
+        for key in sorted(self.came):
+            if only is None or key[0] == only:
+                self.parts[key[0]][key[1]] = add(self.parts[key[0]][key[1]], self.came.pop(key))
+
+    def second(self):
+        self.settle()
+        self.ends = []
+        r = 1
+        while r < len(self.parts):
+            self.ends.append(swap(jnp.concatenate(self.parts[r], axis=0), r << 1))
+            r *= 2
+
+    def result(self):
+        return add_all([jnp.concatenate(self.parts[0], axis=0)] + self.ends)
 
 
 def to_chips(blocks):
@@ -138,10 +171,10 @@
         return [add(kept, came) for kept, came in zip(self.kept, self.came)]
 
 
-class LineSum:
+class LineTree:
     def __init__(self, share):
         self.share = share
-        self.moving = lax.ppermute(self.share, "seq", [(0, 1), (3, 2)])
+        self.moving = lax.ppermute(share, "seq", [(0, 1), (3, 2)])
 
     def across(self):
         self.share = add(self.share, self.moving)
@@ -157,11 +190,35 @@
         return jnp.where(inner, self.share, self.moving).astype(f32)
 
 
-def gather_group(line):
-    rows = []
-    for piece in line:
-        rows += [piece, swap(piece, 2, "ctx")]
-    pairs = [jnp.concatenate(rows[2 * i : 2 * i + 2], axis=0) for i in range(4)]
+class LineSum:
+    def __init__(self, share):
+        self.share = share
+
+    def scatter(self):
+        place = lax.axis_index("seq")
+        count = lax.axis_size("seq")
+        rows = self.share.shape[0] // count
+
+        def part(m):
+            return lax.dynamic_slice_in_dim(self.share, (place ^ m) * rows, rows, 0)
+
+        self.parts = [part(0)] + [swap(part(m), m, "seq") for m in range(1, count)]
+
+    def gather(self):
+        total = add_all(self.parts).astype(bf16)
+        self.parts = [total] + [swap(total, m, "seq") for m in range(1, len(self.parts))]
+
+    def result(self):
+        place = lax.axis_index("seq")
+        rows = self.parts[0].shape[0]
+        out = self.share
+        for m, values in enumerate(self.parts):
+            out = lax.dynamic_update_slice_in_dim(out, values, (place ^ m) * rows, 0)
+        return out
+
+
+def gather_lanes(pairs):
+    pairs = [jnp.concatenate(pair, axis=0) for pair in pairs]
     others = [swap(pair, 1, "ctx") for pair in pairs]
     return jnp.concatenate([half for both in zip(pairs, others) for half in both], axis=0)
 
@@ -225,6 +282,28 @@
         compiler_params=pltpu.CompilerParams(vmem_limit_bytes=24 * 1024 * 1024),
         name="place_columns",
     )(at.astype(jnp.int32)[None], values)
+
+
+class LineGather:
+    def __init__(self, own):
+        self.own, self.right, self.left = own, [], []
+
+    def step(self):
+        at = len(self.right)
+        count = lax.axis_size("seq")
+        right = self.right[-1] if at else self.own
+        left = self.left[-1] if at else self.own
+        pairs = [(i, i + 1) for i in range(at, count - 1)]
+        self.right.append(lax.ppermute(right, "seq", pairs))
+        back = [(i, i - 1) for i in range(count - 1 - at, 0, -1)]
+        self.left.append(lax.ppermute(left, "seq", back))
+
+    def result(self):
+        count = lax.axis_size("seq")
+        rows = self.own.shape[0]
+        around = jnp.concatenate([*self.right[::-1], self.own, *self.left], axis=0)
+        start = (count - 1 - lax.axis_index("seq")) * rows
+        return lax.dynamic_slice_in_dim(around, start, count * rows, 0)
 
 
 def stack_heads(block, heads, rows, first):
@@ -475,9 +554,9 @@
         ],
         compiler_params=pltpu.CompilerParams(vmem_limit_bytes=40 * 1024 * 1024),
         cost_estimate=pl.CostEstimate(
-            flops=tiles * keys * width * 128 * 10,
+            flops=tiles * keys * width * 8,
             bytes_accessed=8 * 1024 * 1024,
-            transcendentals=tiles * keys * width // 2,
+            transcendentals=0,
         ),
         name="attend_backward",
     )(q, do, kv, ot, lse)
@@ -548,6 +627,85 @@
         ),
         name="turn_back",
     )(x, cosine, -sine)
+
+
+def tiles_of(count):
+    return [(at, min(256, count - at)) for at in range(0, count, 256)]
+
+
+def feed_body(x_ref, w_ref, values_ref, hidden_ref):
+    count = hidden_ref.shape[1]
+    for at, size in tiles_of(count):
+        here, there = slice(at, at + size), slice(count + at, count + at + size)
+        gate = dot(x_ref[...], w_ref[:, here])
+        up = dot(x_ref[...], w_ref[:, there])
+        values_ref[:, here] = gate
+        values_ref[:, there] = up
+        hidden_ref[:, here] = (gate * jax.nn.sigmoid(gate) * up).astype(bf16)
+
+
+def feed_back_body(c_ref, d_ref, values_ref, slope_ref):
+    count = d_ref.shape[0]
+    for at, size in tiles_of(count):
+        here, there = slice(at, at + size), slice(count + at, count + at + size)
+        slope = dot(c_ref[...], d_ref[here, :], NT)
+        gate, up = values_ref[:, here], values_ref[:, there]
+        sigmoid = jax.nn.sigmoid(gate)
+        silu = gate * sigmoid
+        slope_ref[:, here] = (slope * up * sigmoid * (1.0 + gate * (1.0 - sigmoid))).astype(bf16)
+        slope_ref[:, there] = (slope * silu).astype(bf16)
+
+
+def feed(x, both, count):
+    tokens, width = x.shape
+    tile = min(tokens, 256)
+    return pl.pallas_call(
+        feed_body,
+        grid=(tokens // tile,),
+        out_shape=(
+            jax.ShapeDtypeStruct((tokens, 2 * count), f32),
+            jax.ShapeDtypeStruct((tokens, count), bf16),
+        ),
+        in_specs=[
+            pl.BlockSpec((tile, width), lambda i: (i, 0)),
+            pl.BlockSpec(both.shape, lambda i: (0, 0), pipeline_mode=pl.Buffered(1)),
+        ],
+        out_specs=(
+            pl.BlockSpec((tile, 2 * count), lambda i: (i, 0)),
+            pl.BlockSpec((tile, count), lambda i: (i, 0)),
+        ),
+        compiler_params=pltpu.CompilerParams(vmem_limit_bytes=40 * 1024 * 1024),
+        cost_estimate=pl.CostEstimate(
+            flops=4 * tokens * width * count,
+            bytes_accessed=2 * (tokens * width + 2 * width * count + 5 * tokens * count),
+            transcendentals=tokens * count,
+        ),
+        name="feed",
+    )(x, both)
+
+
+def feed_back(cotangent, down, values):
+    tokens, width = cotangent.shape
+    count = down.shape[0]
+    tile = min(tokens, 256)
+    return pl.pallas_call(
+        feed_back_body,
+        grid=(tokens // tile,),
+        out_shape=jax.ShapeDtypeStruct((tokens, 2 * count), bf16),
+        in_specs=[
+            pl.BlockSpec((tile, width), lambda i: (i, 0)),
+            pl.BlockSpec(down.shape, lambda i: (0, 0), pipeline_mode=pl.Buffered(1)),
+            pl.BlockSpec((tile, 2 * count), lambda i: (i, 0)),
+        ],
+        out_specs=pl.BlockSpec((tile, 2 * count), lambda i: (i, 0)),
+        compiler_params=pltpu.CompilerParams(vmem_limit_bytes=32 * 1024 * 1024),
+        cost_estimate=pl.CostEstimate(
+            flops=2 * tokens * width * count,
+            bytes_accessed=2 * (tokens * width + width * count + 6 * tokens * count),
+            transcendentals=tokens * count,
+        ),
+        name="feed_back",
+    )(cotangent, down, values)
 
 
 def on_device(
@@ -615,7 +773,8 @@
     line_pairs = [paired] + [swap(paired, m, "seq") for m in (1, 2, 3)]
     both_full = jnp.broadcast_to(moved[0, 0] * 0.0, (own_rows * owners, 2 * hidden_part))
     line_pairs[0], both_full = tie(line_pairs[0], both_full)
-    all_pairs = gather_group(line_pairs).reshape(group, group, rows, -1)
+    pairs = [(piece, swap(piece, 2, "ctx")) for piece in line_pairs]
+    all_pairs = gather_lanes(pairs).reshape(group, group, rows, -1)
     query_scale = HEAD_DIM**-0.5 * log2_e
     queries = project(first_input, query_full, cosine, sine, query_scale, width)
 
@@ -660,18 +819,24 @@
     feed_slope.second()
     feed_input = feed_input.result()
 
-    gate_values = dot(feed_input, both_full[:, :hidden_part])
-    up_values = dot(feed_input, both_full[:, hidden_part:])
-    feed_slope.rest, up_values, gate_values = tie(feed_slope.rest, up_values, gate_values)
+    if hidden_part % 128:
+        gate_values = dot(feed_input, both_full[:, :hidden_part])
+        up_values = dot(feed_input, both_full[:, hidden_part:])
+        gate_sigmoid = jax.nn.sigmoid(gate_values)
+        hidden = (gate_values * gate_sigmoid * up_values).astype(bf16)
+    else:
+        feed_values, hidden = feed(feed_input, both_full, hidden_part)
+    hidden, feed_slope.rest = tie(hidden, feed_slope.rest)
     feed_slope = feed_slope.result()
-    hidden_slope = dot(feed_slope, down_full, NT)
-    gate_sigmoid = jax.nn.sigmoid(gate_values)
-    hidden = (gate_values * gate_sigmoid * up_values).astype(bf16)
-    gate_slope = (
-        hidden_slope * up_values * gate_sigmoid * (1.0 + gate_values * (1.0 - gate_sigmoid))
-    ).astype(bf16)
-    up_slope = (hidden_slope * gate_values * gate_sigmoid).astype(bf16)
-    both_slope = jnp.concatenate([gate_slope, up_slope], axis=1)
+    if hidden_part % 128:
+        hidden_slope = dot(feed_slope, down_full, NT)
+        gate_slope = (
+            hidden_slope * up_values * gate_sigmoid * (1.0 + gate_values * (1.0 - gate_sigmoid))
+        ).astype(bf16)
+        up_slope = (hidden_slope * gate_values * gate_sigmoid).astype(bf16)
+        both_slope = jnp.concatenate([gate_slope, up_slope], axis=1)
+    else:
+        both_slope = feed_back(feed_slope, down_full, feed_values)
 
     def by_chip(share):
         return [share[r * token_count : (r + 1) * token_count] for r in range(chips)]
@@ -689,111 +854,116 @@
 
     feed_share = dot(both_slope, both_full, NT).astype(bf16)
     feed_share, both_slope, hidden = tie(feed_share, both_slope, hidden)
-    second_parts = to_chips(by_chip(feed_share))
-    down_rows_two = swap_rows(dot(hidden, feed_slope, TN).astype(bf16))
-    both_slope, down_rows_two = tie(both_slope, down_rows_two)
-    down_part = lax.psum_scatter(add(*down_rows_two), "seq", scatter_dimension=0, tiled=True)
+    second_slope = ChipSum(by_chip(feed_share))
+    second_slope.first()
+    down_share = dot(hidden, feed_slope, TN).astype(bf16)
+    second_slope.came, down_share, both_slope = tie(second_slope.came, down_share, both_slope)
+    second_slope.second()
+    down_two = swap_rows(down_share)
+    down_two, both_slope = tie(down_two, both_slope)
+    down_part = lax.psum_scatter(add(*down_two), "seq", scatter_dimension=0, tiled=True)
     both_lanes = LaneSum(dot(feed_input, both_slope, TN).astype(bf16))
     both_stack = jnp.stack(both_lanes.blocks())
-    second_parts, both_stack = tie(second_parts, both_stack)
+    second_slope.ends, both_stack = tie(second_slope.ends, both_stack)
     both_part = lax.psum_scatter(both_stack, "seq", scatter_dimension=1, tiled=True)
-    second_slope = add_all(second_parts)
+    second_slope = second_slope.result()
     second_gain_share = jnp.sum(second_slope * second_normed, axis=0)
     middle_slope = slopes.astype(f32) + norm_backward(
         second_slope * second_scale, second_normed, second_inverse
     )
     attention_slope = middle_slope.astype(bf16)
     attended_slope = dot(attention_slope, output_full, NT).astype(bf16)
-
-    attended_slope, attention_slope, first_input, attended = tie(
-        attended_slope, attention_slope, first_input, attended
-    )
-    slope_chunks = to_chips([attention_slope] * chips)
-    attended_columns = to_chips(for_chips(attended))
-    first_columns = to_chips(for_chips(first_input))
+    payload = [
+        jnp.concatenate([attention_slope, *both], axis=1)
+        for both in zip(for_chips(attended), for_chips(first_input))
+    ]
+
+    attended_slope, payload = tie(attended_slope, payload)
+    payload = to_chips(payload)
     query_turned, pair_terms = attend_backward(
         queries, attended_slope, all_pairs, raw_outputs, log_sums, 0, group // 2
     )
-    query_turned, pair_terms, slope_chunks, attended_columns, first_columns, down_part = tie(
-        query_turned, pair_terms, slope_chunks, attended_columns, first_columns, down_part
+    query_turned, pair_terms, payload, down_part = tie(
+        query_turned, pair_terms, payload, down_part
     )
 
     pair_slope = GroupSum(pair_terms.reshape(token_count * group, -1))
     down_sum = lax.all_gather(down_part, "seq", axis=0, tiled=True)
     query_slope = turn_back(query_turned, cosine, sine)
+    pair_slope.came, query_slope, payload = tie(pair_slope.came, query_slope, payload)
+    pair_slope.along_x()
+    payload = jnp.concatenate(payload)
+    output_share = dot(payload[:, width : width + 2 * own_rows], payload[:, :width], TN)
+    first_columns = payload[:, width + 2 * own_rows :]
     query_side = dot(query_slope, query_full, NT)
-    pair_slope.came, query_slope, query_side, both_part, hidden, slope_chunks = tie(
-        pair_slope.came, query_slope, query_side, both_part, hidden, slope_chunks
-    )
-    pair_slope.along_x()
+    pair_slope.came, output_share, query_side, query_slope, both_part, hidden = tie(
+        pair_slope.came, output_share.astype(bf16), query_side, query_slope, both_part, hidden
+    )
+    pair_slope.along_seq()
     both_part = to_chips([both_part[r] for r in range(chips)])
-    out_share = dot(hidden, down_full).astype(bf16)
-    output_share = dot(
-        jnp.concatenate(attended_columns), jnp.concatenate(slope_chunks), TN
-    ).astype(bf16)
-    pair_slope.came, both_part, out_share, output_share, query_slope = tie(
-        pair_slope.came, both_part, out_share, output_share, query_slope
-    )
-    pair_slope.along_seq()
-    both_stack = jnp.stack(both_part)
     query_chunks = to_chips([query_slope] * chips)
     output_own = add(*swap_rows(output_share))
-    pair_slope.came, output_own, both_stack, down_sum = tie(
-        pair_slope.came, output_own, both_stack, down_sum
-    )
-    both_sums = lax.all_gather(both_stack, "seq", axis=1, tiled=True)
-    outputs = LineSum(output_own)
+    out_share = dot(hidden, down_full).astype(bf16)
+    pair_slope.came, both_part, output_own, out_share = tie(
+        pair_slope.came, both_part, output_own, out_share
+    )
+    both_sums = lax.all_gather(jnp.stack(both_part), "seq", axis=1, tiled=True)
     kv_slope = turn_back(pair_slope.result().astype(bf16), pair_cosine, pair_sine)
     first_slope = query_side + dot(kv_slope, pair_weight[:, : 2 * kv_width], NT)
     input_gradient = middle_slope + norm_backward(
         first_slope * first_scale, first_normed, first_inverse
     )
     gain_shares = jnp.stack([jnp.sum(first_slope * first_normed, axis=0), second_gain_share])
-    input_gradient, kv_slope, gain_shares, query_chunks, outputs.moving = tie(
-        input_gradient.astype(bf16),
-        kv_slope,
-        gain_shares.astype(bf16),
-        query_chunks,
-        outputs.moving,
+    input_gradient, kv_slope, gain_shares, query_chunks = tie(
+        input_gradient.astype(bf16), kv_slope, gain_shares.astype(bf16), query_chunks
     )
     kv_chunks = to_chips([kv_slope] * chips)
     gain_parts = to_chips(for_chips(gain_shares))
-    outputs.across()
-    first_columns = jnp.concatenate(first_columns)
     query_share = dot(first_columns, jnp.concatenate(query_chunks), TN).astype(bf16)
     query_own = add(*swap_rows(query_share))
-    query_own, kv_chunks, gain_parts, outputs.moving, input_gradient, out_share = tie(
-        query_own, kv_chunks, gain_parts, outputs.moving, input_gradient, out_share
-    )
-    outputs.outwards()
-    squares = LineSum(query_own)
-    input_gradient = spread(input_gradient)
+    query_own, kv_chunks, gain_parts, out_share, down_sum = tie(
+        query_own, kv_chunks, gain_parts, out_share, down_sum
+    )
     out_parts = to_chips(by_chip(out_share))
     kv_share = dot(first_columns, jnp.concatenate(kv_chunks), TN).astype(bf16)
     gain_two = swap_rows(add_all(gain_parts).T.astype(bf16))
-    pairs = jnp.concatenate(
-        [add(*swap_rows(kv_share)), jnp.pad(add(*gain_two), ((0, 0), (0, 126)))], axis=1
-    )
-    squares.moving, pairs, outputs.moving, input_gradient = tie(
-        squares.moving, pairs, outputs.moving, input_gradient
-    )
-    squares.across()
-    pairs = LineSum(pairs)
-    squares.moving, pairs.moving, out_parts = tie(squares.moving, pairs.moving, out_parts)
-    squares.outwards()
-    pairs.across()
-    layer_output = spread((middle + add_all(out_parts)).astype(bf16))
-    squares.moving, pairs.moving = tie(squares.moving, pairs.moving)
-    pairs.outwards()
-    pairs.moving, both_sums, layer_output = tie(pairs.moving, both_sums, layer_output)
-
+    last = jnp.concatenate(
+        [
+            query_own,
+            output_own,
+            add(*swap_rows(kv_share)),
+            jnp.pad(add(*gain_two), ((0, 0), (0, 126))),
+        ],
+        axis=1,
+    )
+    last, input_gradient, both_sums, down_sum = tie(last, input_gradient, both_sums, down_sum)
+    lasts = [LineTree(last[half]) for half in halves(own_rows)[:1]]
+    input_gradient = spread(input_gradient)
+    gate_gradient, up_gradient = place_columns(both_sums, chip)
+    lasts[0].moving, gate_gradient, last = tie(lasts[0].moving, gate_gradient, last)
+    lasts[0].across()
+    lasts.append(LineTree(last[halves(own_rows)[1]]))
+    layer_output = (middle + add_all(out_parts)).astype(bf16)
+    lasts[0].moving, lasts[1].moving, layer_output = tie(
+        lasts[0].moving, lasts[1].moving, layer_output
+    )
+    lasts[0].outwards()
+    lasts[1].across()
+    layer_output = spread(layer_output)
+    lasts[1].moving, input_gradient = tie(lasts[1].moving, input_gradient)
+    lasts[1].outwards()
+    down_gradient = down_sum.astype(f32)
     input_gradient = input_gradient.astype(f32)
-    down_gradient = down_sum.astype(f32)
-    query_gradient, output_gradient = squares.result(), outputs.result()
-    pairs = pairs.result()
+    lasts[0].moving, lasts[1].moving, layer_output, down_gradient, input_gradient = tie(
+        lasts[0].moving, lasts[1].moving, layer_output, down_gradient, input_gradient
+    )
+
+    last = jnp.concatenate([part.result() for part in lasts])
+    query_gradient = last[:, :width]
+    output_gradient = last[:, width : 2 * width]
+    pairs = last[:, 2 * width :]
     gain_gradients = pairs[:, 2 * kv_width : 2 * kv_width + 2].T
     pairs = pairs[:, : 2 * kv_width].reshape(own_rows, KV_HEADS, 2, HEAD_DIM)
-    gate_gradient, up_gradient = place_columns(both_sums, chip)
     return (
         layer_output,
         input_gradient,

time: 944 us -> 906 us (0.960)
  starting transfers between devices: 183 us -> 98.1 us
  waiting for transfers between devices: 319 us -> 367 us
  matrix products: 114 us -> 81.3 us
  Pallas kernels: 132 us -> 163 us
    all_to_all x4, starting transfers between devices: 90.2 us -> 21.1 us  [spread(): return lax.all_to_all(shaped, GROUP, 0, 0, tiled=True).reshape(rows.shape)]
    all_gather x1, waiting for transfers between devices: 0.01 us -> 40.4 us  [on_device(): both_sums = lax.all_gather(jnp.stack(both_part), 'seq', axis=1, tiled=True)]
    dot_general x14 -> x11, matrix products: 114 us -> 81.3 us  [dot(): return lax.dot_general(left, right, dims, preferred_element_type=f32)]
    pallas_call x0 -> x2, Pallas kernels: none -> 31.4 us  [the longest x1 19.9 us: feed(): pl.pallas_call(feed_body, grid=(tokens // tile,), out_shape=(jax.ShapeDty...]
    all_to_all x4, waiting for transfers between devices: 0.01 us -> 31.4 us  [spread(): return lax.all_to_all(shaped, GROUP, 0, 0, tiled=True).reshape(rows.shape)]
    ppermute x3 -> x2, waiting for transfers between devices: 62.5 us -> 37.4 us  [outwards(): self.moving = lax.ppermute(self.share, 'seq', [(1, 0), (2, 3)])]
    convert_element_type x5 -> x1, other arithmetic: 14.2 us -> 3.02 us  [on_device(): layer_output = (middle + add_all(out_parts)).astype(bf16)]
    ppermute x77 -> x72, waiting for transfers between devices: 226 us -> 235 us  [swap(): return lax.ppermute(values, axes, [(i, i ^ mask) for i in range(count)])]
  transfers between devices with their start and end apart: 96 -> 88, of which waited for: 37 -> 41; matrix products, arithmetic and copies ran while one was open for 22% -> 21% of each run, Pallas kernels for 14% -> 17%
where the time goes in v2:
time: 906 us; the launch traced here: 897 us
  waiting for transfers between devices  367 us (41%)
  Pallas kernels  163 us (18%)
  starting transfers between devices  98.1 us (11%)
  local copies, waits for them, and re-layouts  88.2 us (10%)
  other arithmetic  82.7 us (9%)
  matrix products  81.3 us (9%)
  between operations  16.4 us (2%)
    ppermute x72, waiting for transfers between devices, swap(): return lax.ppermute(values, axes, [(i, i ^ mask) for i in range(count)])  235 us
    dot_general x11, matrix products, dot(): return lax.dot_general(left, right, dims, preferred_element_type=f32)  81.3 us
    pallas_call x1, Pallas kernels, attend_backward(): pl.pallas_call(partial(backward_body, groups=groups, heads=heads, rows=ro...  70.2 us
    ppermute x72, starting transfers between devices, swap(): return lax.ppermute(values, axes, [(i, i ^ mask) for i in range(count)])  62.6 us
    pallas_call x1, Pallas kernels, attend_forward(): pl.pallas_call(partial(forward_body, groups=groups, heads=heads, rows=row...  45.4 us
    all_gather x1, waiting for transfers between devices, on_device(): both_sums = lax.all_gather(jnp.stack(both_part), 'seq', axis=1, tiled=True)  40.4 us
    ppermute x2, waiting for transfers between devices, outwards(): self.moving = lax.ppermute(self.share, 'seq', [(1, 0), (2, 3)])  37.4 us
    unnamed x143, local copies, waits for them, and re-layouts  35.6 us
  transfers between devices with their start and end apart: 88, of which 41 were waited for; matrix products, arithmetic and copies ran while one was open for 21% of the time, Pallas kernels for 17%

profile of v2, /device:TPU:0, one launch (start us, length us, event | category | flops | bytes accessed | tf_op | source)
XLA Modules:
  0.0 897.1 jit_solution(13499422720543727956)
XLA Ops:
  20.5 5.0 all-to-all-start
  25.5 4.3 constant_dynamic-slice_fusion.21
  37.1 13.7 %collective-permute-done.5 = bf16[128,640]{1,0:T(8,128)(2,1)S(1)} collective-permute-done((bf16[128,640]{1,0:T(8,128)(2,1)S(1)}, bf16[128,640]{1,0:T(8,128)(2,1)S(1)}, u32[]{:S(2)}, u32[]{:S(2)}) %collective-permute-start.5) | collective-permute-done | bytes 163872 | tf_op jit(solution)/shard_map/ppermute | solution.py:55
  63.8 3.4 collective-permute-start.14
  68.4 5.0 broadcast_in_dim.44
  78.2 10.0 %collective-permute-done.9 = bf16[256,512]{1,0:T(8,128)(2,1)S(1)} collective-permute-done((bf16[256,512]{1,0:T(8,128)(2,1)S(1)}, bf16[256,512]{1,0:T(8,128)(2,1)S(1)}, u32[]{:S(2)}, u32[]{:S(2)}) %collective-permute-start.9) | collective-permute-done | bytes 262176 | tf_op jit(solution)/shard_map/ppermute | solution.py:55
  90.5 4.5 collective-permute-done.12
  95.1 5.5 collective-permute-done.15
  100.7 5.9 collective-permute-done.18
  110.7 3.4 copy-done.4
  114.1 4.7 project.2.q_ref
  119.4 4.8 all-to-all-start.1
  130.5 45.4 %attend_forward.1 = (bf16[256,2048]{1,0:T(8,128)(2,1)S(1)}, f32[8,4,64,256]{3,2,1,0:T(8,128)S(1)}, f32[8,4,256]{2,1,0:T(4,128)S(1)}) custom-call(bf16[256,2048]{1,0:T(8,128)(2,1)S(1)} %project.2.q_ref, bf16[16,16,16,512]{3,2,1,0:T(8,128)(2,1)S(1)} %bitcast.91), custom_call_target="tpu_custom_call" | custom-call | flops 36507222016 | bytes 6291456 | tf_op jit(solution)/shard_map/attend_forward/pallas_call | solution.py:399
  179.8 6.1 multiply_reduce_fusion.2
  194.4 5.8 maximum_select_fusion.d_ref
  200.3 21.2 %collective-permute-done.26 = bf16[256,2816]{1,0:T(8,128)(2,1)} collective-permute-done((bf16[256,2816]{1,0:T(8,128)(2,1)}, bf16[256,2816]{1,0:T(8,128)(2,1)}, u32[]{:S(2)}, u32[]{:S(2)}) %collective-permute-start.26) | collective-permute-done | bytes 1441824 | tf_op jit(solution)/shard_map/ppermute | solution.py:55
  221.4 21.3 %collective-permute-done.22 = bf16[256,2048]{1,0:T(8,128)(2,1)S(1)} collective-permute-done((bf16[256,2048]{1,0:T(8,128)(2,1)}, bf16[256,2048]{1,0:T(8,128)(2,1)S(1)}, u32[]{:S(2)}, u32[]{:S(2)}) %collective-permute-start.22) | collective-permute-done | bytes 1048608 | tf_op jit(solution)/shard_map/ppermute | solution.py:55
  252.0 28.1 %collective-permute-done.29 = bf16[128,2048]{1,0:T(8,128)(2,1)S(1)} collective-permute-done((bf16[128,2048]{1,0:T(8,128)(2,1)S(1)}, bf16[128,2048]{1,0:T(8,128)(2,1)S(1)}, u32[]{:S(2)}, u32[]{:S(2)}) %collective-permute-start.29) | collective-permute-done | bytes 524320 | tf_op jit(solution)/shard_map/ppermute | solution.py:55
  293.7 19.9 %feed.1 = (f32[1024,2816]{1,0:T(8,128)}, bf16[1024,1408]{1,0:T(8,128)(2,1)S(1)}) custom-call(bf16[1024,2048]{1,0:T(8,128)(2,1)S(1)} %constant_dynamic-update-slice_fusion.12.x_ref, bf16[2048,2816]{1,0:T(8,128)(2,1)} %constant_dynamic-update-slice_fusion.26.w_ref), custom_call_target="tpu_custom_call" | custom-call | flops 11811160064 | bytes 30146560 | tf_op jit(solution)/shard_map/feed/pallas_call | solution.py:662
  313.7 11.5 %feed_back.1 = bf16[1024,2816]{1,0:T(8,128)(2,1)S(1)} custom-call(bf16[1024,2048]{1,0:T(8,128)(2,1)S(1)} %constant_dynamic-update-slice_fusion.17.c_ref, bf16[1408,2048]{1,0:T(8,128)(2,1)S(1)} %maximum_select_fusion.d_ref, f32[1024,2816]{1,0:T(8,128)} %get-tuple-element.162.values_ref), custom_call_target="tpu_custom_call" | custom-call | flops 5905580032 | bytes 27262976 | tf_op jit(solution)/shard_map/feed_back/pallas_call | solution.py:691
  325.2 18.4 %convolution_convert_fusion.2 = bf16[1024,2048]{1,0:T(8,128)(2,1)} fusion(bf16[1024,2816]{1,0:T(8,128)(2,1)S(1)} %feed_back.1, bf16[2048,2816]{1,0:T(8,128)(2,1)} %constant_dynamic-update-slice_fusion.26.w_ref), kind=kOutput, calls=%fused_computation.19 | convolution fusion | flops 11813257216 | bytes 21495808 | tf_op jit(solution)/shard_map/dot_general | solution.py:28
  348.5 6.5 convolution_convert_fusion.1
  355.0 5.1 collective-permute-done.36
  362.1 5.3 collective-permute-done.40
  370.2 16.0 %convolution_convert_fusion = bf16[2048,2816]{1,0:T(8,128)(2,1)S(1)} fusion(bf16[1024,2048]{1,0:T(8,128)(2,1)} %copy-done.16, bf16[1024,2816]{1,0:T(8,128)(2,1)} %copy-done.6), kind=kOutput, calls=%fused_computation | convolution fusion | flops 11816927232 | bytes 21495808 | tf_op jit(solution)/shard_map/dot_general | solution.py:28
  397.2 5.3 fusion.38
  402.5 4.2 pad_maximum_fusion
  406.7 9.2 %collective-permute-done.38 = bf16[256,2048]{1,0:T(8,128)(2,1)} collective-permute-done((bf16[256,2048]{1,0:T(8,128)(2,1)}, bf16[256,2048]{1,0:T(8,128)(2,1)}, u32[]{:S(2)}, u32[]{:S(2)}) %collective-permute-start.38) | collective-permute-done | bytes 1048608 | tf_op jit(solution)/shard_map/ppermute | solution.py:55
  419.0 2.8 multiply_reduce_fusion
  421.8 4.7 fusion.71
  426.5 3.9 fusion.37
  430.4 5.9 convolution_convert_fusion.4.do_ref
  439.8 70.2 %attend_backward.1 = (bf16[256,2048]{1,0:T(8,128)(2,1)S(1)}, bf16[16,16,16,512]{3,2,1,0:T(8,128)(2,1)S(1)}) custom-call(bf16[256,2048]{1,0:T(8,128)(2,1)S(1)} %project.2.q_ref, bf16[256,2048]{1,0:T(8,128)(2,1)S(1)} %convolution_convert_fusion.4.do_ref, bf16[16,16,16,512]{3,2,1,0:T(8,128)(2,1)S(1)} %bitcast.92, f32[8,4,64,256]{3,2,1,0:T(8,128)S(1)} %copy-done.12, ...), custom_call_target="tpu_custom_call" | custom-call | flops 285212672 | bytes 8388608 | tf_op jit(solution)/shard_map/attend_backward/pallas_call | solution.py:529
  515.3 3.8 fusion.74
  520.7 4.2 turn_back.2
  526.3 2.9 fusion.11
  536.2 3.7 fusion.16
  539.9 3.7 fusion.77
  543.6 11.2 %collective-permute-done.49 = bf16[4,256,512]{2,1,0:T(8,128)(2,1)S(1)} collective-permute-done((bf16[4,256,512]{2,1,0:T(8,128)(2,1)S(1)}, bf16[4,256,512]{2,1,0:T(8,128)(2,1)S(1)}, u32[]{:S(2)}, u32[]{:S(2)}) %collective-permute-start.49) | collective-permute-done | bytes 1048608 | tf_op jit(solution)/shard_map/ppermute | solution.py:55
  561.5 11.0 %convolution_convert_fusion.3 = bf16[1024,2048]{1,0:T(8,128)(2,1)} fusion(bf16[1024,1408]{1,0:T(8,128)(2,1)S(1)} %copy-done.18, bf16[1408,2048]{1,0:T(8,128)(2,1)} %copy-done), kind=kOutput, calls=%fused_computation.20 | convolution fusion | flops 5907677184 | bytes 12845056 | tf_op jit(solution)/shard_map/dot_general | solution.py:28
  572.5 8.5 collective-permute-done.50
  585.3 3.8 collective-permute-done.51
  589.0 4.9 collective-permute-done.52
  593.9 4.0 collective-permute-done.54
  606.7 3.1 fusion.30
  609.8 3.0 fusion.29
  612.8 12.9 %collective-permute-done.57 = bf16[256,2048]{1,0:T(8,128)(2,1)} collective-permute-done((bf16[256,2048]{1,0:T(8,128)(2,1)}, bf16[256,2048]{1,0:T(8,128)(2,1)}, u32[]{:S(2)}, u32[]{:S(2)}) %collective-permute-start.57) | collective-permute-done | bytes 1048608 | tf_op jit(solution)/shard_map/ppermute | solution.py:55
  625.7 21.2 %collective-permute-done.58 = bf16[256,2048]{1,0:T(8,128)(2,1)} collective-permute-done((bf16[256,2048]{1,0:T(8,128)(2,1)}, bf16[256,2048]{1,0:T(8,128)(2,1)}, u32[]{:S(2)}, u32[]{:S(2)}) %collective-permute-start.58) | collective-permute-done | bytes 1048608 | tf_op jit(solution)/shard_map/ppermute | solution.py:55
  646.9 4.7 fusion.19
  663.7 11.7 %collective-permute-done.65 = bf16[2,512]{0,1:T(8,128)(2,1)S(1)} collective-permute-done((bf16[2,512]{0,1:T(8,128)(2,1)}, bf16[2,512]{0,1:T(8,128)(2,1)S(1)}, u32[]{:S(2)}, u32[]{:S(2)}) %collective-permute-start.65) | collective-permute-done | bytes 2080 | tf_op jit(solution)/shard_map/ppermute | solution.py:55
  680.8 40.4 %all-gather.11.cloned.1.call-done.values_ref = bf16[4,256,2816]{2,1,0:T(8,128)(2,1)} async-done(((bf16[4,64,2816]{2,1,0:T(8,128)(2,1)}), bf16[4,256,2816]{2,1,0:T(8,128)(2,1)}) %all-gather.11.cloned.1.call-update) | async-done | bytes 5767184 | tf_op jit(solution)/shard_map/all_gather | solution.py:910
  728.7 4.4 place_columns.1
  733.1 16.1 %collective-permute-done.69 = bf16[128,4736]{1,0:T(8,128)(2,1)S(1)} collective-permute-done((bf16[128,4736]{1,0:T(8,128)(2,1)S(1)}, bf16[128,4736]{1,0:T(8,128)(2,1)S(1)}, u32[]{:S(2)}, u32[]{:S(2)}) %collective-permute-start.69) | collective-permute-done | bytes 1212448 | tf_op jit(solution)/shard_map/ppermute | solution.py:177
  753.3 7.0 collective-permute-start.71
  760.3 13.4 %collective-permute-done.73 = bf16[256,2048]{1,0:T(8,128)(2,1)S(1)} collective-permute-done((bf16[256,2048]{1,0:T(8,128)(2,1)S(1)}, bf16[256,2048]{1,0:T(8,128)(2,1)S(1)}, u32[]{:S(2)}, u32[]{:S(2)}) %collective-permute-start.73) | collective-permute-done | bytes 1048608 | tf_op jit(solution)/shard_map/ppermute | solution.py:55
  773.8 3.0 add_convert_fusion.9
  776.8 4.5 all-to-all-start.2
  781.3 4.8 collective-permute-done.71
  792.7 12.1 %all-to-all-done.2 = bf16[16,16,2048]{2,1,0:T(8,128)(2,1)S(1)} async-done(((bf16[16,16,2048]{2,1,0:T(8,128)(2,1)}), bf16[16,16,2048]{2,1,0:T(8,128)(2,1)S(1)}, u32[]{:S(2)}, u32[]{:S(2)}) %all-to-all-start.2) | async-done | bytes 1048608 | tf_op jit(solution)/shard_map/all_to_all | solution.py:249
  804.7 6.8 all-to-all-start.3
  815.8 5.1 convert_element_type.382
  822.5 11.0 %collective-permute-done.75 = bf16[128,4736]{1,0:T(8,128)(2,1)} collective-permute-done((bf16[128,4736]{1,0:T(8,128)(2,1)S(1)}, bf16[128,4736]{1,0:T(8,128)(2,1)}, u32[]{:S(2)}, u32[]{:S(2)}) %collective-permute-start.75) | collective-permute-done | bytes 1212448 | tf_op jit(solution)/shard_map/ppermute | solution.py:185
  833.5 19.3 %all-to-all-done.3 = bf16[16,16,2048]{2,1,0:T(8,128)(2,1)} async-done(((bf16[16,16,2048]{2,1,0:T(8,128)(2,1)}), bf16[16,16,2048]{2,1,0:T(8,128)(2,1)}, u32[]{:S(2)}, u32[]{:S(2)}) %all-to-all-start.3) | async-done | bytes 1048608 | tf_op jit(solution)/shard_map/all_to_all | solution.py:249
  852.8 26.4 %collective-permute-done.77 = bf16[128,4736]{1,0:T(8,128)(2,1)} collective-permute-done((bf16[128,4736]{1,0:T(8,128)(2,1)S(1)}, bf16[128,4736]{1,0:T(8,128)(2,1)}, u32[]{:S(2)}, u32[]{:S(2)}) %collective-permute-start.77) | collective-permute-done | bytes 1212448 | tf_op jit(solution)/shard_map/ppermute | solution.py:185
  (405 shorter events, 201.4 us)
Async XLA Ops:
  7.2 103.6 %all-gather.5.cloned.1.call-start = ((), (), s32[]{:S(2)}) async-start(), calls=%async_computation.6 | async-start | bytes 9437184 | tf_op jit(solution)/shard_map/all_gather | solution.py:749
  7.9 171.9 %all-gather.7.cloned.1.call-start = ((), (), s32[]{:S(2)}) async-start(), calls=%async_computation.7 | async-start | bytes 9437184 | tf_op jit(solution)/shard_map/all_gather | solution.py:750
  13.4 22.7 %collective-permute-start = (bf16[256,640]{1,0:T(8,128)(2,1)}, bf16[256,640]{1,0:T(8,128)(2,1)}, u32[]{:S(2)}, u32[]{:S(2)}) collective-permute-start(bf16[256,640]{1,0:T(8,128)(2,1)} %get-tuple-element.339), channel_id=1, source_target_pairs={{0,1},{1,0},{2,3},{3,2},{16,17},{17,16},{18,19},{19,18},{4,5},{5,4... | collective-permute-start | bytes 983048 | tf_op jit(solution)/shard_map/ppermute | solution.py:55
  13.8 19.6 %collective-permute-start.1 = (bf16[256,640]{1,0:T(8,128)(2,1)}, bf16[256,640]{1,0:T(8,128)(2,1)S(1)}, u32[]{:S(2)}, u32[]{:S(2)}) collective-permute-start(bf16[256,640]{1,0:T(8,128)(2,1)} %get-tuple-element.339), channel_id=1, source_target_pairs={{0,2},{1,3},{2,0},{3,1},{16,18},{17,19},{18,16},{19,17},{4,6},{5,7... | collective-permute-start | bytes 983048 | tf_op jit(solution)/shard_map/ppermute | solution.py:55
  16.3 17.5 %collective-permute-start.3 = (bf16[256,640]{1,0:T(8,128)(2,1)}, bf16[256,640]{1,0:T(8,128)(2,1)S(1)}, u32[]{:S(2)}, u32[]{:S(2)}) collective-permute-start(bf16[256,640]{1,0:T(8,128)(2,1)} %get-tuple-element.339), channel_id=1, source_target_pairs={{0,16},{1,17},{2,18},{3,19},{16,0},{17,1},{18,2},{19,3},{4,20},{5,... | collective-permute-start | bytes 983048 | tf_op jit(solution)/shard_map/ppermute | solution.py:55
  20.5 33.0 %all-to-all-start = ((bf16[16,16,2176]{2,1,0:T(8,128)(2,1)}), bf16[16,16,2176]{2,1,0:T(8,128)(2,1)}, u32[]{:S(2)}, u32[]{:S(2)}) async-start(bf16[16,16,2176]{2,1,0:T(8,128)(2,1)} %bitcast.94), calls=%async_computation | async-start | bytes 2228224 | tf_op jit(solution)/shard_map/all_to_all | solution.py:249
  33.4 17.9 %collective-permute-start.2 = (bf16[256,640]{1,0:T(8,128)(2,1)S(1)}, bf16[256,640]{1,0:T(8,128)(2,1)S(1)}, u32[]{:S(2)}, u32[]{:S(2)}) collective-permute-start(bf16[256,640]{1,0:T(8,128)(2,1)S(1)} %collective-permute-done.1), channel_id=1, source_target_pairs={{0,1},{1,0},{2,3},{3,2},{16,17},{17,16},{18,19},{19,18},{4,5},{5,4... | collective-permute-start | bytes 983048 | tf_op jit(solution)/shard_map/ppermute | solution.py:55
  33.8 17.0 %collective-permute-start.5 = (bf16[128,640]{1,0:T(8,128)(2,1)S(1)}, bf16[128,640]{1,0:T(8,128)(2,1)S(1)}, u32[]{:S(2)}, u32[]{:S(2)}) collective-permute-start(bf16[128,640]{1,0:T(8,128)(2,1)S(1)} %slice.215), channel_id=1, source_target_pairs={{0,2},{1,3},{2,0},{3,1},{16,18},{17,19},{18,16},{19,17},{4,6},{5,7... | collective-permute-start | bytes 491528 | tf_op jit(solution)/shard_map/ppermute | solution.py:55
  36.1 15.4 %collective-permute-start.4 = (bf16[256,640]{1,0:T(8,128)(2,1)S(1)}, bf16[256,640]{1,0:T(8,128)(2,1)S(1)}, u32[]{:S(2)}, u32[]{:S(2)}) collective-permute-start(bf16[256,640]{1,0:T(8,128)(2,1)S(1)} %collective-permute-done.3), channel_id=1, source_target_pairs={{0,1},{1,0},{2,3},{3,2},{16,17},{17,16},{18,19},{19,18},{4,5},{5,4... | collective-permute-start | bytes 983048 | tf_op jit(solution)/shard_map/ppermute | solution.py:55
  63.8 24.5 %collective-permute-start.14 = (bf16[256,512]{1,0:T(8,128)(2,1)S(1)}, bf16[256,512]{1,0:T(8,128)(2,1)S(1)}, u32[]{:S(2)}, u32[]{:S(2)}) collective-permute-start(bf16[256,512]{1,0:T(8,128)(2,1)S(1)} %project.3), channel_id=1, source_target_pairs={{0,8},{4,12},{8,0},{12,4},{1,9},{5,13},{9,1},{13,5},{2,10},{6,14},... | collective-permute-start | bytes 786440 | tf_op jit(solution)/shard_map/ppermute | solution.py:55
  67.2 22.2 %collective-permute-start.17 = (bf16[256,512]{1,0:T(8,128)(2,1)S(1)}, bf16[256,512]{1,0:T(8,128)(2,1)S(1)}, u32[]{:S(2)}, u32[]{:S(2)}) collective-permute-start(bf16[256,512]{1,0:T(8,128)(2,1)S(1)} %project.3), channel_id=1, source_target_pairs={{0,12},{4,8},{8,4},{12,0},{1,13},{5,9},{9,5},{13,1},{2,14},{6,10},... | collective-permute-start | bytes 786440 | tf_op jit(solution)/shard_map/ppermute | solution.py:55
  77.0 18.0 %collective-permute-start.12 = (bf16[256,512]{1,0:T(8,128)(2,1)S(1)}, bf16[256,512]{1,0:T(8,128)(2,1)S(1)}, u32[]{:S(2)}, u32[]{:S(2)}) collective-permute-start(bf16[256,512]{1,0:T(8,128)(2,1)S(1)} %collective-permute-done.11), channel_id=1, source_target_pairs={{0,2},{1,3},{2,0},{3,1},{4,6},{5,7},{6,4},{7,5},{8,10},{9,11},{10,... | collective-permute-start | bytes 786440 | tf_op jit(solution)/shard_map/ppermute | solution.py:55
  88.2 18.5 %collective-permute-start.10 = (bf16[512,512]{1,0:T(8,128)(2,1)S(1)}, bf16[512,512]{1,0:T(8,128)(2,1)S(1)}, u32[]{:S(2)}, u32[]{:S(2)}) collective-permute-start(bf16[512,512]{1,0:T(8,128)(2,1)S(1)} %pad_maximum_fusion.12), channel_id=1, source_target_pairs={{0,1},{1,0},{2,3},{3,2},{4,5},{5,4},{6,7},{7,6},{8,9},{9,8},{10,11... | collective-permute-start | bytes 1572872 | tf_op jit(solution)/shard_map/ppermute | solution.py:55
  89.3 17.3 %collective-permute-start.18 = (bf16[256,512]{1,0:T(8,128)(2,1)S(1)}, bf16[256,512]{1,0:T(8,128)(2,1)S(1)}, u32[]{:S(2)}, u32[]{:S(2)}) collective-permute-start(bf16[256,512]{1,0:T(8,128)(2,1)S(1)} %collective-permute-done.17), channel_id=1, source_target_pairs={{0,2},{1,3},{2,0},{3,1},{4,6},{5,7},{6,4},{7,5},{8,10},{9,11},{10,... | collective-permute-start | bytes 786440 | tf_op jit(solution)/shard_map/ppermute | solution.py:55
  118.8 60.9 %collective-permute-start.20 = (bf16[704,2048]{1,0:T(8,128)(2,1)}, bf16[704,2048]{1,0:T(8,128)(2,1)}, u32[]{:S(2)}, u32[]{:S(2)}) collective-permute-start(bf16[704,2048]{1,0:T(8,128)(2,1)} %param.21), channel_id=1, source_target_pairs={{0,1},{1,0},{2,3},{3,2},{16,17},{17,16},{18,19},{19,18},{4,5},{5,4... | collective-permute-start | bytes 8650760 | tf_op jit(solution)/shard_map/ppermute | solution.py:55
  119.0 60.7 %collective-permute-start.21 = (bf16[256,2816]{1,0:T(8,128)(2,1)}, bf16[256,2816]{1,0:T(8,128)(2,1)}, u32[]{:S(2)}, u32[]{:S(2)}) collective-permute-start(bf16[256,2816]{1,0:T(8,128)(2,1)} %pad_maximum_fusion.5), channel_id=1, source_target_pairs={{0,1},{1,0},{2,3},{3,2},{16,17},{17,16},{18,19},{19,18},{4,5},{5,4... | collective-permute-start | bytes 4325384 | tf_op jit(solution)/shard_map/ppermute | solution.py:55
  119.4 69.0 %all-to-all-start.1 = ((bf16[16,16,2048]{2,1,0:T(8,128)(2,1)}), bf16[16,16,2048]{2,1,0:T(8,128)(2,1)}, u32[]{:S(2)}, u32[]{:S(2)}) async-start(bf16[16,16,2048]{2,1,0:T(8,128)(2,1)} %bitcast.99), calls=%async_computation.1 | async-start | bytes 2097152 | tf_op jit(solution)/shard_map/all_to_all | solution.py:249
  124.2 391.2 %reduce-scatter.3.cloned.1.call-start = ((), (), s32[]{:S(2)}) async-start(), calls=%async_computation.8 | async-start | bytes 3604480 | tf_op jit(solution)/shard_map/reduce_scatter | solution.py:864
  124.7 75.5 %collective-permute-start.24 = (bf16[256,2816]{1,0:T(8,128)(2,1)}, bf16[256,2816]{1,0:T(8,128)(2,1)}, u32[]{:S(2)}, u32[]{:S(2)}) collective-permute-start(bf16[256,2816]{1,0:T(8,128)(2,1)} %pad_maximum_fusion.6), channel_id=1, source_target_pairs={{0,2},{1,3},{2,0},{3,1},{16,18},{17,19},{18,16},{19,17},{4,6},{5,7... | collective-permute-start | bytes 4325384 | tf_op jit(solution)/shard_map/ppermute | solution.py:55
  126.6 73.6 %collective-permute-start.25 = (bf16[256,2816]{1,0:T(8,128)(2,1)}, bf16[256,2816]{1,0:T(8,128)(2,1)}, u32[]{:S(2)}, u32[]{:S(2)}) collective-permute-start(bf16[256,2816]{1,0:T(8,128)(2,1)} %pad_maximum_fusion.7), channel_id=1, source_target_pairs={{0,16},{1,17},{2,18},{3,19},{16,0},{17,1},{18,2},{19,3},{4,20},{5,... | collective-permute-start | bytes 4325384 | tf_op jit(solution)/shard_map/ppermute | solution.py:55
  128.1 93.3 %collective-permute-start.26 = (bf16[256,2816]{1,0:T(8,128)(2,1)}, bf16[256,2816]{1,0:T(8,128)(2,1)}, u32[]{:S(2)}, u32[]{:S(2)}) collective-permute-start(bf16[256,2816]{1,0:T(8,128)(2,1)} %pad_maximum_fusion.8), channel_id=1, source_target_pairs={{0,18},{1,19},{2,16},{3,17},{16,2},{17,3},{18,0},{19,1},{4,22},{5,... | collective-permute-start | bytes 4325384 | tf_op jit(solution)/shard_map/ppermute | solution.py:55
  188.4 54.3 %collective-permute-start.22 = (bf16[256,2048]{1,0:T(8,128)(2,1)}, bf16[256,2048]{1,0:T(8,128)(2,1)S(1)}, u32[]{:S(2)}, u32[]{:S(2)}) collective-permute-start(bf16[256,2048]{1,0:T(8,128)(2,1)} %multiply_convert_fusion), channel_id=1, source_target_pairs={{0,2},{1,3},{2,0},{3,1},{16,18},{17,19},{18,16},{19,17},{4,6},{5,7... | collective-permute-start | bytes 3145736 | tf_op jit(solution)/shard_map/ppermute | solution.py:55
  190.3 53.2 %collective-permute-start.23 = (bf16[256,2048]{1,0:T(8,128)(2,1)}, bf16[256,2048]{1,0:T(8,128)(2,1)S(1)}, u32[]{:S(2)}, u32[]{:S(2)}) collective-permute-start(bf16[256,2048]{1,0:T(8,128)(2,1)} %multiply_convert_fusion), channel_id=1, source_target_pairs={{0,16},{1,17},{2,18},{3,19},{16,0},{17,1},{18,2},{19,3},{4,20},{5,... | collective-permute-start | bytes 3145736 | tf_op jit(solution)/shard_map/ppermute | solution.py:55
  243.6 37.0 %collective-permute-start.27 = (bf16[256,2048]{1,0:T(8,128)(2,1)}, bf16[256,2048]{1,0:T(8,128)(2,1)S(1)}, u32[]{:S(2)}, u32[]{:S(2)}) collective-permute-start(bf16[256,2048]{1,0:T(8,128)(2,1)} %bitcast.9), channel_id=1, source_target_pairs={{0,2},{1,3},{2,0},{3,1},{16,18},{17,19},{18,16},{19,17},{4,6},{5,7... | collective-permute-start | bytes 3145736 | tf_op jit(solution)/shard_map/ppermute | solution.py:55
  244.1 36.5 %collective-permute-start.28 = (bf16[256,2048]{1,0:T(8,128)(2,1)}, bf16[256,2048]{1,0:T(8,128)(2,1)S(1)}, u32[]{:S(2)}, u32[]{:S(2)}) collective-permute-start(bf16[256,2048]{1,0:T(8,128)(2,1)} %bitcast.9), channel_id=1, source_target_pairs={{0,16},{1,17},{2,18},{3,19},{16,0},{17,1},{18,2},{19,3},{4,20},{5,... | collective-permute-start | bytes 3145736 | tf_op jit(solution)/shard_map/ppermute | solution.py:55
  244.8 35.3 %collective-permute-start.29 = (bf16[128,2048]{1,0:T(8,128)(2,1)S(1)}, bf16[128,2048]{1,0:T(8,128)(2,1)S(1)}, u32[]{:S(2)}, u32[]{:S(2)}) collective-permute-start(bf16[128,2048]{1,0:T(8,128)(2,1)S(1)} %slice.174), channel_id=1, source_target_pairs={{0,2},{1,3},{2,0},{3,1},{16,18},{17,19},{18,16},{19,17},{4,6},{5,7... | collective-permute-start | bytes 1572872 | tf_op jit(solution)/shard_map/ppermute | solution.py:55
  246.4 34.0 %collective-permute-start.30 = (bf16[128,2048]{1,0:T(8,128)(2,1)S(1)}, bf16[128,2048]{1,0:T(8,128)(2,1)S(1)}, u32[]{:S(2)}, u32[]{:S(2)}) collective-permute-start(bf16[128,2048]{1,0:T(8,128)(2,1)S(1)} %slice.175), channel_id=1, source_target_pairs={{0,16},{1,17},{2,18},{3,19},{16,0},{17,1},{18,2},{19,3},{4,20},{5,... | collective-permute-start | bytes 1572872 | tf_op jit(solution)/shard_map/ppermute | solution.py:55
  247.9 36.5 %collective-permute-start.31 = (bf16[256,2816]{1,0:T(8,128)(2,1)}, bf16[256,2816]{1,0:T(8,128)(2,1)S(1)}, u32[]{:S(2)}, u32[]{:S(2)}) collective-permute-start(bf16[256,2816]{1,0:T(8,128)(2,1)} %collective-permute-done.24), channel_id=1, source_target_pairs={{0,1},{1,0},{2,3},{3,2},{16,17},{17,16},{18,19},{19,18},{4,5},{5,4... | collective-permute-start | bytes 4325384 | tf_op jit(solution)/shard_map/ppermute | solution.py:55
  281.5 32.1 %collective-permute-start.34 = (bf16[128,2048]{1,0:T(8,128)(2,1)}, bf16[128,2048]{1,0:T(8,128)(2,1)S(1)}, u32[]{:S(2)}, u32[]{:S(2)}) collective-permute-start(bf16[128,2048]{1,0:T(8,128)(2,1)} %slice.176), channel_id=1, source_target_pairs={{0,2},{1,3},{2,0},{3,1},{16,18},{17,19},{18,16},{19,17},{4,6},{5,7... | collective-permute-start | bytes 1572872 | tf_op jit(solution)/shard_map/ppermute | solution.py:55
  283.5 30.1 %collective-permute-start.35 = (bf16[128,2048]{1,0:T(8,128)(2,1)}, bf16[128,2048]{1,0:T(8,128)(2,1)S(1)}, u32[]{:S(2)}, u32[]{:S(2)}) collective-permute-start(bf16[128,2048]{1,0:T(8,128)(2,1)} %slice.177), channel_id=1, source_target_pairs={{0,16},{1,17},{2,18},{3,19},{16,0},{17,1},{18,2},{19,3},{4,20},{5,... | collective-permute-start | bytes 1572872 | tf_op jit(solution)/shard_map/ppermute | solution.py:55
  370.2 184.6 %reduce-scatter.5.cloned.1.call-start = ((), (), s32[]{:S(2)}) async-start(), calls=%async_computation.9 | async-start | bytes 7208960 | tf_op jit(solution)/shard_map/reduce_scatter | solution.py:868
  390.4 25.5 %collective-permute-start.38 = (bf16[256,2048]{1,0:T(8,128)(2,1)}, bf16[256,2048]{1,0:T(8,128)(2,1)}, u32[]{:S(2)}, u32[]{:S(2)}) collective-permute-start(bf16[256,2048]{1,0:T(8,128)(2,1)} %pad_maximum_fusion.10), channel_id=1, source_target_pairs={{0,2},{1,3},{2,0},{3,1},{16,18},{17,19},{18,16},{19,17},{4,6},{5,7... | collective-permute-start | bytes 3145736 | tf_op jit(solution)/shard_map/ppermute | solution.py:55
  392.0 25.3 %collective-permute-start.39 = (bf16[256,2048]{1,0:T(8,128)(2,1)}, bf16[256,2048]{1,0:T(8,128)(2,1)}, u32[]{:S(2)}, u32[]{:S(2)}) collective-permute-start(bf16[256,2048]{1,0:T(8,128)(2,1)} %pad_maximum_fusion.11), channel_id=1, source_target_pairs={{0,16},{1,17},{2,18},{3,19},{16,0},{17,1},{18,2},{19,3},{4,20},{5,... | collective-permute-start | bytes 3145736 | tf_op jit(solution)/shard_map/ppermute | solution.py:55
  417.3 246.4 %all-gather.9.cloned.1.call-start = ((), (), s32[]{:S(2)}) async-start(), calls=%async_computation.10 | async-start | bytes 3604480 | tf_op jit(solution)/shard_map/all_gather | solution.py:891
  436.3 76.8 %collective-permute-start.45 = (bf16[256,3072]{1,0:T(8,128)(2,1)S(1)}, bf16[256,3072]{1,0:T(8,128)(2,1)S(1)}, u32[]{:S(2)}, u32[]{:S(2)}) collective-permute-start(bf16[256,3072]{1,0:T(8,128)(2,1)S(1)} %get-tuple-element.180), channel_id=1, source_target_pairs={{0,2},{1,3},{2,0},{3,1},{16,18},{17,19},{18,16},{19,17},{4,6},{5,7... | collective-permute-start | bytes 4718600 | tf_op jit(solution)/shard_map/ppermute | solution.py:55
  437.8 75.3 %collective-permute-start.46 = (bf16[256,3072]{1,0:T(8,128)(2,1)S(1)}, bf16[256,3072]{1,0:T(8,128)(2,1)S(1)}, u32[]{:S(2)}, u32[]{:S(2)}) collective-permute-start(bf16[256,3072]{1,0:T(8,128)(2,1)S(1)} %get-tuple-element.181), channel_id=1, source_target_pairs={{0,16},{1,17},{2,18},{3,19},{16,0},{17,1},{18,2},{19,3},{4,20},{5,... | collective-permute-start | bytes 4718600 | tf_op jit(solution)/shard_map/ppermute | solution.py:55
  438.5 76.9 %collective-permute-start.47 = (bf16[256,3072]{1,0:T(8,128)(2,1)S(1)}, bf16[256,3072]{1,0:T(8,128)(2,1)}, u32[]{:S(2)}, u32[]{:S(2)}) collective-permute-start(bf16[256,3072]{1,0:T(8,128)(2,1)S(1)} %get-tuple-element.182), channel_id=1, source_target_pairs={{0,18},{1,19},{2,16},{3,17},{16,2},{17,3},{18,0},{19,1},{4,22},{5,... | collective-permute-start | bytes 4718600 | tf_op jit(solution)/shard_map/ppermute | solution.py:55
  520.6 200.5 %all-gather.11.cloned.1.call-start = ((), (), s32[]{:S(2)}) async-start(), calls=%async_computation.11 | async-start | bytes 7208960 | tf_op jit(solution)/shard_map/all_gather | solution.py:910
  529.3 25.5 %collective-permute-start.49 = (bf16[4,256,512]{2,1,0:T(8,128)(2,1)S(1)}, bf16[4,256,512]{2,1,0:T(8,128)(2,1)S(1)}, u32[]{:S(2)}, u32[]{:S(2)}) collective-permute-start(bf16[4,256,512]{2,1,0:T(8,128)(2,1)S(1)} %slice_bitcast_fusion.1), channel_id=1, source_target_pairs={{0,2},{1,3},{2,0},{3,1},{4,6},{5,7},{6,4},{7,5},{8,10},{9,11},{10,... | collective-permute-start | bytes 3145736 | tf_op jit(solution)/shard_map/ppermute | solution.py:55
  555.2 25.8 %collective-permute-start.50 = (bf16[256,512]{1,0:T(8,128)(2,1)S(1)}, bf16[256,512]{1,0:T(8,128)(2,1)S(1)}, u32[]{:S(2)}, u32[]{:S(2)}) collective-permute-start(bf16[256,512]{1,0:T(8,128)(2,1)S(1)} %get-tuple-element.320), channel_id=1, source_target_pairs={{0,4},{4,0},{8,12},{12,8},{1,5},{5,1},{9,13},{13,9},{2,6},{6,2},{1... | collective-permute-start | bytes 786440 | tf_op jit(solution)/shard_map/ppermute | solution.py:55
  556.7 32.3 %collective-permute-start.51 = (bf16[256,512]{1,0:T(8,128)(2,1)S(1)}, bf16[256,512]{1,0:T(8,128)(2,1)S(1)}, u32[]{:S(2)}, u32[]{:S(2)}) collective-permute-start(bf16[256,512]{1,0:T(8,128)(2,1)S(1)} %get-tuple-element.319), channel_id=1, source_target_pairs={{0,8},{4,12},{8,0},{12,4},{1,9},{5,13},{9,1},{13,5},{2,10},{6,14},... | collective-permute-start | bytes 786440 | tf_op jit(solution)/shard_map/ppermute | solution.py:55
  559.2 34.7 %collective-permute-start.52 = (bf16[256,512]{1,0:T(8,128)(2,1)S(1)}, bf16[256,512]{1,0:T(8,128)(2,1)S(1)}, u32[]{:S(2)}, u32[]{:S(2)}) collective-permute-start(bf16[256,512]{1,0:T(8,128)(2,1)S(1)} %get-tuple-element.318), channel_id=1, source_target_pairs={{0,12},{4,8},{8,4},{12,0},{1,13},{5,9},{9,5},{13,1},{2,14},{6,10},... | collective-permute-start | bytes 786440 | tf_op jit(solution)/shard_map/ppermute | solution.py:55
  559.7 34.2 %collective-permute-start.53 = (bf16[64,2816]{1,0:T(8,128)(2,1)S(1)}, bf16[64,2816]{1,0:T(8,128)(2,1)S(1)}, u32[]{:S(2)}, u32[]{:S(2)}) collective-permute-start(bf16[64,2816]{1,0:T(8,128)(2,1)S(1)} %get-tuple-element.316), channel_id=1, source_target_pairs={{0,2},{1,3},{2,0},{3,1},{16,18},{17,19},{18,16},{19,17},{4,6},{5,7... | collective-permute-start | bytes 1081352 | tf_op jit(solution)/shard_map/ppermute | solution.py:55
  561.4 20.3 %collective-permute-start.56 = (bf16[256,2048]{1,0:T(8,128)(2,1)S(1)}, bf16[256,2048]{1,0:T(8,128)(2,1)S(1)}, u32[]{:S(2)}, u32[]{:S(2)}) collective-permute-start(bf16[256,2048]{1,0:T(8,128)(2,1)S(1)} %constant_dynamic-slice_fusion.6), channel_id=1, source_target_pairs={{0,1},{1,0},{2,3},{3,2},{16,17},{17,16},{18,19},{19,18},{4,5},{5,4... | collective-permute-start | bytes 3145736 | tf_op jit(solution)/shard_map/ppermute | solution.py:55
  581.0 16.9 %collective-permute-start.54 = (bf16[64,2816]{1,0:T(8,128)(2,1)S(1)}, bf16[64,2816]{1,0:T(8,128)(2,1)S(1)}, u32[]{:S(2)}, u32[]{:S(2)}) collective-permute-start(bf16[64,2816]{1,0:T(8,128)(2,1)S(1)} %get-tuple-element.315), channel_id=1, source_target_pairs={{0,16},{1,17},{2,18},{3,19},{16,0},{17,1},{18,2},{19,3},{4,20},{5,... | collective-permute-start | bytes 1081352 | tf_op jit(solution)/shard_map/ppermute | solution.py:55
  581.7 16.2 %collective-permute-start.55 = (bf16[64,2816]{1,0:T(8,128)(2,1)S(1)}, bf16[64,2816]{1,0:T(8,128)(2,1)S(1)}, u32[]{:S(2)}, u32[]{:S(2)}) collective-permute-start(bf16[64,2816]{1,0:T(8,128)(2,1)S(1)} %get-tuple-element.314), channel_id=1, source_target_pairs={{0,18},{1,19},{2,16},{3,17},{16,2},{17,3},{18,0},{19,1},{4,22},{5,... | collective-permute-start | bytes 1081352 | tf_op jit(solution)/shard_map/ppermute | solution.py:55
  599.2 26.5 %collective-permute-start.57 = (bf16[256,2048]{1,0:T(8,128)(2,1)}, bf16[256,2048]{1,0:T(8,128)(2,1)}, u32[]{:S(2)}, u32[]{:S(2)}) collective-permute-start(bf16[256,2048]{1,0:T(8,128)(2,1)} %turn_back.2), channel_id=1, source_target_pairs={{0,2},{1,3},{2,0},{3,1},{16,18},{17,19},{18,16},{19,17},{4,6},{5,7... | collective-permute-start | bytes 3145736 | tf_op jit(solution)/shard_map/ppermute | solution.py:55
  600.8 46.2 %collective-permute-start.58 = (bf16[256,2048]{1,0:T(8,128)(2,1)}, bf16[256,2048]{1,0:T(8,128)(2,1)}, u32[]{:S(2)}, u32[]{:S(2)}) collective-permute-start(bf16[256,2048]{1,0:T(8,128)(2,1)} %turn_back.2), channel_id=1, source_target_pairs={{0,16},{1,17},{2,18},{3,19},{16,0},{17,1},{18,2},{19,3},{4,20},{5,... | collective-permute-start | bytes 3145736 | tf_op jit(solution)/shard_map/ppermute | solution.py:55
  601.6 45.3 %collective-permute-start.59 = (bf16[256,2048]{1,0:T(8,128)(2,1)}, bf16[256,2048]{1,0:T(8,128)(2,1)}, u32[]{:S(2)}, u32[]{:S(2)}) collective-permute-start(bf16[256,2048]{1,0:T(8,128)(2,1)} %turn_back.2), channel_id=1, source_target_pairs={{0,18},{1,19},{2,16},{3,17},{16,2},{17,3},{18,0},{19,1},{4,22},{5,... | collective-permute-start | bytes 3145736 | tf_op jit(solution)/shard_map/ppermute | solution.py:55
  654.3 21.1 %collective-permute-start.61 = (bf16[256,512]{1,0:T(8,128)(2,1)}, bf16[256,512]{1,0:T(8,128)(2,1)}, u32[]{:S(2)}, u32[]{:S(2)}) collective-permute-start(bf16[256,512]{1,0:T(8,128)(2,1)} %turn_back.3), channel_id=1, source_target_pairs={{0,2},{1,3},{2,0},{3,1},{16,18},{17,19},{18,16},{19,17},{4,6},{5,7... | collective-permute-start | bytes 786440 | tf_op jit(solution)/shard_map/ppermute | solution.py:55
  655.8 19.6 %collective-permute-start.62 = (bf16[256,512]{1,0:T(8,128)(2,1)}, bf16[256,512]{1,0:T(8,128)(2,1)}, u32[]{:S(2)}, u32[]{:S(2)}) collective-permute-start(bf16[256,512]{1,0:T(8,128)(2,1)} %turn_back.3), channel_id=1, source_target_pairs={{0,16},{1,17},{2,18},{3,19},{16,0},{17,1},{18,2},{19,3},{4,20},{5,... | collective-permute-start | bytes 786440 | tf_op jit(solution)/shard_map/ppermute | solution.py:55
  656.4 19.1 %collective-permute-start.63 = (bf16[256,512]{1,0:T(8,128)(2,1)}, bf16[256,512]{1,0:T(8,128)(2,1)}, u32[]{:S(2)}, u32[]{:S(2)}) collective-permute-start(bf16[256,512]{1,0:T(8,128)(2,1)} %turn_back.3), channel_id=1, source_target_pairs={{0,18},{1,19},{2,16},{3,17},{16,2},{17,3},{18,0},{19,1},{4,22},{5,... | collective-permute-start | bytes 786440 | tf_op jit(solution)/shard_map/ppermute | solution.py:55
  660.1 15.3 %collective-permute-start.65 = (bf16[2,512]{0,1:T(8,128)(2,1)}, bf16[2,512]{0,1:T(8,128)(2,1)S(1)}, u32[]{:S(2)}, u32[]{:S(2)}) collective-permute-start(bf16[2,512]{0,1:T(8,128)(2,1)} %get-tuple-element.336), channel_id=1, source_target_pairs={{0,16},{1,17},{2,18},{3,19},{16,0},{17,1},{18,2},{19,3},{4,20},{5,... | collective-permute-start | bytes 6152 | tf_op jit(solution)/shard_map/ppermute | solution.py:55
  721.3 28.0 %collective-permute-start.69 = (bf16[128,4736]{1,0:T(8,128)(2,1)S(1)}, bf16[128,4736]{1,0:T(8,128)(2,1)S(1)}, u32[]{:S(2)}, u32[]{:S(2)}) collective-permute-start(bf16[128,4736]{1,0:T(8,128)(2,1)S(1)} %slice.200), channel_id=1, source_target_pairs={{0,4},{12,8},{1,5},{13,9},{2,6},{14,10},{3,7},{15,11},{16,20},{28,... | collective-permute-start | bytes 3637256 | tf_op jit(solution)/shard_map/ppermute | solution.py:177
  725.2 35.2 %collective-permute-start.74 = (bf16[256,2048]{1,0:T(8,128)(2,1)S(1)}, bf16[256,2048]{1,0:T(8,128)(2,1)S(1)}, u32[]{:S(2)}, u32[]{:S(2)}) collective-permute-start(bf16[256,2048]{1,0:T(8,128)(2,1)S(1)} %get-tuple-element.296), channel_id=1, source_target_pairs={{0,18},{1,19},{2,16},{3,17},{16,2},{17,3},{18,0},{19,1},{4,22},{5,... | collective-permute-start | bytes 3145736 | tf_op jit(solution)/shard_map/ppermute | solution.py:55
  727.6 46.1 %collective-permute-start.73 = (bf16[256,2048]{1,0:T(8,128)(2,1)S(1)}, bf16[256,2048]{1,0:T(8,128)(2,1)S(1)}, u32[]{:S(2)}, u32[]{:S(2)}) collective-permute-start(bf16[256,2048]{1,0:T(8,128)(2,1)S(1)} %get-tuple-element.297), channel_id=1, source_target_pairs={{0,16},{1,17},{2,18},{3,19},{16,0},{17,1},{18,2},{19,3},{4,20},{5,... | collective-permute-start | bytes 3145736 | tf_op jit(solution)/shard_map/ppermute | solution.py:55
  728.2 45.6 %collective-permute-start.72 = (bf16[256,2048]{1,0:T(8,128)(2,1)S(1)}, bf16[256,2048]{1,0:T(8,128)(2,1)S(1)}, u32[]{:S(2)}, u32[]{:S(2)}) collective-permute-start(bf16[256,2048]{1,0:T(8,128)(2,1)S(1)} %get-tuple-element.295), channel_id=1, source_target_pairs={{0,2},{1,3},{2,0},{3,1},{16,18},{17,19},{18,16},{19,17},{4,6},{5,7... | collective-permute-start | bytes 3145736 | tf_op jit(solution)/shard_map/ppermute | solution.py:55
  750.5 30.8 %collective-permute-start.70 = (bf16[128,4736]{1,0:T(8,128)(2,1)}, bf16[128,4736]{1,0:T(8,128)(2,1)}, u32[]{:S(2)}, u32[]{:S(2)}) collective-permute-start(bf16[128,4736]{1,0:T(8,128)(2,1)} %add_convert_fusion.8), channel_id=1, source_target_pairs={{4,8},{8,4},{5,9},{9,5},{6,10},{10,6},{7,11},{11,7},{20,24},{24,20... | collective-permute-start | bytes 3637256 | tf_op jit(solution)/shard_map/ppermute | solution.py:181
  753.3 32.8 %collective-permute-start.71 = (bf16[128,4736]{1,0:T(8,128)(2,1)}, bf16[128,4736]{1,0:T(8,128)(2,1)}, u32[]{:S(2)}, u32[]{:S(2)}) collective-permute-start(bf16[128,4736]{1,0:T(8,128)(2,1)} %slice.201), channel_id=1, source_target_pairs={{0,4},{12,8},{1,5},{13,9},{2,6},{14,10},{3,7},{15,11},{16,20},{28,... | collective-permute-start | bytes 3637256 | tf_op jit(solution)/shard_map/ppermute | solution.py:177
  776.8 27.9 %all-to-all-start.2 = ((bf16[16,16,2048]{2,1,0:T(8,128)(2,1)}), bf16[16,16,2048]{2,1,0:T(8,128)(2,1)S(1)}, u32[]{:S(2)}, u32[]{:S(2)}) async-start(bf16[16,16,2048]{2,1,0:T(8,128)(2,1)} %bitcast.96), calls=%async_computation.4 | async-start | bytes 2097152 | tf_op jit(solution)/shard_map/all_to_all | solution.py:249
  788.7 22.9 %collective-permute-start.76 = (bf16[128,4736]{1,0:T(8,128)(2,1)}, bf16[128,4736]{1,0:T(8,128)(2,1)S(1)}, u32[]{:S(2)}, u32[]{:S(2)}) collective-permute-start(bf16[128,4736]{1,0:T(8,128)(2,1)} %add_convert_fusion.6), channel_id=1, source_target_pairs={{4,8},{8,4},{5,9},{9,5},{6,10},{10,6},{7,11},{11,7},{20,24},{24,20... | collective-permute-start | bytes 3637256 | tf_op jit(solution)/shard_map/ppermute | solution.py:181
  791.4 42.1 %collective-permute-start.75 = (bf16[128,4736]{1,0:T(8,128)(2,1)S(1)}, bf16[128,4736]{1,0:T(8,128)(2,1)}, u32[]{:S(2)}, u32[]{:S(2)}) collective-permute-start(bf16[128,4736]{1,0:T(8,128)(2,1)S(1)} %add_convert_fusion.7), channel_id=1, source_target_pairs={{4,0},{8,12},{5,1},{9,13},{6,2},{10,14},{7,3},{11,15},{20,16},{24,... | collective-permute-start | bytes 3637256 | tf_op jit(solution)/shard_map/ppermute | solution.py:185
  804.7 48.1 %all-to-all-start.3 = ((bf16[16,16,2048]{2,1,0:T(8,128)(2,1)}), bf16[16,16,2048]{2,1,0:T(8,128)(2,1)}, u32[]{:S(2)}, u32[]{:S(2)}) async-start(bf16[16,16,2048]{2,1,0:T(8,128)(2,1)} %bitcast.36), calls=%async_computation.5 | async-start | bytes 2097152 | tf_op jit(solution)/shard_map/all_to_all | solution.py:249
  814.5 64.7 %collective-permute-start.77 = (bf16[128,4736]{1,0:T(8,128)(2,1)S(1)}, bf16[128,4736]{1,0:T(8,128)(2,1)}, u32[]{:S(2)}, u32[]{:S(2)}) collective-permute-start(bf16[128,4736]{1,0:T(8,128)(2,1)S(1)} %add_convert_fusion.5), channel_id=1, source_target_pairs={{4,0},{8,12},{5,1},{9,13},{6,2},{10,14},{7,3},{11,15},{20,16},{24,... | collective-permute-start | bytes 3637256 | tf_op jit(solution)/shard_map/ppermute | solution.py:185
  (81 other events, 693.0 us)
Sparse Core Ops, SparseCore 0:
  9.9 82.5 all-gather.4
  94.3 82.8 all-gather.6
  370.3 55.3 reduce-scatter.2
  428.4 102.0 reduce-scatter.4
  532.0 81.8 all-gather.8
  615.8 105.3 all-gather.10

commit v3 on v2

--- a/solution.py
+++ b/solution.py
@@ -345,20 +345,25 @@
         q = stack_heads(q_ref[...], heads, rows, g * heads)
         qs[g] = jnp.concatenate([q, jnp.zeros((width, HEAD_DIM), bf16)], axis=1)
 
-    def tiles(kt, lo, first):
+    def tiles(kts, lo, first):
         scores = []
         for g in range(groups):
-            kv = kv_ref[:, kt, :, g * 128 : (g + 1) * 128].reshape(keys, 128)
-            scores.append(dot(kv, qs[g, lo:], NT))
+            for kt in kts:
+                kv = kv_ref[:, kt, :, g * 128 : (g + 1) * 128].reshape(keys, 128)
+                scores.append(dot(kv, qs[g, lo:], NT))
         for g in range(groups):
-            st = scores[g]
-            peak = jnp.max(st, axis=0, keepdims=True)
+            sts = scores[g * len(kts) : (g + 1) * len(kts)]
+            peak = jnp.max(sts[0], axis=0, keepdims=True)
+            for st in sts[1:]:
+                peak = jnp.maximum(peak, jnp.max(st, axis=0, keepdims=True))
             if not first:
                 m_old = m_s[g, :, lo:]
                 peak = jnp.maximum(m_old, peak)
-            p = jnp.exp2(st - peak)
-            total = jnp.sum(p, axis=0, keepdims=True)
-            pv = dot(kvt[g, kt], p.astype(bf16))
+            total, pv = 0.0, 0.0
+            for kt, st in zip(kts, sts):
+                p = jnp.exp2(st - peak)
+                total = total + jnp.sum(p, axis=0, keepdims=True)
+                pv = pv + dot(kvt[g, kt], p.astype(bf16))
             if first:
                 l_s[g, :, lo:] = total
                 ot_ref[0, g, :, lo:] = pv
@@ -368,13 +373,13 @@
                 ot_ref[0, g, :, lo:] = ot_ref[0, g, :, lo:] * shrink + pv
             m_s[g, :, lo:] = peak
 
-    def step(kt, carry):
-        tiles(kt, 0, False)
+    def step(i, carry):
+        tiles((2 * i + 1, 2 * i + 2), 0, False)
         return carry
 
-    tiles(0, 0, True)
-    lax.fori_loop(1, 2 * c + 1, step, 0)
-    tiles(2 * c + 1, half, False)
+    tiles((0,), 0, True)
+    lax.fori_loop(0, c, step, 0)
+    tiles((2 * c + 1,), half, False)
     for g in range(groups):
         total = l_s[g]
         o = ot_ref[0, g] / total
@@ -815,7 +820,9 @@
         both_full = lax.dynamic_update_slice_in_dim(
             both_full, other, (owner ^ (2 * r + 1)) * own_rows, 0
         )
-    feed_slope.ends, feed_input.rest = tie(feed_slope.ends, feed_input.rest)
+    feed_slope.ends, feed_input.rest, both_full = tie(
+        feed_slope.ends, feed_input.rest, both_full
+    )
     feed_slope.second()
     feed_input = feed_input.result()
 

time: 906 us -> 899 us (level)
    ppermute x72, waiting for transfers between devices: 235 us -> 220 us  [swap(): return lax.ppermute(values, axes, [(i, i ^ mask) for i in range(count)])]
  transfers between devices with their start and end apart: 88 -> 88, of which waited for: 41 -> 41; matrix products, arithmetic and copies ran while one was open for 21% -> 22% of each run, Pallas kernels for 17% -> 16%
where the time goes in v3:
time: 899 us; the launch traced here: 889 us
  waiting for transfers between devices  359 us (40%)
  Pallas kernels  156 us (17%)
  starting transfers between devices  98.3 us (11%)
  local copies, waits for them, and re-layouts  94.5 us (11%)
  other arithmetic  84.4 us (9%)
  matrix products  81.2 us (9%)
  between operations  16.4 us (2%)
    ppermute x72, waiting for transfers between devices, swap(): return lax.ppermute(values, axes, [(i, i ^ mask) for i in range(count)])  220 us
    dot_general x11, matrix products, dot(): return lax.dot_general(left, right, dims, preferred_element_type=f32)  81.2 us
    pallas_call x1, Pallas kernels, attend_backward(): pl.pallas_call(partial(backward_body, groups=groups, heads=heads, rows=ro...  70.2 us
    ppermute x72, starting transfers between devices, swap(): return lax.ppermute(values, axes, [(i, i ^ mask) for i in range(count)])  62.9 us
    all_gather x1, waiting for transfers between devices, on_device(): both_sums = lax.all_gather(jnp.stack(both_part), 'seq', axis=1, tiled=True)  41.1 us
    unnamed x143, local copies, waits for them, and re-layouts  39.8 us
    ppermute x2, waiting for transfers between devices, outwards(): self.moving = lax.ppermute(self.share, 'seq', [(1, 0), (2, 3)])  37.4 us
    pallas_call x1, Pallas kernels, attend_forward(): pl.pallas_call(partial(forward_body, groups=groups, heads=heads, rows=row...  36.4 us
  transfers between devices with their start and end apart: 88, of which 41 were waited for; matrix products, arithmetic and copies ran while one was open for 22% of the time, Pallas kernels for 16%

profile of v3, /device:TPU:0, one launch (start us, length us, event | category | flops | bytes accessed | tf_op | source)
XLA Modules:
  0.0 889.4 jit_solution(17127130433746879460)
XLA Ops:
  20.5 5.0 all-to-all-start
  25.5 4.3 constant_dynamic-slice_fusion.21
  37.1 13.7 %collective-permute-done.5 = bf16[128,640]{1,0:T(8,128)(2,1)S(1)} collective-permute-done((bf16[128,640]{1,0:T(8,128)(2,1)S(1)}, bf16[128,640]{1,0:T(8,128)(2,1)S(1)}, u32[]{:S(2)}, u32[]{:S(2)}) %collective-permute-start.5) | collective-permute-done | bytes 163872 | tf_op jit(solution)/shard_map/ppermute | solution.py:55
  63.8 3.4 collective-permute-start.14
  68.4 5.0 broadcast_in_dim.44
  78.2 10.0 %collective-permute-done.9 = bf16[256,512]{1,0:T(8,128)(2,1)S(1)} collective-permute-done((bf16[256,512]{1,0:T(8,128)(2,1)S(1)}, bf16[256,512]{1,0:T(8,128)(2,1)S(1)}, u32[]{:S(2)}, u32[]{:S(2)}) %collective-permute-start.9) | collective-permute-done | bytes 262176 | tf_op jit(solution)/shard_map/ppermute | solution.py:55
  90.5 4.5 collective-permute-done.12
  95.1 5.5 collective-permute-done.15
  100.7 5.9 collective-permute-done.18
  110.7 3.4 copy-done.3
  114.1 4.7 project.2.q_ref
  119.4 4.8 all-to-all-start.1
  130.4 36.4 %attend_forward.1 = (bf16[256,2048]{1,0:T(8,128)(2,1)S(1)}, f32[8,4,64,256]{3,2,1,0:T(8,128)S(1)}, f32[8,4,256]{2,1,0:T(4,128)S(1)}) custom-call(bf16[256,2048]{1,0:T(8,128)(2,1)S(1)} %project.2.q_ref, bf16[16,16,16,512]{3,2,1,0:T(8,128)(2,1)S(1)} %bitcast.93), custom_call_target="tpu_custom_call" | custom-call | flops 36507222016 | bytes 6291456 | tf_op jit(solution)/shard_map/attend_forward/pallas_call | solution.py:404
  170.8 6.5 all-gather.7.cloned.1.call-done
  177.2 6.1 multiply_reduce_fusion.2
  190.7 7.6 maximum_select_fusion.d_ref
  198.3 23.1 %collective-permute-done.26 = bf16[256,2816]{1,0:T(8,128)(2,1)} collective-permute-done((bf16[256,2816]{1,0:T(8,128)(2,1)}, bf16[256,2816]{1,0:T(8,128)(2,1)}, u32[]{:S(2)}, u32[]{:S(2)}) %collective-permute-start.26) | collective-permute-done | bytes 1441824 | tf_op jit(solution)/shard_map/ppermute | solution.py:55
  221.4 21.4 %collective-permute-done.22 = bf16[256,2048]{1,0:T(8,128)(2,1)} collective-permute-done((bf16[256,2048]{1,0:T(8,128)(2,1)}, bf16[256,2048]{1,0:T(8,128)(2,1)}, u32[]{:S(2)}, u32[]{:S(2)}) %collective-permute-start.22) | collective-permute-done | bytes 1048608 | tf_op jit(solution)/shard_map/ppermute | solution.py:55
  267.7 13.5 %collective-permute-done.29 = bf16[128,2048]{1,0:T(8,128)(2,1)S(1)} collective-permute-done((bf16[128,2048]{1,0:T(8,128)(2,1)S(1)}, bf16[128,2048]{1,0:T(8,128)(2,1)S(1)}, u32[]{:S(2)}, u32[]{:S(2)}) %collective-permute-start.29) | collective-permute-done | bytes 524320 | tf_op jit(solution)/shard_map/ppermute | solution.py:55
  285.5 21.5 %feed.1 = (f32[1024,2816]{1,0:T(8,128)}, bf16[1024,1408]{1,0:T(8,128)(2,1)S(1)}) custom-call(bf16[1024,2048]{1,0:T(8,128)(2,1)S(1)} %constant_dynamic-update-slice_fusion.12.x_ref, bf16[2048,2816]{1,0:T(8,128)(2,1)} %constant_dynamic-update-slice_fusion.26.w_ref), custom_call_target="tpu_custom_call" | custom-call | flops 11811160064 | bytes 30146560 | tf_op jit(solution)/shard_map/feed/pallas_call | solution.py:667
  307.3 11.3 %feed_back.1 = bf16[1024,2816]{1,0:T(8,128)(2,1)S(1)} custom-call(bf16[1024,2048]{1,0:T(8,128)(2,1)S(1)} %constant_dynamic-update-slice_fusion.17.c_ref, bf16[1408,2048]{1,0:T(8,128)(2,1)S(1)} %bitcast.90, f32[1024,2816]{1,0:T(8,128)} %get-tuple-element.164.values_ref), custom_call_target="tpu_custom_call" | custom-call | flops 5905580032 | bytes 27262976 | tf_op jit(solution)/shard_map/feed_back/pallas_call | solution.py:696
  318.6 18.4 %convolution_convert_fusion.2 = bf16[1024,2048]{1,0:T(8,128)(2,1)} fusion(bf16[1024,2816]{1,0:T(8,128)(2,1)S(1)} %feed_back.1, bf16[2048,2816]{1,0:T(8,128)(2,1)} %constant_dynamic-update-slice_fusion.26.w_ref), kind=kOutput, calls=%fused_computation.19 | convolution fusion | flops 11813257216 | bytes 21495808 | tf_op jit(solution)/shard_map/dot_general | solution.py:28
  341.5 6.5 convolution_convert_fusion.1
  348.0 4.3 collective-permute-done.36
  353.6 5.3 collective-permute-done.40
  361.7 16.0 %convolution_convert_fusion = bf16[2048,2816]{1,0:T(8,128)(2,1)S(1)} fusion(bf16[1024,2048]{1,0:T(8,128)(2,1)} %copy-done.15, bf16[1024,2816]{1,0:T(8,128)(2,1)} %copy-done.5), kind=kOutput, calls=%fused_computation | convolution fusion | flops 11816927232 | bytes 21495808 | tf_op jit(solution)/shard_map/dot_general | solution.py:28
  388.7 5.3 fusion.38
  394.0 4.2 pad_maximum_fusion
  398.2 9.2 %collective-permute-done.38 = bf16[256,2048]{1,0:T(8,128)(2,1)} collective-permute-done((bf16[256,2048]{1,0:T(8,128)(2,1)}, bf16[256,2048]{1,0:T(8,128)(2,1)}, u32[]{:S(2)}, u32[]{:S(2)}) %collective-permute-start.38) | collective-permute-done | bytes 1048608 | tf_op jit(solution)/shard_map/ppermute | solution.py:55
  414.0 4.7 fusion.71
  418.7 3.8 fusion.37
  422.5 5.9 convolution_convert_fusion.4.do_ref
  432.0 70.2 %attend_backward.1 = (bf16[256,2048]{1,0:T(8,128)(2,1)S(1)}, bf16[16,16,16,512]{3,2,1,0:T(8,128)(2,1)S(1)}) custom-call(bf16[256,2048]{1,0:T(8,128)(2,1)S(1)} %project.2.q_ref, bf16[256,2048]{1,0:T(8,128)(2,1)S(1)} %convolution_convert_fusion.4.do_ref, bf16[16,16,16,512]{3,2,1,0:T(8,128)(2,1)S(1)} %bitcast.94, f32[8,4,64,256]{3,2,1,0:T(8,128)S(1)} %copy-done.11, ...), custom_call_target="tpu_custom_call" | custom-call | flops 285212672 | bytes 8388608 | tf_op jit(solution)/shard_map/attend_backward/pallas_call | solution.py:534
  507.5 3.8 fusion.74
  512.8 4.2 turn_back.2
  518.5 2.9 fusion.11
  528.3 3.7 fusion.16
  532.0 3.7 fusion.77
  535.7 11.3 %collective-permute-done.49 = bf16[4,256,512]{2,1,0:T(8,128)(2,1)S(1)} collective-permute-done((bf16[4,256,512]{2,1,0:T(8,128)(2,1)S(1)}, bf16[4,256,512]{2,1,0:T(8,128)(2,1)S(1)}, u32[]{:S(2)}, u32[]{:S(2)}) %collective-permute-start.49) | collective-permute-done | bytes 1048608 | tf_op jit(solution)/shard_map/ppermute | solution.py:55
  553.1 11.0 %convolution_convert_fusion.3 = bf16[1024,2048]{1,0:T(8,128)(2,1)} fusion(bf16[1024,1408]{1,0:T(8,128)(2,1)S(1)} %copy-done.17, bf16[1408,2048]{1,0:T(8,128)(2,1)} %maximum_select_fusion.d_ref), kind=kOutput, calls=%fused_computation.20 | convolution fusion | flops 5907677184 | bytes 12845056 | tf_op jit(solution)/shard_map/dot_general | solution.py:28
  564.1 9.0 %collective-permute-done.50 = bf16[256,512]{1,0:T(8,128)(2,1)S(1)} collective-permute-done((bf16[256,512]{1,0:T(8,128)(2,1)S(1)}, bf16[256,512]{1,0:T(8,128)(2,1)S(1)}, u32[]{:S(2)}, u32[]{:S(2)}) %collective-permute-start.50) | collective-permute-done | bytes 262176 | tf_op jit(solution)/shard_map/ppermute | solution.py:55
  576.8 4.4 collective-permute-done.51
  581.2 4.9 collective-permute-done.52
  586.1 3.9 collective-permute-done.54
  598.8 3.1 fusion.30
  601.9 3.0 fusion.29
  604.9 12.9 %collective-permute-done.57 = bf16[256,2048]{1,0:T(8,128)(2,1)} collective-permute-done((bf16[256,2048]{1,0:T(8,128)(2,1)}, bf16[256,2048]{1,0:T(8,128)(2,1)}, u32[]{:S(2)}, u32[]{:S(2)}) %collective-permute-start.57) | collective-permute-done | bytes 1048608 | tf_op jit(solution)/shard_map/ppermute | solution.py:55
  617.8 20.8 %collective-permute-done.58 = bf16[256,2048]{1,0:T(8,128)(2,1)} collective-permute-done((bf16[256,2048]{1,0:T(8,128)(2,1)}, bf16[256,2048]{1,0:T(8,128)(2,1)}, u32[]{:S(2)}, u32[]{:S(2)}) %collective-permute-start.58) | collective-permute-done | bytes 1048608 | tf_op jit(solution)/shard_map/ppermute | solution.py:55
  638.6 4.6 fusion.19
  656.2 10.8 %collective-permute-done.65 = bf16[2,512]{0,1:T(8,128)(2,1)S(1)} collective-permute-done((bf16[2,512]{0,1:T(8,128)(2,1)}, bf16[2,512]{0,1:T(8,128)(2,1)S(1)}, u32[]{:S(2)}, u32[]{:S(2)}) %collective-permute-start.65) | collective-permute-done | bytes 2080 | tf_op jit(solution)/shard_map/ppermute | solution.py:55
  672.3 41.1 %all-gather.11.cloned.1.call-done.values_ref = bf16[4,256,2816]{2,1,0:T(8,128)(2,1)} async-done(((bf16[4,64,2816]{2,1,0:T(8,128)(2,1)}), bf16[4,256,2816]{2,1,0:T(8,128)(2,1)}) %all-gather.11.cloned.1.call-update) | async-done | bytes 5767184 | tf_op jit(solution)/shard_map/all_gather | solution.py:917
  721.0 4.4 place_columns.1
  725.4 16.1 %collective-permute-done.69 = bf16[128,4736]{1,0:T(8,128)(2,1)S(1)} collective-permute-done((bf16[128,4736]{1,0:T(8,128)(2,1)S(1)}, bf16[128,4736]{1,0:T(8,128)(2,1)S(1)}, u32[]{:S(2)}, u32[]{:S(2)}) %collective-permute-start.69) | collective-permute-done | bytes 1212448 | tf_op jit(solution)/shard_map/ppermute | solution.py:177
  745.7 7.0 collective-permute-start.71
  752.6 13.4 %collective-permute-done.73 = bf16[256,2048]{1,0:T(8,128)(2,1)S(1)} collective-permute-done((bf16[256,2048]{1,0:T(8,128)(2,1)S(1)}, bf16[256,2048]{1,0:T(8,128)(2,1)S(1)}, u32[]{:S(2)}, u32[]{:S(2)}) %collective-permute-start.73) | collective-permute-done | bytes 1048608 | tf_op jit(solution)/shard_map/ppermute | solution.py:55
  766.1 3.0 add_convert_fusion.9
  769.1 4.5 all-to-all-start.2
  773.6 4.8 collective-permute-done.71
  785.0 12.1 %all-to-all-done.2 = bf16[16,16,2048]{2,1,0:T(8,128)(2,1)S(1)} async-done(((bf16[16,16,2048]{2,1,0:T(8,128)(2,1)}), bf16[16,16,2048]{2,1,0:T(8,128)(2,1)S(1)}, u32[]{:S(2)}, u32[]{:S(2)}) %all-to-all-start.2) | async-done | bytes 1048608 | tf_op jit(solution)/shard_map/all_to_all | solution.py:249
  797.0 6.8 all-to-all-start.3
  808.2 5.1 convert_element_type.382
  814.8 11.0 %collective-permute-done.75 = bf16[128,4736]{1,0:T(8,128)(2,1)} collective-permute-done((bf16[128,4736]{1,0:T(8,128)(2,1)S(1)}, bf16[128,4736]{1,0:T(8,128)(2,1)}, u32[]{:S(2)}, u32[]{:S(2)}) %collective-permute-start.75) | collective-permute-done | bytes 1212448 | tf_op jit(solution)/shard_map/ppermute | solution.py:185
  825.8 19.3 %all-to-all-done.3 = bf16[16,16,2048]{2,1,0:T(8,128)(2,1)} async-done(((bf16[16,16,2048]{2,1,0:T(8,128)(2,1)}), bf16[16,16,2048]{2,1,0:T(8,128)(2,1)}, u32[]{:S(2)}, u32[]{:S(2)}) %all-to-all-start.3) | async-done | bytes 1048608 | tf_op jit(solution)/shard_map/all_to_all | solution.py:249
  845.1 26.4 %collective-permute-done.77 = bf16[128,4736]{1,0:T(8,128)(2,1)} collective-permute-done((bf16[128,4736]{1,0:T(8,128)(2,1)S(1)}, bf16[128,4736]{1,0:T(8,128)(2,1)}, u32[]{:S(2)}, u32[]{:S(2)}) %collective-permute-start.77) | collective-permute-done | bytes 1212448 | tf_op jit(solution)/shard_map/ppermute | solution.py:185
  (406 shorter events, 208.9 us)
Async XLA Ops:
  7.2 103.5 %all-gather.5.cloned.1.call-start = ((), (), s32[]{:S(2)}) async-start(), calls=%async_computation.6 | async-start | bytes 9437184 | tf_op jit(solution)/shard_map/all_gather | solution.py:754
  7.9 169.3 %all-gather.7.cloned.1.call-start = ((), (), s32[]{:S(2)}) async-start(), calls=%async_computation.7 | async-start | bytes 9437184 | tf_op jit(solution)/shard_map/all_gather | solution.py:755
  13.4 22.7 %collective-permute-start = (bf16[256,640]{1,0:T(8,128)(2,1)}, bf16[256,640]{1,0:T(8,128)(2,1)}, u32[]{:S(2)}, u32[]{:S(2)}) collective-permute-start(bf16[256,640]{1,0:T(8,128)(2,1)} %get-tuple-element.341), channel_id=1, source_target_pairs={{0,1},{1,0},{2,3},{3,2},{16,17},{17,16},{18,19},{19,18},{4,5},{5,4... | collective-permute-start | bytes 983048 | tf_op jit(solution)/shard_map/ppermute | solution.py:55
  13.8 19.6 %collective-permute-start.1 = (bf16[256,640]{1,0:T(8,128)(2,1)}, bf16[256,640]{1,0:T(8,128)(2,1)S(1)}, u32[]{:S(2)}, u32[]{:S(2)}) collective-permute-start(bf16[256,640]{1,0:T(8,128)(2,1)} %get-tuple-element.341), channel_id=1, source_target_pairs={{0,2},{1,3},{2,0},{3,1},{16,18},{17,19},{18,16},{19,17},{4,6},{5,7... | collective-permute-start | bytes 983048 | tf_op jit(solution)/shard_map/ppermute | solution.py:55
  16.3 17.5 %collective-permute-start.3 = (bf16[256,640]{1,0:T(8,128)(2,1)}, bf16[256,640]{1,0:T(8,128)(2,1)S(1)}, u32[]{:S(2)}, u32[]{:S(2)}) collective-permute-start(bf16[256,640]{1,0:T(8,128)(2,1)} %get-tuple-element.341), channel_id=1, source_target_pairs={{0,16},{1,17},{2,18},{3,19},{16,0},{17,1},{18,2},{19,3},{4,20},{5,... | collective-permute-start | bytes 983048 | tf_op jit(solution)/shard_map/ppermute | solution.py:55
  20.5 33.0 %all-to-all-start = ((bf16[16,16,2176]{2,1,0:T(8,128)(2,1)}), bf16[16,16,2176]{2,1,0:T(8,128)(2,1)}, u32[]{:S(2)}, u32[]{:S(2)}) async-start(bf16[16,16,2176]{2,1,0:T(8,128)(2,1)} %bitcast.96), calls=%async_computation | async-start | bytes 2228224 | tf_op jit(solution)/shard_map/all_to_all | solution.py:249
  33.4 17.9 %collective-permute-start.2 = (bf16[256,640]{1,0:T(8,128)(2,1)S(1)}, bf16[256,640]{1,0:T(8,128)(2,1)S(1)}, u32[]{:S(2)}, u32[]{:S(2)}) collective-permute-start(bf16[256,640]{1,0:T(8,128)(2,1)S(1)} %collective-permute-done.1), channel_id=1, source_target_pairs={{0,1},{1,0},{2,3},{3,2},{16,17},{17,16},{18,19},{19,18},{4,5},{5,4... | collective-permute-start | bytes 983048 | tf_op jit(solution)/shard_map/ppermute | solution.py:55
  33.8 17.0 %collective-permute-start.5 = (bf16[128,640]{1,0:T(8,128)(2,1)S(1)}, bf16[128,640]{1,0:T(8,128)(2,1)S(1)}, u32[]{:S(2)}, u32[]{:S(2)}) collective-permute-start(bf16[128,640]{1,0:T(8,128)(2,1)S(1)} %slice.215), channel_id=1, source_target_pairs={{0,2},{1,3},{2,0},{3,1},{16,18},{17,19},{18,16},{19,17},{4,6},{5,7... | collective-permute-start | bytes 491528 | tf_op jit(solution)/shard_map/ppermute | solution.py:55
  35.6 15.2 %collective-permute-start.7 = (bf16[128,640]{1,0:T(8,128)(2,1)S(1)}, bf16[128,640]{1,0:T(8,128)(2,1)S(1)}, u32[]{:S(2)}, u32[]{:S(2)}) collective-permute-start(bf16[128,640]{1,0:T(8,128)(2,1)S(1)} %slice.216), channel_id=1, source_target_pairs={{0,16},{1,17},{2,18},{3,19},{16,0},{17,1},{18,2},{19,3},{4,20},{5,... | collective-permute-start | bytes 491528 | tf_op jit(solution)/shard_map/ppermute | solution.py:55
  36.1 15.4 %collective-permute-start.4 = (bf16[256,640]{1,0:T(8,128)(2,1)S(1)}, bf16[256,640]{1,0:T(8,128)(2,1)S(1)}, u32[]{:S(2)}, u32[]{:S(2)}) collective-permute-start(bf16[256,640]{1,0:T(8,128)(2,1)S(1)} %collective-permute-done.3), channel_id=1, source_target_pairs={{0,1},{1,0},{2,3},{3,2},{16,17},{17,16},{18,19},{19,18},{4,5},{5,4... | collective-permute-start | bytes 983048 | tf_op jit(solution)/shard_map/ppermute | solution.py:55
  63.8 24.5 %collective-permute-start.14 = (bf16[256,512]{1,0:T(8,128)(2,1)S(1)}, bf16[256,512]{1,0:T(8,128)(2,1)S(1)}, u32[]{:S(2)}, u32[]{:S(2)}) collective-permute-start(bf16[256,512]{1,0:T(8,128)(2,1)S(1)} %project.3), channel_id=1, source_target_pairs={{0,8},{4,12},{8,0},{12,4},{1,9},{5,13},{9,1},{13,5},{2,10},{6,14},... | collective-permute-start | bytes 786440 | tf_op jit(solution)/shard_map/ppermute | solution.py:55
  67.2 22.1 %collective-permute-start.17 = (bf16[256,512]{1,0:T(8,128)(2,1)S(1)}, bf16[256,512]{1,0:T(8,128)(2,1)S(1)}, u32[]{:S(2)}, u32[]{:S(2)}) collective-permute-start(bf16[256,512]{1,0:T(8,128)(2,1)S(1)} %project.3), channel_id=1, source_target_pairs={{0,12},{4,8},{8,4},{12,0},{1,13},{5,9},{9,5},{13,1},{2,14},{6,10},... | collective-permute-start | bytes 786440 | tf_op jit(solution)/shard_map/ppermute | solution.py:55
  77.0 18.0 %collective-permute-start.12 = (bf16[256,512]{1,0:T(8,128)(2,1)S(1)}, bf16[256,512]{1,0:T(8,128)(2,1)S(1)}, u32[]{:S(2)}, u32[]{:S(2)}) collective-permute-start(bf16[256,512]{1,0:T(8,128)(2,1)S(1)} %collective-permute-done.11), channel_id=1, source_target_pairs={{0,2},{1,3},{2,0},{3,1},{4,6},{5,7},{6,4},{7,5},{8,10},{9,11},{10,... | collective-permute-start | bytes 786440 | tf_op jit(solution)/shard_map/ppermute | solution.py:55
  88.2 18.5 %collective-permute-start.10 = (bf16[512,512]{1,0:T(8,128)(2,1)S(1)}, bf16[512,512]{1,0:T(8,128)(2,1)S(1)}, u32[]{:S(2)}, u32[]{:S(2)}) collective-permute-start(bf16[512,512]{1,0:T(8,128)(2,1)S(1)} %pad_maximum_fusion.12), channel_id=1, source_target_pairs={{0,1},{1,0},{2,3},{3,2},{4,5},{5,4},{6,7},{7,6},{8,9},{9,8},{10,11... | collective-permute-start | bytes 1572872 | tf_op jit(solution)/shard_map/ppermute | solution.py:55
  89.3 17.3 %collective-permute-start.18 = (bf16[256,512]{1,0:T(8,128)(2,1)S(1)}, bf16[256,512]{1,0:T(8,128)(2,1)S(1)}, u32[]{:S(2)}, u32[]{:S(2)}) collective-permute-start(bf16[256,512]{1,0:T(8,128)(2,1)S(1)} %collective-permute-done.17), channel_id=1, source_target_pairs={{0,2},{1,3},{2,0},{3,1},{4,6},{5,7},{6,4},{7,5},{8,10},{9,11},{10,... | collective-permute-start | bytes 786440 | tf_op jit(solution)/shard_map/ppermute | solution.py:55
  118.8 51.9 %collective-permute-start.20 = (bf16[704,2048]{1,0:T(8,128)(2,1)}, bf16[704,2048]{1,0:T(8,128)(2,1)}, u32[]{:S(2)}, u32[]{:S(2)}) collective-permute-start(bf16[704,2048]{1,0:T(8,128)(2,1)} %param.21), channel_id=1, source_target_pairs={{0,1},{1,0},{2,3},{3,2},{16,17},{17,16},{18,19},{19,18},{4,5},{5,4... | collective-permute-start | bytes 8650760 | tf_op jit(solution)/shard_map/ppermute | solution.py:55
  119.0 51.7 %collective-permute-start.21 = (bf16[256,2816]{1,0:T(8,128)(2,1)}, bf16[256,2816]{1,0:T(8,128)(2,1)}, u32[]{:S(2)}, u32[]{:S(2)}) collective-permute-start(bf16[256,2816]{1,0:T(8,128)(2,1)} %pad_maximum_fusion.5), channel_id=1, source_target_pairs={{0,1},{1,0},{2,3},{3,2},{16,17},{17,16},{18,19},{19,18},{4,5},{5,4... | collective-permute-start | bytes 4325384 | tf_op jit(solution)/shard_map/ppermute | solution.py:55
  119.4 66.4 %all-to-all-start.1 = ((bf16[16,16,2048]{2,1,0:T(8,128)(2,1)}), bf16[16,16,2048]{2,1,0:T(8,128)(2,1)}, u32[]{:S(2)}, u32[]{:S(2)}) async-start(bf16[16,16,2048]{2,1,0:T(8,128)(2,1)} %bitcast.101), calls=%async_computation.1 | async-start | bytes 2097152 | tf_op jit(solution)/shard_map/all_to_all | solution.py:249
  124.2 383.3 %reduce-scatter.3.cloned.1.call-start = ((), (), s32[]{:S(2)}) async-start(), calls=%async_computation.8 | async-start | bytes 3604480 | tf_op jit(solution)/shard_map/reduce_scatter | solution.py:871
  124.7 73.6 %collective-permute-start.24 = (bf16[256,2816]{1,0:T(8,128)(2,1)}, bf16[256,2816]{1,0:T(8,128)(2,1)}, u32[]{:S(2)}, u32[]{:S(2)}) collective-permute-start(bf16[256,2816]{1,0:T(8,128)(2,1)} %pad_maximum_fusion.6), channel_id=1, source_target_pairs={{0,2},{1,3},{2,0},{3,1},{16,18},{17,19},{18,16},{19,17},{4,6},{5,7... | collective-permute-start | bytes 4325384 | tf_op jit(solution)/shard_map/ppermute | solution.py:55
  126.6 71.7 %collective-permute-start.25 = (bf16[256,2816]{1,0:T(8,128)(2,1)}, bf16[256,2816]{1,0:T(8,128)(2,1)}, u32[]{:S(2)}, u32[]{:S(2)}) collective-permute-start(bf16[256,2816]{1,0:T(8,128)(2,1)} %pad_maximum_fusion.7), channel_id=1, source_target_pairs={{0,16},{1,17},{2,18},{3,19},{16,0},{17,1},{18,2},{19,3},{4,20},{5,... | collective-permute-start | bytes 4325384 | tf_op jit(solution)/shard_map/ppermute | solution.py:55
  128.1 93.3 %collective-permute-start.26 = (bf16[256,2816]{1,0:T(8,128)(2,1)}, bf16[256,2816]{1,0:T(8,128)(2,1)}, u32[]{:S(2)}, u32[]{:S(2)}) collective-permute-start(bf16[256,2816]{1,0:T(8,128)(2,1)} %pad_maximum_fusion.8), channel_id=1, source_target_pairs={{0,18},{1,19},{2,16},{3,17},{16,2},{17,3},{18,0},{19,1},{4,22},{5,... | collective-permute-start | bytes 4325384 | tf_op jit(solution)/shard_map/ppermute | solution.py:55
  185.8 57.0 %collective-permute-start.22 = (bf16[256,2048]{1,0:T(8,128)(2,1)}, bf16[256,2048]{1,0:T(8,128)(2,1)}, u32[]{:S(2)}, u32[]{:S(2)}) collective-permute-start(bf16[256,2048]{1,0:T(8,128)(2,1)} %multiply_convert_fusion), channel_id=1, source_target_pairs={{0,2},{1,3},{2,0},{3,1},{16,18},{17,19},{18,16},{19,17},{4,6},{5,7... | collective-permute-start | bytes 3145736 | tf_op jit(solution)/shard_map/ppermute | solution.py:55
  186.0 56.8 %collective-permute-start.23 = (bf16[256,2048]{1,0:T(8,128)(2,1)}, bf16[256,2048]{1,0:T(8,128)(2,1)}, u32[]{:S(2)}, u32[]{:S(2)}) collective-permute-start(bf16[256,2048]{1,0:T(8,128)(2,1)} %multiply_convert_fusion), channel_id=1, source_target_pairs={{0,16},{1,17},{2,18},{3,19},{16,0},{17,1},{18,2},{19,3},{4,20},{5,... | collective-permute-start | bytes 3145736 | tf_op jit(solution)/shard_map/ppermute | solution.py:55
  244.1 38.1 %collective-permute-start.27 = (bf16[256,2048]{1,0:T(8,128)(2,1)}, bf16[256,2048]{1,0:T(8,128)(2,1)S(1)}, u32[]{:S(2)}, u32[]{:S(2)}) collective-permute-start(bf16[256,2048]{1,0:T(8,128)(2,1)} %bitcast.9), channel_id=1, source_target_pairs={{0,2},{1,3},{2,0},{3,1},{16,18},{17,19},{18,16},{19,17},{4,6},{5,7... | collective-permute-start | bytes 3145736 | tf_op jit(solution)/shard_map/ppermute | solution.py:55
  245.5 36.7 %collective-permute-start.28 = (bf16[256,2048]{1,0:T(8,128)(2,1)}, bf16[256,2048]{1,0:T(8,128)(2,1)S(1)}, u32[]{:S(2)}, u32[]{:S(2)}) collective-permute-start(bf16[256,2048]{1,0:T(8,128)(2,1)} %bitcast.9), channel_id=1, source_target_pairs={{0,16},{1,17},{2,18},{3,19},{16,0},{17,1},{18,2},{19,3},{4,20},{5,... | collective-permute-start | bytes 3145736 | tf_op jit(solution)/shard_map/ppermute | solution.py:55
  247.3 33.9 %collective-permute-start.29 = (bf16[128,2048]{1,0:T(8,128)(2,1)S(1)}, bf16[128,2048]{1,0:T(8,128)(2,1)S(1)}, u32[]{:S(2)}, u32[]{:S(2)}) collective-permute-start(bf16[128,2048]{1,0:T(8,128)(2,1)S(1)} %slice.174), channel_id=1, source_target_pairs={{0,2},{1,3},{2,0},{3,1},{16,18},{17,19},{18,16},{19,17},{4,6},{5,7... | collective-permute-start | bytes 1572872 | tf_op jit(solution)/shard_map/ppermute | solution.py:55
  262.2 20.0 %collective-permute-start.30 = (bf16[128,2048]{1,0:T(8,128)(2,1)S(1)}, bf16[128,2048]{1,0:T(8,128)(2,1)S(1)}, u32[]{:S(2)}, u32[]{:S(2)}) collective-permute-start(bf16[128,2048]{1,0:T(8,128)(2,1)S(1)} %slice.175), channel_id=1, source_target_pairs={{0,16},{1,17},{2,18},{3,19},{16,0},{17,1},{18,2},{19,3},{4,20},{5,... | collective-permute-start | bytes 1572872 | tf_op jit(solution)/shard_map/ppermute | solution.py:55
  282.3 24.9 %collective-permute-start.34 = (bf16[128,2048]{1,0:T(8,128)(2,1)S(1)}, bf16[128,2048]{1,0:T(8,128)(2,1)S(1)}, u32[]{:S(2)}, u32[]{:S(2)}) collective-permute-start(bf16[128,2048]{1,0:T(8,128)(2,1)S(1)} %slice.176), channel_id=1, source_target_pairs={{0,2},{1,3},{2,0},{3,1},{16,18},{17,19},{18,16},{19,17},{4,6},{5,7... | collective-permute-start | bytes 1572872 | tf_op jit(solution)/shard_map/ppermute | solution.py:55
  283.9 23.3 %collective-permute-start.35 = (bf16[128,2048]{1,0:T(8,128)(2,1)}, bf16[128,2048]{1,0:T(8,128)(2,1)S(1)}, u32[]{:S(2)}, u32[]{:S(2)}) collective-permute-start(bf16[128,2048]{1,0:T(8,128)(2,1)} %slice.177), channel_id=1, source_target_pairs={{0,16},{1,17},{2,18},{3,19},{16,0},{17,1},{18,2},{19,3},{4,20},{5,... | collective-permute-start | bytes 1572872 | tf_op jit(solution)/shard_map/ppermute | solution.py:55
  361.7 185.3 %reduce-scatter.5.cloned.1.call-start = ((), (), s32[]{:S(2)}) async-start(), calls=%async_computation.9 | async-start | bytes 7208960 | tf_op jit(solution)/shard_map/reduce_scatter | solution.py:875
  381.9 25.5 %collective-permute-start.38 = (bf16[256,2048]{1,0:T(8,128)(2,1)}, bf16[256,2048]{1,0:T(8,128)(2,1)}, u32[]{:S(2)}, u32[]{:S(2)}) collective-permute-start(bf16[256,2048]{1,0:T(8,128)(2,1)} %pad_maximum_fusion.10), channel_id=1, source_target_pairs={{0,2},{1,3},{2,0},{3,1},{16,18},{17,19},{18,16},{19,17},{4,6},{5,7... | collective-permute-start | bytes 3145736 | tf_op jit(solution)/shard_map/ppermute | solution.py:55
  384.2 25.2 %collective-permute-start.39 = (bf16[256,2048]{1,0:T(8,128)(2,1)}, bf16[256,2048]{1,0:T(8,128)(2,1)}, u32[]{:S(2)}, u32[]{:S(2)}) collective-permute-start(bf16[256,2048]{1,0:T(8,128)(2,1)} %pad_maximum_fusion.11), channel_id=1, source_target_pairs={{0,16},{1,17},{2,18},{3,19},{16,0},{17,1},{18,2},{19,3},{4,20},{5,... | collective-permute-start | bytes 3145736 | tf_op jit(solution)/shard_map/ppermute | solution.py:55
  409.4 246.7 %all-gather.9.cloned.1.call-start = ((), (), s32[]{:S(2)}) async-start(), calls=%async_computation.10 | async-start | bytes 3604480 | tf_op jit(solution)/shard_map/all_gather | solution.py:898
  428.4 76.8 %collective-permute-start.45 = (bf16[256,3072]{1,0:T(8,128)(2,1)S(1)}, bf16[256,3072]{1,0:T(8,128)(2,1)S(1)}, u32[]{:S(2)}, u32[]{:S(2)}) collective-permute-start(bf16[256,3072]{1,0:T(8,128)(2,1)S(1)} %get-tuple-element.182), channel_id=1, source_target_pairs={{0,2},{1,3},{2,0},{3,1},{16,18},{17,19},{18,16},{19,17},{4,6},{5,7... | collective-permute-start | bytes 4718600 | tf_op jit(solution)/shard_map/ppermute | solution.py:55
  429.3 75.9 %collective-permute-start.46 = (bf16[256,3072]{1,0:T(8,128)(2,1)S(1)}, bf16[256,3072]{1,0:T(8,128)(2,1)S(1)}, u32[]{:S(2)}, u32[]{:S(2)}) collective-permute-start(bf16[256,3072]{1,0:T(8,128)(2,1)S(1)} %get-tuple-element.183), channel_id=1, source_target_pairs={{0,16},{1,17},{2,18},{3,19},{16,0},{17,1},{18,2},{19,3},{4,20},{5,... | collective-permute-start | bytes 4718600 | tf_op jit(solution)/shard_map/ppermute | solution.py:55
  430.7 76.8 %collective-permute-start.47 = (bf16[256,3072]{1,0:T(8,128)(2,1)S(1)}, bf16[256,3072]{1,0:T(8,128)(2,1)}, u32[]{:S(2)}, u32[]{:S(2)}) collective-permute-start(bf16[256,3072]{1,0:T(8,128)(2,1)S(1)} %get-tuple-element.184), channel_id=1, source_target_pairs={{0,18},{1,19},{2,16},{3,17},{16,2},{17,3},{18,0},{19,1},{4,22},{5,... | collective-permute-start | bytes 4718600 | tf_op jit(solution)/shard_map/ppermute | solution.py:55
  512.8 200.7 %all-gather.11.cloned.1.call-start = ((), (), s32[]{:S(2)}) async-start(), calls=%async_computation.11 | async-start | bytes 7208960 | tf_op jit(solution)/shard_map/all_gather | solution.py:917
  521.4 25.5 %collective-permute-start.49 = (bf16[4,256,512]{2,1,0:T(8,128)(2,1)S(1)}, bf16[4,256,512]{2,1,0:T(8,128)(2,1)S(1)}, u32[]{:S(2)}, u32[]{:S(2)}) collective-permute-start(bf16[4,256,512]{2,1,0:T(8,128)(2,1)S(1)} %slice_bitcast_fusion.1), channel_id=1, source_target_pairs={{0,2},{1,3},{2,0},{3,1},{4,6},{5,7},{6,4},{7,5},{8,10},{9,11},{10,... | collective-permute-start | bytes 3145736 | tf_op jit(solution)/shard_map/ppermute | solution.py:55
  547.3 25.8 %collective-permute-start.50 = (bf16[256,512]{1,0:T(8,128)(2,1)S(1)}, bf16[256,512]{1,0:T(8,128)(2,1)S(1)}, u32[]{:S(2)}, u32[]{:S(2)}) collective-permute-start(bf16[256,512]{1,0:T(8,128)(2,1)S(1)} %get-tuple-element.322), channel_id=1, source_target_pairs={{0,4},{4,0},{8,12},{12,8},{1,5},{5,1},{9,13},{13,9},{2,6},{6,2},{1... | collective-permute-start | bytes 786440 | tf_op jit(solution)/shard_map/ppermute | solution.py:55
  548.8 32.3 %collective-permute-start.51 = (bf16[256,512]{1,0:T(8,128)(2,1)S(1)}, bf16[256,512]{1,0:T(8,128)(2,1)S(1)}, u32[]{:S(2)}, u32[]{:S(2)}) collective-permute-start(bf16[256,512]{1,0:T(8,128)(2,1)S(1)} %get-tuple-element.321), channel_id=1, source_target_pairs={{0,8},{4,12},{8,0},{12,4},{1,9},{5,13},{9,1},{13,5},{2,10},{6,14},... | collective-permute-start | bytes 786440 | tf_op jit(solution)/shard_map/ppermute | solution.py:55
  551.3 34.8 %collective-permute-start.52 = (bf16[256,512]{1,0:T(8,128)(2,1)S(1)}, bf16[256,512]{1,0:T(8,128)(2,1)S(1)}, u32[]{:S(2)}, u32[]{:S(2)}) collective-permute-start(bf16[256,512]{1,0:T(8,128)(2,1)S(1)} %get-tuple-element.320), channel_id=1, source_target_pairs={{0,12},{4,8},{8,4},{12,0},{1,13},{5,9},{9,5},{13,1},{2,14},{6,10},... | collective-permute-start | bytes 786440 | tf_op jit(solution)/shard_map/ppermute | solution.py:55
  551.9 34.2 %collective-permute-start.53 = (bf16[64,2816]{1,0:T(8,128)(2,1)S(1)}, bf16[64,2816]{1,0:T(8,128)(2,1)S(1)}, u32[]{:S(2)}, u32[]{:S(2)}) collective-permute-start(bf16[64,2816]{1,0:T(8,128)(2,1)S(1)} %get-tuple-element.318), channel_id=1, source_target_pairs={{0,2},{1,3},{2,0},{3,1},{16,18},{17,19},{18,16},{19,17},{4,6},{5,7... | collective-permute-start | bytes 1081352 | tf_op jit(solution)/shard_map/ppermute | solution.py:55
  553.0 20.9 %collective-permute-start.56 = (bf16[256,2048]{1,0:T(8,128)(2,1)S(1)}, bf16[256,2048]{1,0:T(8,128)(2,1)S(1)}, u32[]{:S(2)}, u32[]{:S(2)}) collective-permute-start(bf16[256,2048]{1,0:T(8,128)(2,1)S(1)} %constant_dynamic-slice_fusion.6), channel_id=1, source_target_pairs={{0,1},{1,0},{2,3},{3,2},{16,17},{17,16},{18,19},{19,18},{4,5},{5,4... | collective-permute-start | bytes 3145736 | tf_op jit(solution)/shard_map/ppermute | solution.py:55
  573.1 16.9 %collective-permute-start.54 = (bf16[64,2816]{1,0:T(8,128)(2,1)S(1)}, bf16[64,2816]{1,0:T(8,128)(2,1)S(1)}, u32[]{:S(2)}, u32[]{:S(2)}) collective-permute-start(bf16[64,2816]{1,0:T(8,128)(2,1)S(1)} %get-tuple-element.317), channel_id=1, source_target_pairs={{0,16},{1,17},{2,18},{3,19},{16,0},{17,1},{18,2},{19,3},{4,20},{5,... | collective-permute-start | bytes 1081352 | tf_op jit(solution)/shard_map/ppermute | solution.py:55
  573.9 16.1 %collective-permute-start.55 = (bf16[64,2816]{1,0:T(8,128)(2,1)S(1)}, bf16[64,2816]{1,0:T(8,128)(2,1)S(1)}, u32[]{:S(2)}, u32[]{:S(2)}) collective-permute-start(bf16[64,2816]{1,0:T(8,128)(2,1)S(1)} %get-tuple-element.316), channel_id=1, source_target_pairs={{0,18},{1,19},{2,16},{3,17},{16,2},{17,3},{18,0},{19,1},{4,22},{5,... | collective-permute-start | bytes 1081352 | tf_op jit(solution)/shard_map/ppermute | solution.py:55
  591.4 26.5 %collective-permute-start.57 = (bf16[256,2048]{1,0:T(8,128)(2,1)}, bf16[256,2048]{1,0:T(8,128)(2,1)}, u32[]{:S(2)}, u32[]{:S(2)}) collective-permute-start(bf16[256,2048]{1,0:T(8,128)(2,1)} %turn_back.2), channel_id=1, source_target_pairs={{0,2},{1,3},{2,0},{3,1},{16,18},{17,19},{18,16},{19,17},{4,6},{5,7... | collective-permute-start | bytes 3145736 | tf_op jit(solution)/shard_map/ppermute | solution.py:55
  592.5 46.1 %collective-permute-start.58 = (bf16[256,2048]{1,0:T(8,128)(2,1)}, bf16[256,2048]{1,0:T(8,128)(2,1)}, u32[]{:S(2)}, u32[]{:S(2)}) collective-permute-start(bf16[256,2048]{1,0:T(8,128)(2,1)} %turn_back.2), channel_id=1, source_target_pairs={{0,16},{1,17},{2,18},{3,19},{16,0},{17,1},{18,2},{19,3},{4,20},{5,... | collective-permute-start | bytes 3145736 | tf_op jit(solution)/shard_map/ppermute | solution.py:55
  593.9 44.7 %collective-permute-start.59 = (bf16[256,2048]{1,0:T(8,128)(2,1)}, bf16[256,2048]{1,0:T(8,128)(2,1)}, u32[]{:S(2)}, u32[]{:S(2)}) collective-permute-start(bf16[256,2048]{1,0:T(8,128)(2,1)} %turn_back.2), channel_id=1, source_target_pairs={{0,18},{1,19},{2,16},{3,17},{16,2},{17,3},{18,0},{19,1},{4,22},{5,... | collective-permute-start | bytes 3145736 | tf_op jit(solution)/shard_map/ppermute | solution.py:55
  646.8 20.2 %collective-permute-start.61 = (bf16[256,512]{1,0:T(8,128)(2,1)}, bf16[256,512]{1,0:T(8,128)(2,1)}, u32[]{:S(2)}, u32[]{:S(2)}) collective-permute-start(bf16[256,512]{1,0:T(8,128)(2,1)} %turn_back.3), channel_id=1, source_target_pairs={{0,2},{1,3},{2,0},{3,1},{16,18},{17,19},{18,16},{19,17},{4,6},{5,7... | collective-permute-start | bytes 786440 | tf_op jit(solution)/shard_map/ppermute | solution.py:55
  647.4 19.6 %collective-permute-start.62 = (bf16[256,512]{1,0:T(8,128)(2,1)}, bf16[256,512]{1,0:T(8,128)(2,1)}, u32[]{:S(2)}, u32[]{:S(2)}) collective-permute-start(bf16[256,512]{1,0:T(8,128)(2,1)} %turn_back.3), channel_id=1, source_target_pairs={{0,16},{1,17},{2,18},{3,19},{16,0},{17,1},{18,2},{19,3},{4,20},{5,... | collective-permute-start | bytes 786440 | tf_op jit(solution)/shard_map/ppermute | solution.py:55
  649.1 17.9 %collective-permute-start.63 = (bf16[256,512]{1,0:T(8,128)(2,1)}, bf16[256,512]{1,0:T(8,128)(2,1)}, u32[]{:S(2)}, u32[]{:S(2)}) collective-permute-start(bf16[256,512]{1,0:T(8,128)(2,1)} %turn_back.3), channel_id=1, source_target_pairs={{0,18},{1,19},{2,16},{3,17},{16,2},{17,3},{18,0},{19,1},{4,22},{5,... | collective-permute-start | bytes 786440 | tf_op jit(solution)/shard_map/ppermute | solution.py:55
  651.6 15.3 %collective-permute-start.65 = (bf16[2,512]{0,1:T(8,128)(2,1)}, bf16[2,512]{0,1:T(8,128)(2,1)S(1)}, u32[]{:S(2)}, u32[]{:S(2)}) collective-permute-start(bf16[2,512]{0,1:T(8,128)(2,1)} %get-tuple-element.338), channel_id=1, source_target_pairs={{0,16},{1,17},{2,18},{3,19},{16,0},{17,1},{18,2},{19,3},{4,20},{5,... | collective-permute-start | bytes 6152 | tf_op jit(solution)/shard_map/ppermute | solution.py:55
  713.6 28.0 %collective-permute-start.69 = (bf16[128,4736]{1,0:T(8,128)(2,1)S(1)}, bf16[128,4736]{1,0:T(8,128)(2,1)S(1)}, u32[]{:S(2)}, u32[]{:S(2)}) collective-permute-start(bf16[128,4736]{1,0:T(8,128)(2,1)S(1)} %slice.200), channel_id=1, source_target_pairs={{0,4},{12,8},{1,5},{13,9},{2,6},{14,10},{3,7},{15,11},{16,20},{28,... | collective-permute-start | bytes 3637256 | tf_op jit(solution)/shard_map/ppermute | solution.py:177
  717.5 35.2 %collective-permute-start.74 = (bf16[256,2048]{1,0:T(8,128)(2,1)S(1)}, bf16[256,2048]{1,0:T(8,128)(2,1)S(1)}, u32[]{:S(2)}, u32[]{:S(2)}) collective-permute-start(bf16[256,2048]{1,0:T(8,128)(2,1)S(1)} %get-tuple-element.298), channel_id=1, source_target_pairs={{0,18},{1,19},{2,16},{3,17},{16,2},{17,3},{18,0},{19,1},{4,22},{5,... | collective-permute-start | bytes 3145736 | tf_op jit(solution)/shard_map/ppermute | solution.py:55
  719.9 46.1 %collective-permute-start.73 = (bf16[256,2048]{1,0:T(8,128)(2,1)S(1)}, bf16[256,2048]{1,0:T(8,128)(2,1)S(1)}, u32[]{:S(2)}, u32[]{:S(2)}) collective-permute-start(bf16[256,2048]{1,0:T(8,128)(2,1)S(1)} %get-tuple-element.299), channel_id=1, source_target_pairs={{0,16},{1,17},{2,18},{3,19},{16,0},{17,1},{18,2},{19,3},{4,20},{5,... | collective-permute-start | bytes 3145736 | tf_op jit(solution)/shard_map/ppermute | solution.py:55
  720.5 45.6 %collective-permute-start.72 = (bf16[256,2048]{1,0:T(8,128)(2,1)S(1)}, bf16[256,2048]{1,0:T(8,128)(2,1)S(1)}, u32[]{:S(2)}, u32[]{:S(2)}) collective-permute-start(bf16[256,2048]{1,0:T(8,128)(2,1)S(1)} %get-tuple-element.297), channel_id=1, source_target_pairs={{0,2},{1,3},{2,0},{3,1},{16,18},{17,19},{18,16},{19,17},{4,6},{5,7... | collective-permute-start | bytes 3145736 | tf_op jit(solution)/shard_map/ppermute | solution.py:55
  742.8 30.8 %collective-permute-start.70 = (bf16[128,4736]{1,0:T(8,128)(2,1)}, bf16[128,4736]{1,0:T(8,128)(2,1)}, u32[]{:S(2)}, u32[]{:S(2)}) collective-permute-start(bf16[128,4736]{1,0:T(8,128)(2,1)} %add_convert_fusion.8), channel_id=1, source_target_pairs={{4,8},{8,4},{5,9},{9,5},{6,10},{10,6},{7,11},{11,7},{20,24},{24,20... | collective-permute-start | bytes 3637256 | tf_op jit(solution)/shard_map/ppermute | solution.py:181
  745.7 32.8 %collective-permute-start.71 = (bf16[128,4736]{1,0:T(8,128)(2,1)}, bf16[128,4736]{1,0:T(8,128)(2,1)}, u32[]{:S(2)}, u32[]{:S(2)}) collective-permute-start(bf16[128,4736]{1,0:T(8,128)(2,1)} %slice.201), channel_id=1, source_target_pairs={{0,4},{12,8},{1,5},{13,9},{2,6},{14,10},{3,7},{15,11},{16,20},{28,... | collective-permute-start | bytes 3637256 | tf_op jit(solution)/shard_map/ppermute | solution.py:177
  769.1 27.9 %all-to-all-start.2 = ((bf16[16,16,2048]{2,1,0:T(8,128)(2,1)}), bf16[16,16,2048]{2,1,0:T(8,128)(2,1)S(1)}, u32[]{:S(2)}, u32[]{:S(2)}) async-start(bf16[16,16,2048]{2,1,0:T(8,128)(2,1)} %bitcast.98), calls=%async_computation.4 | async-start | bytes 2097152 | tf_op jit(solution)/shard_map/all_to_all | solution.py:249
  781.0 22.9 %collective-permute-start.76 = (bf16[128,4736]{1,0:T(8,128)(2,1)}, bf16[128,4736]{1,0:T(8,128)(2,1)S(1)}, u32[]{:S(2)}, u32[]{:S(2)}) collective-permute-start(bf16[128,4736]{1,0:T(8,128)(2,1)} %add_convert_fusion.6), channel_id=1, source_target_pairs={{4,8},{8,4},{5,9},{9,5},{6,10},{10,6},{7,11},{11,7},{20,24},{24,20... | collective-permute-start | bytes 3637256 | tf_op jit(solution)/shard_map/ppermute | solution.py:181
  783.7 42.1 %collective-permute-start.75 = (bf16[128,4736]{1,0:T(8,128)(2,1)S(1)}, bf16[128,4736]{1,0:T(8,128)(2,1)}, u32[]{:S(2)}, u32[]{:S(2)}) collective-permute-start(bf16[128,4736]{1,0:T(8,128)(2,1)S(1)} %add_convert_fusion.7), channel_id=1, source_target_pairs={{4,0},{8,12},{5,1},{9,13},{6,2},{10,14},{7,3},{11,15},{20,16},{24,... | collective-permute-start | bytes 3637256 | tf_op jit(solution)/shard_map/ppermute | solution.py:185
  797.0 48.1 %all-to-all-start.3 = ((bf16[16,16,2048]{2,1,0:T(8,128)(2,1)}), bf16[16,16,2048]{2,1,0:T(8,128)(2,1)}, u32[]{:S(2)}, u32[]{:S(2)}) async-start(bf16[16,16,2048]{2,1,0:T(8,128)(2,1)} %bitcast.36), calls=%async_computation.5 | async-start | bytes 2097152 | tf_op jit(solution)/shard_map/all_to_all | solution.py:249
  806.8 64.7 %collective-permute-start.77 = (bf16[128,4736]{1,0:T(8,128)(2,1)S(1)}, bf16[128,4736]{1,0:T(8,128)(2,1)}, u32[]{:S(2)}, u32[]{:S(2)}) collective-permute-start(bf16[128,4736]{1,0:T(8,128)(2,1)S(1)} %add_convert_fusion.5), channel_id=1, source_target_pairs={{4,0},{8,12},{5,1},{9,13},{6,2},{10,14},{7,3},{11,15},{20,16},{24,... | collective-permute-start | bytes 3637256 | tf_op jit(solution)/shard_map/ppermute | solution.py:185
  (81 other events, 624.6 us)
Sparse Core Ops, SparseCore 0:
  9.9 82.5 all-gather.4
  94.4 82.8 all-gather.6
  361.8 56.1 reduce-scatter.2
  420.7 102.0 reduce-scatter.4
  524.3 81.8 all-gather.8
  608.1 105.3 all-gather.10

commit v4 on v3

--- a/solution.py
+++ b/solution.py
@@ -936,20 +936,23 @@
     gain_two = swap_rows(add_all(gain_parts).T.astype(bf16))
     last = jnp.concatenate(
         [
-            query_own,
             output_own,
             add(*swap_rows(kv_share)),
             jnp.pad(add(*gain_two), ((0, 0), (0, 126))),
         ],
         axis=1,
     )
-    last, input_gradient, both_sums, down_sum = tie(last, input_gradient, both_sums, down_sum)
-    lasts = [LineTree(last[half]) for half in halves(own_rows)[:1]]
+    last, query_own, input_gradient, both_sums, down_sum = tie(
+        last, query_own, input_gradient, both_sums, down_sum
+    )
+    lasts = [LineTree(last)]
     input_gradient = spread(input_gradient)
     gate_gradient, up_gradient = place_columns(both_sums, chip)
-    lasts[0].moving, gate_gradient, last = tie(lasts[0].moving, gate_gradient, last)
+    lasts[0].moving, gate_gradient, query_own = tie(
+        lasts[0].moving, gate_gradient, query_own
+    )
     lasts[0].across()
-    lasts.append(LineTree(last[halves(own_rows)[1]]))
+    lasts.append(LineTree(query_own))
     layer_output = (middle + add_all(out_parts)).astype(bf16)
     lasts[0].moving, lasts[1].moving, layer_output = tie(
         lasts[0].moving, lasts[1].moving, layer_output
@@ -965,10 +968,8 @@
         lasts[0].moving, lasts[1].moving, layer_output, down_gradient, input_gradient
     )
 
-    last = jnp.concatenate([part.result() for part in lasts])
-    query_gradient = last[:, :width]
-    output_gradient = last[:, width : 2 * width]
-    pairs = last[:, 2 * width :]
+    last, query_gradient = lasts[0].result(), lasts[1].result()
+    output_gradient, pairs = last[:, :width], last[:, width:]
     gain_gradients = pairs[:, 2 * kv_width : 2 * kv_width + 2].T
     pairs = pairs[:, : 2 * kv_width].reshape(own_rows, KV_HEADS, 2, HEAD_DIM)
     return (

time: 899 us -> 905 us (level)
    all_to_all x4, waiting for transfers between devices: 31.4 us -> 1.54 us  [spread(): return lax.all_to_all(shaped, GROUP, 0, 0, tiled=True).reshape(rows.shape)]
    ppermute x2, waiting for transfers between devices: 37.4 us -> 57.8 us  [outwards(): self.moving = lax.ppermute(self.share, 'seq', [(1, 0), (2, 3)])]
    ppermute x2, waiting for transfers between devices: 20.9 us -> 35.4 us  [__init__(): self.moving = lax.ppermute(share, 'seq', [(0, 1), (3, 2)])]
    unnamed x143 -> x147, local copies, waits for them, and re-layouts: 39.8 us -> 38.9 us
  transfers between devices with their start and end apart: 88 -> 88, of which waited for: 41 -> 40; matrix products, arithmetic and copies ran while one was open for 22% -> 22% of each run, Pallas kernels for 16% -> 16%
where the time goes in v4:
time: 905 us; the launch traced here: 895 us
  waiting for transfers between devices  367 us (41%)
  Pallas kernels  156 us (17%)
  starting transfers between devices  99.4 us (11%)
  local copies, waits for them, and re-layouts  92.2 us (10%)
  other arithmetic  83.9 us (9%)
  matrix products  81.2 us (9%)
  between operations  16.4 us (2%)
    ppermute x72, waiting for transfers between devices, swap(): return lax.ppermute(values, axes, [(i, i ^ mask) for i in range(count)])  221 us
    dot_general x11, matrix products, dot(): return lax.dot_general(left, right, dims, preferred_element_type=f32)  81.2 us
    pallas_call x1, Pallas kernels, attend_backward(): pl.pallas_call(partial(backward_body, groups=groups, heads=heads, rows=ro...  70.2 us
    ppermute x72, starting transfers between devices, swap(): return lax.ppermute(values, axes, [(i, i ^ mask) for i in range(count)])  62.7 us
    ppermute x2, waiting for transfers between devices, outwards(): self.moving = lax.ppermute(self.share, 'seq', [(1, 0), (2, 3)])  57.8 us
    all_gather x1, waiting for transfers between devices, on_device(): both_sums = lax.all_gather(jnp.stack(both_part), 'seq', axis=1, tiled=True)  43 us
    unnamed x147, local copies, waits for them, and re-layouts  38.9 us
    pallas_call x1, Pallas kernels, attend_forward(): pl.pallas_call(partial(forward_body, groups=groups, heads=heads, rows=row...  36.4 us
  transfers between devices with their start and end apart: 88, of which 40 were waited for; matrix products, arithmetic and copies ran while one was open for 22% of the time, Pallas kernels for 16%

profile of v4, /device:TPU:0, one launch (start us, length us, event | category | flops | bytes accessed | tf_op | source)
XLA Modules:
  0.0 895.5 jit_solution(17033440292590384991)
XLA Ops:
  20.5 5.0 all-to-all-start
  25.5 4.3 constant_dynamic-slice_fusion.21
  37.1 13.7 %collective-permute-done.5 = bf16[128,640]{1,0:T(8,128)(2,1)S(1)} collective-permute-done((bf16[128,640]{1,0:T(8,128)(2,1)S(1)}, bf16[128,640]{1,0:T(8,128)(2,1)S(1)}, u32[]{:S(2)}, u32[]{:S(2)}) %collective-permute-start.5) | collective-permute-done | bytes 163872 | tf_op jit(solution)/shard_map/ppermute | solution.py:55
  63.8 3.4 collective-permute-start.14
  68.4 5.0 broadcast_in_dim.44
  78.2 10.0 %collective-permute-done.9 = bf16[256,512]{1,0:T(8,128)(2,1)S(1)} collective-permute-done((bf16[256,512]{1,0:T(8,128)(2,1)S(1)}, bf16[256,512]{1,0:T(8,128)(2,1)S(1)}, u32[]{:S(2)}, u32[]{:S(2)}) %collective-permute-start.9) | collective-permute-done | bytes 262176 | tf_op jit(solution)/shard_map/ppermute | solution.py:55
  90.5 4.5 collective-permute-done.12
  95.1 5.5 collective-permute-done.15
  100.7 5.9 collective-permute-done.18
  110.7 3.4 copy-done.3
  114.1 4.7 project.2.q_ref
  119.3 4.8 all-to-all-start.1
  130.4 36.4 %attend_forward.1 = (bf16[256,2048]{1,0:T(8,128)(2,1)S(1)}, f32[8,4,64,256]{3,2,1,0:T(8,128)S(1)}, f32[8,4,256]{2,1,0:T(4,128)S(1)}) custom-call(bf16[256,2048]{1,0:T(8,128)(2,1)S(1)} %project.2.q_ref, bf16[16,16,16,512]{3,2,1,0:T(8,128)(2,1)S(1)} %bitcast.93), custom_call_target="tpu_custom_call" | custom-call | flops 36507222016 | bytes 6291456 | tf_op jit(solution)/shard_map/attend_forward/pallas_call | solution.py:404
  170.7 6.6 all-gather.7.cloned.1.call-done
  177.3 6.1 multiply_reduce_fusion.2
  190.8 7.6 maximum_select_fusion.d_ref
  198.4 23.0 %collective-permute-done.26 = bf16[256,2816]{1,0:T(8,128)(2,1)} collective-permute-done((bf16[256,2816]{1,0:T(8,128)(2,1)}, bf16[256,2816]{1,0:T(8,128)(2,1)}, u32[]{:S(2)}, u32[]{:S(2)}) %collective-permute-start.26) | collective-permute-done | bytes 1441824 | tf_op jit(solution)/shard_map/ppermute | solution.py:55
  221.4 21.4 %collective-permute-done.22 = bf16[256,2048]{1,0:T(8,128)(2,1)} collective-permute-done((bf16[256,2048]{1,0:T(8,128)(2,1)}, bf16[256,2048]{1,0:T(8,128)(2,1)}, u32[]{:S(2)}, u32[]{:S(2)}) %collective-permute-start.22) | collective-permute-done | bytes 1048608 | tf_op jit(solution)/shard_map/ppermute | solution.py:55
  267.7 13.5 %collective-permute-done.29 = bf16[128,2048]{1,0:T(8,128)(2,1)S(1)} collective-permute-done((bf16[128,2048]{1,0:T(8,128)(2,1)S(1)}, bf16[128,2048]{1,0:T(8,128)(2,1)S(1)}, u32[]{:S(2)}, u32[]{:S(2)}) %collective-permute-start.29) | collective-permute-done | bytes 524320 | tf_op jit(solution)/shard_map/ppermute | solution.py:55
  285.5 21.5 %feed.1 = (f32[1024,2816]{1,0:T(8,128)}, bf16[1024,1408]{1,0:T(8,128)(2,1)S(1)}) custom-call(bf16[1024,2048]{1,0:T(8,128)(2,1)S(1)} %constant_dynamic-update-slice_fusion.12.x_ref, bf16[2048,2816]{1,0:T(8,128)(2,1)} %constant_dynamic-update-slice_fusion.26.w_ref), custom_call_target="tpu_custom_call" | custom-call | flops 11811160064 | bytes 30146560 | tf_op jit(solution)/shard_map/feed/pallas_call | solution.py:667
  307.3 11.3 %feed_back.1 = bf16[1024,2816]{1,0:T(8,128)(2,1)S(1)} custom-call(bf16[1024,2048]{1,0:T(8,128)(2,1)S(1)} %constant_dynamic-update-slice_fusion.17.c_ref, bf16[1408,2048]{1,0:T(8,128)(2,1)S(1)} %bitcast.90, f32[1024,2816]{1,0:T(8,128)} %get-tuple-element.165.values_ref), custom_call_target="tpu_custom_call" | custom-call | flops 5905580032 | bytes 27262976 | tf_op jit(solution)/shard_map/feed_back/pallas_call | solution.py:696
  318.6 18.4 %convolution_convert_fusion.2 = bf16[1024,2048]{1,0:T(8,128)(2,1)} fusion(bf16[1024,2816]{1,0:T(8,128)(2,1)S(1)} %feed_back.1, bf16[2048,2816]{1,0:T(8,128)(2,1)} %constant_dynamic-update-slice_fusion.26.w_ref), kind=kOutput, calls=%fused_computation.17 | convolution fusion | flops 11813257216 | bytes 21495808 | tf_op jit(solution)/shard_map/dot_general | solution.py:28
  341.6 6.5 convolution_convert_fusion.1
  348.1 4.2 collective-permute-done.36
  353.6 5.3 collective-permute-done.40
  361.7 16.0 %convolution_convert_fusion = bf16[2048,2816]{1,0:T(8,128)(2,1)S(1)} fusion(bf16[1024,2048]{1,0:T(8,128)(2,1)} %copy-done.15, bf16[1024,2816]{1,0:T(8,128)(2,1)} %copy-done.5), kind=kOutput, calls=%fused_computation | convolution fusion | flops 11816927232 | bytes 21495808 | tf_op jit(solution)/shard_map/dot_general | solution.py:28
  388.7 5.3 fusion.37
  394.0 4.2 pad_maximum_fusion
  398.2 9.3 %collective-permute-done.38 = bf16[256,2048]{1,0:T(8,128)(2,1)} collective-permute-done((bf16[256,2048]{1,0:T(8,128)(2,1)}, bf16[256,2048]{1,0:T(8,128)(2,1)}, u32[]{:S(2)}, u32[]{:S(2)}) %collective-permute-start.38) | collective-permute-done | bytes 1048608 | tf_op jit(solution)/shard_map/ppermute | solution.py:55
  414.0 4.7 fusion.71
  418.7 3.9 fusion.36
  422.6 5.9 convolution_convert_fusion.4.do_ref
  432.0 70.2 %attend_backward.1 = (bf16[256,2048]{1,0:T(8,128)(2,1)S(1)}, bf16[16,16,16,512]{3,2,1,0:T(8,128)(2,1)S(1)}) custom-call(bf16[256,2048]{1,0:T(8,128)(2,1)S(1)} %project.2.q_ref, bf16[256,2048]{1,0:T(8,128)(2,1)S(1)} %convolution_convert_fusion.4.do_ref, bf16[16,16,16,512]{3,2,1,0:T(8,128)(2,1)S(1)} %bitcast.94, f32[8,4,64,256]{3,2,1,0:T(8,128)S(1)} %copy-done.11, ...), custom_call_target="tpu_custom_call" | custom-call | flops 285212672 | bytes 8388608 | tf_op jit(solution)/shard_map/attend_backward/pallas_call | solution.py:534
  507.6 3.8 fusion.73
  512.9 4.1 turn_back.2
  518.5 2.9 fusion.10
  528.3 3.7 fusion.15
  532.1 3.7 fusion.76
  535.7 11.2 %collective-permute-done.49 = bf16[4,256,512]{2,1,0:T(8,128)(2,1)S(1)} collective-permute-done((bf16[4,256,512]{2,1,0:T(8,128)(2,1)S(1)}, bf16[4,256,512]{2,1,0:T(8,128)(2,1)S(1)}, u32[]{:S(2)}, u32[]{:S(2)}) %collective-permute-start.49) | collective-permute-done | bytes 1048608 | tf_op jit(solution)/shard_map/ppermute | solution.py:55
  553.1 11.0 %convolution_convert_fusion.3 = bf16[1024,2048]{1,0:T(8,128)(2,1)} fusion(bf16[1024,1408]{1,0:T(8,128)(2,1)S(1)} %copy-done.17, bf16[1408,2048]{1,0:T(8,128)(2,1)} %maximum_select_fusion.d_ref), kind=kOutput, calls=%fused_computation.18 | convolution fusion | flops 5907677184 | bytes 12845056 | tf_op jit(solution)/shard_map/dot_general | solution.py:28
  564.1 9.0 %collective-permute-done.50 = bf16[256,512]{1,0:T(8,128)(2,1)S(1)} collective-permute-done((bf16[256,512]{1,0:T(8,128)(2,1)S(1)}, bf16[256,512]{1,0:T(8,128)(2,1)S(1)}, u32[]{:S(2)}, u32[]{:S(2)}) %collective-permute-start.50) | collective-permute-done | bytes 262176 | tf_op jit(solution)/shard_map/ppermute | solution.py:55
  576.7 4.5 collective-permute-done.51
  581.2 4.8 collective-permute-done.52
  586.1 3.9 collective-permute-done.54
  598.8 3.1 fusion.29
  601.9 3.0 fusion.28
  604.9 12.9 %collective-permute-done.57 = bf16[256,2048]{1,0:T(8,128)(2,1)} collective-permute-done((bf16[256,2048]{1,0:T(8,128)(2,1)}, bf16[256,2048]{1,0:T(8,128)(2,1)}, u32[]{:S(2)}, u32[]{:S(2)}) %collective-permute-start.57) | collective-permute-done | bytes 1048608 | tf_op jit(solution)/shard_map/ppermute | solution.py:55
  617.8 20.8 %collective-permute-done.58 = bf16[256,2048]{1,0:T(8,128)(2,1)} collective-permute-done((bf16[256,2048]{1,0:T(8,128)(2,1)}, bf16[256,2048]{1,0:T(8,128)(2,1)}, u32[]{:S(2)}, u32[]{:S(2)}) %collective-permute-start.58) | collective-permute-done | bytes 1048608 | tf_op jit(solution)/shard_map/ppermute | solution.py:55
  638.6 4.7 fusion.18
  656.6 9.6 %collective-permute-done.65 = bf16[2,512]{0,1:T(8,128)(2,1)S(1)} collective-permute-done((bf16[2,512]{0,1:T(8,128)(2,1)S(1)}, bf16[2,512]{0,1:T(8,128)(2,1)S(1)}, u32[]{:S(2)}, u32[]{:S(2)}) %collective-permute-start.65) | collective-permute-done | bytes 2080 | tf_op jit(solution)/shard_map/ppermute | solution.py:55
  670.4 43.0 %all-gather.11.cloned.1.call-done.values_ref = bf16[4,256,2816]{2,1,0:T(8,128)(2,1)} async-done(((bf16[4,64,2816]{2,1,0:T(8,128)(2,1)}), bf16[4,256,2816]{2,1,0:T(8,128)(2,1)}) %all-gather.11.cloned.1.call-update) | async-done | bytes 5767184 | tf_op jit(solution)/shard_map/all_gather | solution.py:917
  715.1 3.7 fusion.72
  722.3 4.4 place_columns.1
  726.6 18.3 %collective-permute-done.69 = bf16[256,2688]{1,0:T(8,128)(2,1)S(1)} collective-permute-done((bf16[256,2688]{1,0:T(8,128)(2,1)S(1)}, bf16[256,2688]{1,0:T(8,128)(2,1)S(1)}, u32[]{:S(2)}, u32[]{:S(2)}) %collective-permute-start.69) | collective-permute-done | bytes 1376288 | tf_op jit(solution)/shard_map/ppermute | solution.py:177
  747.2 6.4 all-to-all-start.2
  753.6 4.0 collective-permute-start.71
  757.6 10.0 %collective-permute-done.73 = bf16[256,2048]{1,0:T(8,128)(2,1)} collective-permute-done((bf16[256,2048]{1,0:T(8,128)(2,1)}, bf16[256,2048]{1,0:T(8,128)(2,1)}, u32[]{:S(2)}, u32[]{:S(2)}) %collective-permute-start.73) | collective-permute-done | bytes 1048608 | tf_op jit(solution)/shard_map/ppermute | solution.py:55
  767.6 5.6 collective-permute-done.72
  773.1 4.0 add_convert_fusion.9
  777.1 17.2 %collective-permute-done.71 = bf16[256,2048]{1,0:T(8,128)(2,1)S(1)} collective-permute-done((bf16[256,2048]{1,0:T(8,128)(2,1)}, bf16[256,2048]{1,0:T(8,128)(2,1)S(1)}, u32[]{:S(2)}, u32[]{:S(2)}) %collective-permute-start.71) | collective-permute-done | bytes 1048608 | tf_op jit(solution)/shard_map/ppermute | solution.py:177
  798.8 8.1 all-to-all-start.3
  813.1 5.1 convert_element_type.386
  821.0 35.9 %collective-permute-done.75 = bf16[256,2688]{1,0:T(8,128)(2,1)} collective-permute-done((bf16[256,2688]{1,0:T(8,128)(2,1)S(1)}, bf16[256,2688]{1,0:T(8,128)(2,1)}, u32[]{:S(2)}, u32[]{:S(2)}) %collective-permute-start.75) | collective-permute-done | bytes 1376288 | tf_op jit(solution)/shard_map/ppermute | solution.py:185
  856.9 21.9 %collective-permute-done.77 = bf16[256,2048]{1,0:T(8,128)(2,1)S(1)} collective-permute-done((bf16[256,2048]{1,0:T(8,128)(2,1)S(1)}, bf16[256,2048]{1,0:T(8,128)(2,1)S(1)}, u32[]{:S(2)}, u32[]{:S(2)}) %collective-permute-start.77) | collective-permute-done | bytes 1048608 | tf_op jit(solution)/shard_map/ppermute | solution.py:185
  (407 shorter events, 203.8 us)
Async XLA Ops:
  7.2 103.5 %all-gather.5.cloned.1.call-start = ((), (), s32[]{:S(2)}) async-start(), calls=%async_computation.6 | async-start | bytes 9437184 | tf_op jit(solution)/shard_map/all_gather | solution.py:754
  7.9 169.4 %all-gather.7.cloned.1.call-start = ((), (), s32[]{:S(2)}) async-start(), calls=%async_computation.7 | async-start | bytes 9437184 | tf_op jit(solution)/shard_map/all_gather | solution.py:755
  13.4 22.7 %collective-permute-start = (bf16[256,640]{1,0:T(8,128)(2,1)}, bf16[256,640]{1,0:T(8,128)(2,1)}, u32[]{:S(2)}, u32[]{:S(2)}) collective-permute-start(bf16[256,640]{1,0:T(8,128)(2,1)} %get-tuple-element.341), channel_id=1, source_target_pairs={{0,1},{1,0},{2,3},{3,2},{16,17},{17,16},{18,19},{19,18},{4,5},{5,4... | collective-permute-start | bytes 983048 | tf_op jit(solution)/shard_map/ppermute | solution.py:55
  13.8 19.6 %collective-permute-start.1 = (bf16[256,640]{1,0:T(8,128)(2,1)}, bf16[256,640]{1,0:T(8,128)(2,1)S(1)}, u32[]{:S(2)}, u32[]{:S(2)}) collective-permute-start(bf16[256,640]{1,0:T(8,128)(2,1)} %get-tuple-element.341), channel_id=1, source_target_pairs={{0,2},{1,3},{2,0},{3,1},{16,18},{17,19},{18,16},{19,17},{4,6},{5,7... | collective-permute-start | bytes 983048 | tf_op jit(solution)/shard_map/ppermute | solution.py:55
  16.3 17.5 %collective-permute-start.3 = (bf16[256,640]{1,0:T(8,128)(2,1)}, bf16[256,640]{1,0:T(8,128)(2,1)S(1)}, u32[]{:S(2)}, u32[]{:S(2)}) collective-permute-start(bf16[256,640]{1,0:T(8,128)(2,1)} %get-tuple-element.341), channel_id=1, source_target_pairs={{0,16},{1,17},{2,18},{3,19},{16,0},{17,1},{18,2},{19,3},{4,20},{5,... | collective-permute-start | bytes 983048 | tf_op jit(solution)/shard_map/ppermute | solution.py:55
  20.5 33.0 %all-to-all-start = ((bf16[16,16,2176]{2,1,0:T(8,128)(2,1)}), bf16[16,16,2176]{2,1,0:T(8,128)(2,1)}, u32[]{:S(2)}, u32[]{:S(2)}) async-start(bf16[16,16,2176]{2,1,0:T(8,128)(2,1)} %bitcast.96), calls=%async_computation | async-start | bytes 2228224 | tf_op jit(solution)/shard_map/all_to_all | solution.py:249
  33.4 17.9 %collective-permute-start.2 = (bf16[256,640]{1,0:T(8,128)(2,1)S(1)}, bf16[256,640]{1,0:T(8,128)(2,1)S(1)}, u32[]{:S(2)}, u32[]{:S(2)}) collective-permute-start(bf16[256,640]{1,0:T(8,128)(2,1)S(1)} %collective-permute-done.1), channel_id=1, source_target_pairs={{0,1},{1,0},{2,3},{3,2},{16,17},{17,16},{18,19},{19,18},{4,5},{5,4... | collective-permute-start | bytes 983048 | tf_op jit(solution)/shard_map/ppermute | solution.py:55
  33.8 17.0 %collective-permute-start.5 = (bf16[128,640]{1,0:T(8,128)(2,1)S(1)}, bf16[128,640]{1,0:T(8,128)(2,1)S(1)}, u32[]{:S(2)}, u32[]{:S(2)}) collective-permute-start(bf16[128,640]{1,0:T(8,128)(2,1)S(1)} %slice.203), channel_id=1, source_target_pairs={{0,2},{1,3},{2,0},{3,1},{16,18},{17,19},{18,16},{19,17},{4,6},{5,7... | collective-permute-start | bytes 491528 | tf_op jit(solution)/shard_map/ppermute | solution.py:55
  35.6 15.2 %collective-permute-start.7 = (bf16[128,640]{1,0:T(8,128)(2,1)S(1)}, bf16[128,640]{1,0:T(8,128)(2,1)S(1)}, u32[]{:S(2)}, u32[]{:S(2)}) collective-permute-start(bf16[128,640]{1,0:T(8,128)(2,1)S(1)} %slice.204), channel_id=1, source_target_pairs={{0,16},{1,17},{2,18},{3,19},{16,0},{17,1},{18,2},{19,3},{4,20},{5,... | collective-permute-start | bytes 491528 | tf_op jit(solution)/shard_map/ppermute | solution.py:55
  36.1 15.4 %collective-permute-start.4 = (bf16[256,640]{1,0:T(8,128)(2,1)S(1)}, bf16[256,640]{1,0:T(8,128)(2,1)S(1)}, u32[]{:S(2)}, u32[]{:S(2)}) collective-permute-start(bf16[256,640]{1,0:T(8,128)(2,1)S(1)} %collective-permute-done.3), channel_id=1, source_target_pairs={{0,1},{1,0},{2,3},{3,2},{16,17},{17,16},{18,19},{19,18},{4,5},{5,4... | collective-permute-start | bytes 983048 | tf_op jit(solution)/shard_map/ppermute | solution.py:55
  63.8 24.5 %collective-permute-start.14 = (bf16[256,512]{1,0:T(8,128)(2,1)S(1)}, bf16[256,512]{1,0:T(8,128)(2,1)S(1)}, u32[]{:S(2)}, u32[]{:S(2)}) collective-permute-start(bf16[256,512]{1,0:T(8,128)(2,1)S(1)} %project.3), channel_id=1, source_target_pairs={{0,8},{4,12},{8,0},{12,4},{1,9},{5,13},{9,1},{13,5},{2,10},{6,14},... | collective-permute-start | bytes 786440 | tf_op jit(solution)/shard_map/ppermute | solution.py:55
  67.1 22.1 %collective-permute-start.17 = (bf16[256,512]{1,0:T(8,128)(2,1)S(1)}, bf16[256,512]{1,0:T(8,128)(2,1)S(1)}, u32[]{:S(2)}, u32[]{:S(2)}) collective-permute-start(bf16[256,512]{1,0:T(8,128)(2,1)S(1)} %project.3), channel_id=1, source_target_pairs={{0,12},{4,8},{8,4},{12,0},{1,13},{5,9},{9,5},{13,1},{2,14},{6,10},... | collective-permute-start | bytes 786440 | tf_op jit(solution)/shard_map/ppermute | solution.py:55
  73.4 14.8 %collective-permute-start.9 = (bf16[256,512]{1,0:T(8,128)(2,1)S(1)}, bf16[256,512]{1,0:T(8,128)(2,1)S(1)}, u32[]{:S(2)}, u32[]{:S(2)}) collective-permute-start(bf16[256,512]{1,0:T(8,128)(2,1)S(1)} %project.3), channel_id=1, source_target_pairs={{0,2},{1,3},{2,0},{3,1},{4,6},{5,7},{6,4},{7,5},{8,10},{9,11},{10,... | collective-permute-start | bytes 786440 | tf_op jit(solution)/shard_map/ppermute | solution.py:55
  77.0 18.0 %collective-permute-start.12 = (bf16[256,512]{1,0:T(8,128)(2,1)S(1)}, bf16[256,512]{1,0:T(8,128)(2,1)S(1)}, u32[]{:S(2)}, u32[]{:S(2)}) collective-permute-start(bf16[256,512]{1,0:T(8,128)(2,1)S(1)} %collective-permute-done.11), channel_id=1, source_target_pairs={{0,2},{1,3},{2,0},{3,1},{4,6},{5,7},{6,4},{7,5},{8,10},{9,11},{10,... | collective-permute-start | bytes 786440 | tf_op jit(solution)/shard_map/ppermute | solution.py:55
  88.2 18.5 %collective-permute-start.10 = (bf16[512,512]{1,0:T(8,128)(2,1)S(1)}, bf16[512,512]{1,0:T(8,128)(2,1)S(1)}, u32[]{:S(2)}, u32[]{:S(2)}) collective-permute-start(bf16[512,512]{1,0:T(8,128)(2,1)S(1)} %pad_maximum_fusion.12), channel_id=1, source_target_pairs={{0,1},{1,0},{2,3},{3,2},{4,5},{5,4},{6,7},{7,6},{8,9},{9,8},{10,11... | collective-permute-start | bytes 1572872 | tf_op jit(solution)/shard_map/ppermute | solution.py:55
  89.3 17.3 %collective-permute-start.18 = (bf16[256,512]{1,0:T(8,128)(2,1)S(1)}, bf16[256,512]{1,0:T(8,128)(2,1)S(1)}, u32[]{:S(2)}, u32[]{:S(2)}) collective-permute-start(bf16[256,512]{1,0:T(8,128)(2,1)S(1)} %collective-permute-done.17), channel_id=1, source_target_pairs={{0,2},{1,3},{2,0},{3,1},{4,6},{5,7},{6,4},{7,5},{8,10},{9,11},{10,... | collective-permute-start | bytes 786440 | tf_op jit(solution)/shard_map/ppermute | solution.py:55
  118.8 51.9 %collective-permute-start.20 = (bf16[704,2048]{1,0:T(8,128)(2,1)}, bf16[704,2048]{1,0:T(8,128)(2,1)}, u32[]{:S(2)}, u32[]{:S(2)}) collective-permute-start(bf16[704,2048]{1,0:T(8,128)(2,1)} %param.21), channel_id=1, source_target_pairs={{0,1},{1,0},{2,3},{3,2},{16,17},{17,16},{18,19},{19,18},{4,5},{5,4... | collective-permute-start | bytes 8650760 | tf_op jit(solution)/shard_map/ppermute | solution.py:55
  119.0 51.7 %collective-permute-start.21 = (bf16[256,2816]{1,0:T(8,128)(2,1)}, bf16[256,2816]{1,0:T(8,128)(2,1)}, u32[]{:S(2)}, u32[]{:S(2)}) collective-permute-start(bf16[256,2816]{1,0:T(8,128)(2,1)} %pad_maximum_fusion.5), channel_id=1, source_target_pairs={{0,1},{1,0},{2,3},{3,2},{16,17},{17,16},{18,19},{19,18},{4,5},{5,4... | collective-permute-start | bytes 4325384 | tf_op jit(solution)/shard_map/ppermute | solution.py:55
  119.3 66.5 %all-to-all-start.1 = ((bf16[16,16,2048]{2,1,0:T(8,128)(2,1)}), bf16[16,16,2048]{2,1,0:T(8,128)(2,1)}, u32[]{:S(2)}, u32[]{:S(2)}) async-start(bf16[16,16,2048]{2,1,0:T(8,128)(2,1)} %bitcast.100), calls=%async_computation.1 | async-start | bytes 2097152 | tf_op jit(solution)/shard_map/all_to_all | solution.py:249
  124.1 383.5 %reduce-scatter.3.cloned.1.call-start = ((), (), s32[]{:S(2)}) async-start(), calls=%async_computation.8 | async-start | bytes 3604480 | tf_op jit(solution)/shard_map/reduce_scatter | solution.py:871
  124.6 73.8 %collective-permute-start.24 = (bf16[256,2816]{1,0:T(8,128)(2,1)}, bf16[256,2816]{1,0:T(8,128)(2,1)}, u32[]{:S(2)}, u32[]{:S(2)}) collective-permute-start(bf16[256,2816]{1,0:T(8,128)(2,1)} %pad_maximum_fusion.6), channel_id=1, source_target_pairs={{0,2},{1,3},{2,0},{3,1},{16,18},{17,19},{18,16},{19,17},{4,6},{5,7... | collective-permute-start | bytes 4325384 | tf_op jit(solution)/shard_map/ppermute | solution.py:55
  126.6 71.8 %collective-permute-start.25 = (bf16[256,2816]{1,0:T(8,128)(2,1)}, bf16[256,2816]{1,0:T(8,128)(2,1)}, u32[]{:S(2)}, u32[]{:S(2)}) collective-permute-start(bf16[256,2816]{1,0:T(8,128)(2,1)} %pad_maximum_fusion.7), channel_id=1, source_target_pairs={{0,16},{1,17},{2,18},{3,19},{16,0},{17,1},{18,2},{19,3},{4,20},{5,... | collective-permute-start | bytes 4325384 | tf_op jit(solution)/shard_map/ppermute | solution.py:55
  128.0 93.4 %collective-permute-start.26 = (bf16[256,2816]{1,0:T(8,128)(2,1)}, bf16[256,2816]{1,0:T(8,128)(2,1)}, u32[]{:S(2)}, u32[]{:S(2)}) collective-permute-start(bf16[256,2816]{1,0:T(8,128)(2,1)} %pad_maximum_fusion.8), channel_id=1, source_target_pairs={{0,18},{1,19},{2,16},{3,17},{16,2},{17,3},{18,0},{19,1},{4,22},{5,... | collective-permute-start | bytes 4325384 | tf_op jit(solution)/shard_map/ppermute | solution.py:55
  185.9 56.9 %collective-permute-start.22 = (bf16[256,2048]{1,0:T(8,128)(2,1)}, bf16[256,2048]{1,0:T(8,128)(2,1)}, u32[]{:S(2)}, u32[]{:S(2)}) collective-permute-start(bf16[256,2048]{1,0:T(8,128)(2,1)} %multiply_convert_fusion), channel_id=1, source_target_pairs={{0,2},{1,3},{2,0},{3,1},{16,18},{17,19},{18,16},{19,17},{4,6},{5,7... | collective-permute-start | bytes 3145736 | tf_op jit(solution)/shard_map/ppermute | solution.py:55
  186.1 56.7 %collective-permute-start.23 = (bf16[256,2048]{1,0:T(8,128)(2,1)}, bf16[256,2048]{1,0:T(8,128)(2,1)}, u32[]{:S(2)}, u32[]{:S(2)}) collective-permute-start(bf16[256,2048]{1,0:T(8,128)(2,1)} %multiply_convert_fusion), channel_id=1, source_target_pairs={{0,16},{1,17},{2,18},{3,19},{16,0},{17,1},{18,2},{19,3},{4,20},{5,... | collective-permute-start | bytes 3145736 | tf_op jit(solution)/shard_map/ppermute | solution.py:55
  244.1 38.2 %collective-permute-start.27 = (bf16[256,2048]{1,0:T(8,128)(2,1)}, bf16[256,2048]{1,0:T(8,128)(2,1)S(1)}, u32[]{:S(2)}, u32[]{:S(2)}) collective-permute-start(bf16[256,2048]{1,0:T(8,128)(2,1)} %bitcast.9), channel_id=1, source_target_pairs={{0,2},{1,3},{2,0},{3,1},{16,18},{17,19},{18,16},{19,17},{4,6},{5,7... | collective-permute-start | bytes 3145736 | tf_op jit(solution)/shard_map/ppermute | solution.py:55
  245.5 36.7 %collective-permute-start.28 = (bf16[256,2048]{1,0:T(8,128)(2,1)}, bf16[256,2048]{1,0:T(8,128)(2,1)S(1)}, u32[]{:S(2)}, u32[]{:S(2)}) collective-permute-start(bf16[256,2048]{1,0:T(8,128)(2,1)} %bitcast.9), channel_id=1, source_target_pairs={{0,16},{1,17},{2,18},{3,19},{16,0},{17,1},{18,2},{19,3},{4,20},{5,... | collective-permute-start | bytes 3145736 | tf_op jit(solution)/shard_map/ppermute | solution.py:55
  247.3 33.9 %collective-permute-start.29 = (bf16[128,2048]{1,0:T(8,128)(2,1)S(1)}, bf16[128,2048]{1,0:T(8,128)(2,1)S(1)}, u32[]{:S(2)}, u32[]{:S(2)}) collective-permute-start(bf16[128,2048]{1,0:T(8,128)(2,1)S(1)} %slice.165), channel_id=1, source_target_pairs={{0,2},{1,3},{2,0},{3,1},{16,18},{17,19},{18,16},{19,17},{4,6},{5,7... | collective-permute-start | bytes 1572872 | tf_op jit(solution)/shard_map/ppermute | solution.py:55
  262.2 20.1 %collective-permute-start.30 = (bf16[128,2048]{1,0:T(8,128)(2,1)S(1)}, bf16[128,2048]{1,0:T(8,128)(2,1)S(1)}, u32[]{:S(2)}, u32[]{:S(2)}) collective-permute-start(bf16[128,2048]{1,0:T(8,128)(2,1)S(1)} %slice.166), channel_id=1, source_target_pairs={{0,16},{1,17},{2,18},{3,19},{16,0},{17,1},{18,2},{19,3},{4,20},{5,... | collective-permute-start | bytes 1572872 | tf_op jit(solution)/shard_map/ppermute | solution.py:55
  282.3 24.9 %collective-permute-start.34 = (bf16[128,2048]{1,0:T(8,128)(2,1)S(1)}, bf16[128,2048]{1,0:T(8,128)(2,1)S(1)}, u32[]{:S(2)}, u32[]{:S(2)}) collective-permute-start(bf16[128,2048]{1,0:T(8,128)(2,1)S(1)} %slice.167), channel_id=1, source_target_pairs={{0,2},{1,3},{2,0},{3,1},{16,18},{17,19},{18,16},{19,17},{4,6},{5,7... | collective-permute-start | bytes 1572872 | tf_op jit(solution)/shard_map/ppermute | solution.py:55
  283.9 23.3 %collective-permute-start.35 = (bf16[128,2048]{1,0:T(8,128)(2,1)}, bf16[128,2048]{1,0:T(8,128)(2,1)S(1)}, u32[]{:S(2)}, u32[]{:S(2)}) collective-permute-start(bf16[128,2048]{1,0:T(8,128)(2,1)} %slice.168), channel_id=1, source_target_pairs={{0,16},{1,17},{2,18},{3,19},{16,0},{17,1},{18,2},{19,3},{4,20},{5,... | collective-permute-start | bytes 1572872 | tf_op jit(solution)/shard_map/ppermute | solution.py:55
  361.7 185.3 %reduce-scatter.5.cloned.1.call-start = ((), (), s32[]{:S(2)}) async-start(), calls=%async_computation.9 | async-start | bytes 7208960 | tf_op jit(solution)/shard_map/reduce_scatter | solution.py:875
  381.9 25.5 %collective-permute-start.38 = (bf16[256,2048]{1,0:T(8,128)(2,1)}, bf16[256,2048]{1,0:T(8,128)(2,1)}, u32[]{:S(2)}, u32[]{:S(2)}) collective-permute-start(bf16[256,2048]{1,0:T(8,128)(2,1)} %pad_maximum_fusion.10), channel_id=1, source_target_pairs={{0,2},{1,3},{2,0},{3,1},{16,18},{17,19},{18,16},{19,17},{4,6},{5,7... | collective-permute-start | bytes 3145736 | tf_op jit(solution)/shard_map/ppermute | solution.py:55
  384.2 25.3 %collective-permute-start.39 = (bf16[256,2048]{1,0:T(8,128)(2,1)}, bf16[256,2048]{1,0:T(8,128)(2,1)}, u32[]{:S(2)}, u32[]{:S(2)}) collective-permute-start(bf16[256,2048]{1,0:T(8,128)(2,1)} %pad_maximum_fusion.11), channel_id=1, source_target_pairs={{0,16},{1,17},{2,18},{3,19},{16,0},{17,1},{18,2},{19,3},{4,20},{5,... | collective-permute-start | bytes 3145736 | tf_op jit(solution)/shard_map/ppermute | solution.py:55
  409.5 247.1 %all-gather.9.cloned.1.call-start = ((), (), s32[]{:S(2)}) async-start(), calls=%async_computation.10 | async-start | bytes 3604480 | tf_op jit(solution)/shard_map/all_gather | solution.py:898
  428.5 76.8 %collective-permute-start.45 = (bf16[256,3072]{1,0:T(8,128)(2,1)S(1)}, bf16[256,3072]{1,0:T(8,128)(2,1)S(1)}, u32[]{:S(2)}, u32[]{:S(2)}) collective-permute-start(bf16[256,3072]{1,0:T(8,128)(2,1)S(1)} %get-tuple-element.183), channel_id=1, source_target_pairs={{0,2},{1,3},{2,0},{3,1},{16,18},{17,19},{18,16},{19,17},{4,6},{5,7... | collective-permute-start | bytes 4718600 | tf_op jit(solution)/shard_map/ppermute | solution.py:55
  429.3 75.9 %collective-permute-start.46 = (bf16[256,3072]{1,0:T(8,128)(2,1)S(1)}, bf16[256,3072]{1,0:T(8,128)(2,1)S(1)}, u32[]{:S(2)}, u32[]{:S(2)}) collective-permute-start(bf16[256,3072]{1,0:T(8,128)(2,1)S(1)} %get-tuple-element.184), channel_id=1, source_target_pairs={{0,16},{1,17},{2,18},{3,19},{16,0},{17,1},{18,2},{19,3},{4,20},{5,... | collective-permute-start | bytes 4718600 | tf_op jit(solution)/shard_map/ppermute | solution.py:55
  430.7 76.8 %collective-permute-start.47 = (bf16[256,3072]{1,0:T(8,128)(2,1)S(1)}, bf16[256,3072]{1,0:T(8,128)(2,1)}, u32[]{:S(2)}, u32[]{:S(2)}) collective-permute-start(bf16[256,3072]{1,0:T(8,128)(2,1)S(1)} %get-tuple-element.185), channel_id=1, source_target_pairs={{0,18},{1,19},{2,16},{3,17},{16,2},{17,3},{18,0},{19,1},{4,22},{5,... | collective-permute-start | bytes 4718600 | tf_op jit(solution)/shard_map/ppermute | solution.py:55
  512.9 200.6 %all-gather.11.cloned.1.call-start = ((), (), s32[]{:S(2)}) async-start(), calls=%async_computation.11 | async-start | bytes 7208960 | tf_op jit(solution)/shard_map/all_gather | solution.py:917
  521.5 25.5 %collective-permute-start.49 = (bf16[4,256,512]{2,1,0:T(8,128)(2,1)S(1)}, bf16[4,256,512]{2,1,0:T(8,128)(2,1)S(1)}, u32[]{:S(2)}, u32[]{:S(2)}) collective-permute-start(bf16[4,256,512]{2,1,0:T(8,128)(2,1)S(1)} %slice_bitcast_fusion), channel_id=1, source_target_pairs={{0,2},{1,3},{2,0},{3,1},{4,6},{5,7},{6,4},{7,5},{8,10},{9,11},{10,... | collective-permute-start | bytes 3145736 | tf_op jit(solution)/shard_map/ppermute | solution.py:55
  547.4 25.7 %collective-permute-start.50 = (bf16[256,512]{1,0:T(8,128)(2,1)S(1)}, bf16[256,512]{1,0:T(8,128)(2,1)S(1)}, u32[]{:S(2)}, u32[]{:S(2)}) collective-permute-start(bf16[256,512]{1,0:T(8,128)(2,1)S(1)} %get-tuple-element.322), channel_id=1, source_target_pairs={{0,4},{4,0},{8,12},{12,8},{1,5},{5,1},{9,13},{13,9},{2,6},{6,2},{1... | collective-permute-start | bytes 786440 | tf_op jit(solution)/shard_map/ppermute | solution.py:55
  548.8 32.4 %collective-permute-start.51 = (bf16[256,512]{1,0:T(8,128)(2,1)S(1)}, bf16[256,512]{1,0:T(8,128)(2,1)S(1)}, u32[]{:S(2)}, u32[]{:S(2)}) collective-permute-start(bf16[256,512]{1,0:T(8,128)(2,1)S(1)} %get-tuple-element.321), channel_id=1, source_target_pairs={{0,8},{4,12},{8,0},{12,4},{1,9},{5,13},{9,1},{13,5},{2,10},{6,14},... | collective-permute-start | bytes 786440 | tf_op jit(solution)/shard_map/ppermute | solution.py:55
  551.3 34.8 %collective-permute-start.52 = (bf16[256,512]{1,0:T(8,128)(2,1)S(1)}, bf16[256,512]{1,0:T(8,128)(2,1)S(1)}, u32[]{:S(2)}, u32[]{:S(2)}) collective-permute-start(bf16[256,512]{1,0:T(8,128)(2,1)S(1)} %get-tuple-element.320), channel_id=1, source_target_pairs={{0,12},{4,8},{8,4},{12,0},{1,13},{5,9},{9,5},{13,1},{2,14},{6,10},... | collective-permute-start | bytes 786440 | tf_op jit(solution)/shard_map/ppermute | solution.py:55
  551.9 34.2 %collective-permute-start.53 = (bf16[64,2816]{1,0:T(8,128)(2,1)S(1)}, bf16[64,2816]{1,0:T(8,128)(2,1)S(1)}, u32[]{:S(2)}, u32[]{:S(2)}) collective-permute-start(bf16[64,2816]{1,0:T(8,128)(2,1)S(1)} %get-tuple-element.318), channel_id=1, source_target_pairs={{0,2},{1,3},{2,0},{3,1},{16,18},{17,19},{18,16},{19,17},{4,6},{5,7... | collective-permute-start | bytes 1081352 | tf_op jit(solution)/shard_map/ppermute | solution.py:55
  553.0 20.9 %collective-permute-start.56 = (bf16[256,2048]{1,0:T(8,128)(2,1)S(1)}, bf16[256,2048]{1,0:T(8,128)(2,1)S(1)}, u32[]{:S(2)}, u32[]{:S(2)}) collective-permute-start(bf16[256,2048]{1,0:T(8,128)(2,1)S(1)} %constant_dynamic-slice_fusion.6), channel_id=1, source_target_pairs={{0,1},{1,0},{2,3},{3,2},{16,17},{17,16},{18,19},{19,18},{4,5},{5,4... | collective-permute-start | bytes 3145736 | tf_op jit(solution)/shard_map/ppermute | solution.py:55
  573.1 16.9 %collective-permute-start.54 = (bf16[64,2816]{1,0:T(8,128)(2,1)S(1)}, bf16[64,2816]{1,0:T(8,128)(2,1)S(1)}, u32[]{:S(2)}, u32[]{:S(2)}) collective-permute-start(bf16[64,2816]{1,0:T(8,128)(2,1)S(1)} %get-tuple-element.317), channel_id=1, source_target_pairs={{0,16},{1,17},{2,18},{3,19},{16,0},{17,1},{18,2},{19,3},{4,20},{5,... | collective-permute-start | bytes 1081352 | tf_op jit(solution)/shard_map/ppermute | solution.py:55
  573.9 16.1 %collective-permute-start.55 = (bf16[64,2816]{1,0:T(8,128)(2,1)S(1)}, bf16[64,2816]{1,0:T(8,128)(2,1)S(1)}, u32[]{:S(2)}, u32[]{:S(2)}) collective-permute-start(bf16[64,2816]{1,0:T(8,128)(2,1)S(1)} %get-tuple-element.316), channel_id=1, source_target_pairs={{0,18},{1,19},{2,16},{3,17},{16,2},{17,3},{18,0},{19,1},{4,22},{5,... | collective-permute-start | bytes 1081352 | tf_op jit(solution)/shard_map/ppermute | solution.py:55
  591.3 26.5 %collective-permute-start.57 = (bf16[256,2048]{1,0:T(8,128)(2,1)}, bf16[256,2048]{1,0:T(8,128)(2,1)}, u32[]{:S(2)}, u32[]{:S(2)}) collective-permute-start(bf16[256,2048]{1,0:T(8,128)(2,1)} %turn_back.2), channel_id=1, source_target_pairs={{0,2},{1,3},{2,0},{3,1},{16,18},{17,19},{18,16},{19,17},{4,6},{5,7... | collective-permute-start | bytes 3145736 | tf_op jit(solution)/shard_map/ppermute | solution.py:55
  592.4 46.2 %collective-permute-start.58 = (bf16[256,2048]{1,0:T(8,128)(2,1)}, bf16[256,2048]{1,0:T(8,128)(2,1)}, u32[]{:S(2)}, u32[]{:S(2)}) collective-permute-start(bf16[256,2048]{1,0:T(8,128)(2,1)} %turn_back.2), channel_id=1, source_target_pairs={{0,16},{1,17},{2,18},{3,19},{16,0},{17,1},{18,2},{19,3},{4,20},{5,... | collective-permute-start | bytes 3145736 | tf_op jit(solution)/shard_map/ppermute | solution.py:55
  593.9 44.7 %collective-permute-start.59 = (bf16[256,2048]{1,0:T(8,128)(2,1)}, bf16[256,2048]{1,0:T(8,128)(2,1)}, u32[]{:S(2)}, u32[]{:S(2)}) collective-permute-start(bf16[256,2048]{1,0:T(8,128)(2,1)} %turn_back.2), channel_id=1, source_target_pairs={{0,18},{1,19},{2,16},{3,17},{16,2},{17,3},{18,0},{19,1},{4,22},{5,... | collective-permute-start | bytes 3145736 | tf_op jit(solution)/shard_map/ppermute | solution.py:55
  646.3 20.0 %collective-permute-start.61 = (bf16[256,512]{1,0:T(8,128)(2,1)S(1)}, bf16[256,512]{1,0:T(8,128)(2,1)S(1)}, u32[]{:S(2)}, u32[]{:S(2)}) collective-permute-start(bf16[256,512]{1,0:T(8,128)(2,1)S(1)} %copy-done.49), channel_id=1, source_target_pairs={{0,2},{1,3},{2,0},{3,1},{16,18},{17,19},{18,16},{19,17},{4,6},{5,7... | collective-permute-start | bytes 786440 | tf_op jit(solution)/shard_map/ppermute | solution.py:55
  646.9 19.4 %collective-permute-start.62 = (bf16[256,512]{1,0:T(8,128)(2,1)S(1)}, bf16[256,512]{1,0:T(8,128)(2,1)}, u32[]{:S(2)}, u32[]{:S(2)}) collective-permute-start(bf16[256,512]{1,0:T(8,128)(2,1)S(1)} %copy-done.49), channel_id=1, source_target_pairs={{0,16},{1,17},{2,18},{3,19},{16,0},{17,1},{18,2},{19,3},{4,20},{5,... | collective-permute-start | bytes 786440 | tf_op jit(solution)/shard_map/ppermute | solution.py:55
  648.6 17.7 %collective-permute-start.63 = (bf16[256,512]{1,0:T(8,128)(2,1)S(1)}, bf16[256,512]{1,0:T(8,128)(2,1)}, u32[]{:S(2)}, u32[]{:S(2)}) collective-permute-start(bf16[256,512]{1,0:T(8,128)(2,1)S(1)} %copy-done.49), channel_id=1, source_target_pairs={{0,18},{1,19},{2,16},{3,17},{16,2},{17,3},{18,0},{19,1},{4,22},{5,... | collective-permute-start | bytes 786440 | tf_op jit(solution)/shard_map/ppermute | solution.py:55
  651.1 15.1 %collective-permute-start.65 = (bf16[2,512]{0,1:T(8,128)(2,1)S(1)}, bf16[2,512]{0,1:T(8,128)(2,1)S(1)}, u32[]{:S(2)}, u32[]{:S(2)}) collective-permute-start(bf16[2,512]{0,1:T(8,128)(2,1)S(1)} %get-tuple-element.338), channel_id=1, source_target_pairs={{0,16},{1,17},{2,18},{3,19},{16,0},{17,1},{18,2},{19,3},{4,20},{5,... | collective-permute-start | bytes 6152 | tf_op jit(solution)/shard_map/ppermute | solution.py:55
  713.5 31.5 %collective-permute-start.69 = (bf16[256,2688]{1,0:T(8,128)(2,1)S(1)}, bf16[256,2688]{1,0:T(8,128)(2,1)S(1)}, u32[]{:S(2)}, u32[]{:S(2)}) collective-permute-start(bf16[256,2688]{1,0:T(8,128)(2,1)S(1)} %fusion.41), channel_id=1, source_target_pairs={{0,4},{12,8},{1,5},{13,9},{2,6},{14,10},{3,7},{15,11},{16,20},{28,... | collective-permute-start | bytes 4128776 | tf_op jit(solution)/shard_map/ppermute | solution.py:177
  718.8 38.8 %collective-permute-start.74 = (bf16[256,2048]{1,0:T(8,128)(2,1)}, bf16[256,2048]{1,0:T(8,128)(2,1)}, u32[]{:S(2)}, u32[]{:S(2)}) collective-permute-start(bf16[256,2048]{1,0:T(8,128)(2,1)} %get-tuple-element.298), channel_id=1, source_target_pairs={{0,18},{1,19},{2,16},{3,17},{16,2},{17,3},{18,0},{19,1},{4,22},{5,... | collective-permute-start | bytes 3145736 | tf_op jit(solution)/shard_map/ppermute | solution.py:55
  721.2 46.4 %collective-permute-start.73 = (bf16[256,2048]{1,0:T(8,128)(2,1)}, bf16[256,2048]{1,0:T(8,128)(2,1)}, u32[]{:S(2)}, u32[]{:S(2)}) collective-permute-start(bf16[256,2048]{1,0:T(8,128)(2,1)} %get-tuple-element.299), channel_id=1, source_target_pairs={{0,16},{1,17},{2,18},{3,19},{16,0},{17,1},{18,2},{19,3},{4,20},{5,... | collective-permute-start | bytes 3145736 | tf_op jit(solution)/shard_map/ppermute | solution.py:55
  721.7 51.4 %collective-permute-start.72 = (bf16[256,2048]{1,0:T(8,128)(2,1)}, bf16[256,2048]{1,0:T(8,128)(2,1)}, u32[]{:S(2)}, u32[]{:S(2)}) collective-permute-start(bf16[256,2048]{1,0:T(8,128)(2,1)} %get-tuple-element.297), channel_id=1, source_target_pairs={{0,2},{1,3},{2,0},{3,1},{16,18},{17,19},{18,16},{19,17},{4,6},{5,7... | collective-permute-start | bytes 3145736 | tf_op jit(solution)/shard_map/ppermute | solution.py:55
  745.3 49.0 %collective-permute-start.70 = (bf16[256,2688]{1,0:T(8,128)(2,1)S(1)}, bf16[256,2688]{1,0:T(8,128)(2,1)}, u32[]{:S(2)}, u32[]{:S(2)}) collective-permute-start(bf16[256,2688]{1,0:T(8,128)(2,1)S(1)} %add_convert_fusion.6), channel_id=1, source_target_pairs={{4,8},{8,4},{5,9},{9,5},{6,10},{10,6},{7,11},{11,7},{20,24},{24,20... | collective-permute-start | bytes 4128776 | tf_op jit(solution)/shard_map/ppermute | solution.py:181
  747.2 51.7 %all-to-all-start.2 = ((bf16[16,16,2048]{2,1,0:T(8,128)(2,1)}), bf16[16,16,2048]{2,1,0:T(8,128)(2,1)}, u32[]{:S(2)}, u32[]{:S(2)}) async-start(bf16[16,16,2048]{2,1,0:T(8,128)(2,1)} %bitcast.97), calls=%async_computation.4 | async-start | bytes 2097152 | tf_op jit(solution)/shard_map/all_to_all | solution.py:249
  753.6 40.7 %collective-permute-start.71 = (bf16[256,2048]{1,0:T(8,128)(2,1)}, bf16[256,2048]{1,0:T(8,128)(2,1)S(1)}, u32[]{:S(2)}, u32[]{:S(2)}) collective-permute-start(bf16[256,2048]{1,0:T(8,128)(2,1)} %add_convert_fusion.10), channel_id=1, source_target_pairs={{0,4},{12,8},{1,5},{13,9},{2,6},{14,10},{3,7},{15,11},{16,20},{28,... | collective-permute-start | bytes 3145736 | tf_op jit(solution)/shard_map/ppermute | solution.py:177
  798.8 58.1 %all-to-all-start.3 = ((bf16[16,16,2048]{2,1,0:T(8,128)(2,1)}), bf16[16,16,2048]{2,1,0:T(8,128)(2,1)}, u32[]{:S(2)}, u32[]{:S(2)}) async-start(bf16[16,16,2048]{2,1,0:T(8,128)(2,1)} %bitcast.36), calls=%async_computation.5 | async-start | bytes 2097152 | tf_op jit(solution)/shard_map/all_to_all | solution.py:249
  808.6 48.3 %collective-permute-start.75 = (bf16[256,2688]{1,0:T(8,128)(2,1)S(1)}, bf16[256,2688]{1,0:T(8,128)(2,1)}, u32[]{:S(2)}, u32[]{:S(2)}) collective-permute-start(bf16[256,2688]{1,0:T(8,128)(2,1)S(1)} %add_convert_fusion.5), channel_id=1, source_target_pairs={{4,0},{8,12},{5,1},{9,13},{6,2},{10,14},{7,3},{11,15},{20,16},{24,... | collective-permute-start | bytes 4128776 | tf_op jit(solution)/shard_map/ppermute | solution.py:185
  811.8 67.0 %collective-permute-start.77 = (bf16[256,2048]{1,0:T(8,128)(2,1)S(1)}, bf16[256,2048]{1,0:T(8,128)(2,1)S(1)}, u32[]{:S(2)}, u32[]{:S(2)}) collective-permute-start(bf16[256,2048]{1,0:T(8,128)(2,1)S(1)} %add_convert_fusion.7), channel_id=1, source_target_pairs={{4,0},{8,12},{5,1},{9,13},{6,2},{10,14},{7,3},{11,15},{20,16},{24,... | collective-permute-start | bytes 3145736 | tf_op jit(solution)/shard_map/ppermute | solution.py:185
  (83 other events, 737.2 us)
Sparse Core Ops, SparseCore 0:
  9.9 82.5 all-gather.4
  94.4 82.8 all-gather.6
  361.8 56.1 reduce-scatter.2
  420.7 102.0 reduce-scatter.4
  524.2 81.8 all-gather.8
  608.1 105.3 all-gather.10

commit v5 on v3

--- a/solution.py
+++ b/solution.py
@@ -426,9 +426,9 @@
         ],
         compiler_params=pltpu.CompilerParams(vmem_limit_bytes=40 * 1024 * 1024),
         cost_estimate=pl.CostEstimate(
-            flops=tiles * keys * width * 128 * 8,
+            flops=tiles * keys * width * 8,
             bytes_accessed=6 * 1024 * 1024,
-            transcendentals=tiles * keys * width // 2,
+            transcendentals=0,
         ),
         name="attend_forward",
     )(q, kv)

time: 899 us -> 899 us (level)
  no operation moved by 1% of the time
where the time goes in v5:
time: 899 us; the launch traced here: 889 us
  waiting for transfers between devices  359 us (40%)
  Pallas kernels  156 us (17%)
  starting transfers between devices  98.3 us (11%)
  local copies, waits for them, and re-layouts  94.5 us (11%)
  other arithmetic  84.4 us (9%)
  matrix products  81.2 us (9%)
  between operations  16.5 us (2%)
    ppermute x72, waiting for transfers between devices, swap(): return lax.ppermute(values, axes, [(i, i ^ mask) for i in range(count)])  220 us
    dot_general x11, matrix products, dot(): return lax.dot_general(left, right, dims, preferred_element_type=f32)  81.2 us
    pallas_call x1, Pallas kernels, attend_backward(): pl.pallas_call(partial(backward_body, groups=groups, heads=heads, rows=ro...  70.2 us
    ppermute x72, starting transfers between devices, swap(): return lax.ppermute(values, axes, [(i, i ^ mask) for i in range(count)])  62.9 us
    all_gather x1, waiting for transfers between devices, on_device(): both_sums = lax.all_gather(jnp.stack(both_part), 'seq', axis=1, tiled=True)  41.1 us
    unnamed x143, local copies, waits for them, and re-layouts  39.8 us
    ppermute x2, waiting for transfers between devices, outwards(): self.moving = lax.ppermute(self.share, 'seq', [(1, 0), (2, 3)])  37.4 us
    pallas_call x1, Pallas kernels, attend_forward(): pl.pallas_call(partial(forward_body, groups=groups, heads=heads, rows=row...  36.4 us
  transfers between devices with their start and end apart: 88, of which 41 were waited for; matrix products, arithmetic and copies ran while one was open for 22% of the time, Pallas kernels for 16%

profile of v5, /device:TPU:0, one launch (start us, length us, event | category | flops | bytes accessed | tf_op | source)
XLA Modules:
  0.0 889.4 jit_solution(12398041927712535106)
XLA Ops:
  20.5 5.0 all-to-all-start
  25.5 4.3 constant_dynamic-slice_fusion.21
  37.1 13.7 %collective-permute-done.5 = bf16[128,640]{1,0:T(8,128)(2,1)S(1)} collective-permute-done((bf16[128,640]{1,0:T(8,128)(2,1)S(1)}, bf16[128,640]{1,0:T(8,128)(2,1)S(1)}, u32[]{:S(2)}, u32[]{:S(2)}) %collective-permute-start.5) | collective-permute-done | bytes 163872 | tf_op jit(solution)/shard_map/ppermute | solution.py:55
  63.8 3.4 collective-permute-start.14
  68.4 5.0 broadcast_in_dim.44
  78.2 10.0 %collective-permute-done.9 = bf16[256,512]{1,0:T(8,128)(2,1)S(1)} collective-permute-done((bf16[256,512]{1,0:T(8,128)(2,1)S(1)}, bf16[256,512]{1,0:T(8,128)(2,1)S(1)}, u32[]{:S(2)}, u32[]{:S(2)}) %collective-permute-start.9) | collective-permute-done | bytes 262176 | tf_op jit(solution)/shard_map/ppermute | solution.py:55
  90.5 4.5 collective-permute-done.12
  95.1 5.5 collective-permute-done.15
  100.7 5.9 collective-permute-done.18
  110.7 3.4 copy-done.6
  114.1 4.7 project.2.q_ref
  119.4 4.8 all-to-all-start.1
  130.4 36.4 %attend_forward.1 = (bf16[256,2048]{1,0:T(8,128)(2,1)S(1)}, f32[8,4,64,256]{3,2,1,0:T(8,128)S(1)}, f32[8,4,256]{2,1,0:T(4,128)S(1)}) custom-call(bf16[256,2048]{1,0:T(8,128)(2,1)S(1)} %project.2.q_ref, bf16[16,16,16,512]{3,2,1,0:T(8,128)(2,1)S(1)} %bitcast.91), custom_call_target="tpu_custom_call" | custom-call | flops 285212672 | bytes 6291456 | tf_op jit(solution)/shard_map/attend_forward/pallas_call | solution.py:404
  170.8 6.4 all-gather.7.cloned.1.call-done
  177.2 6.1 multiply_reduce_fusion.2
  190.7 7.6 maximum_select_fusion.d_ref
  198.3 23.1 %collective-permute-done.26 = bf16[256,2816]{1,0:T(8,128)(2,1)} collective-permute-done((bf16[256,2816]{1,0:T(8,128)(2,1)}, bf16[256,2816]{1,0:T(8,128)(2,1)}, u32[]{:S(2)}, u32[]{:S(2)}) %collective-permute-start.26) | collective-permute-done | bytes 1441824 | tf_op jit(solution)/shard_map/ppermute | solution.py:55
  221.4 21.4 %collective-permute-done.22 = bf16[256,2048]{1,0:T(8,128)(2,1)} collective-permute-done((bf16[256,2048]{1,0:T(8,128)(2,1)}, bf16[256,2048]{1,0:T(8,128)(2,1)}, u32[]{:S(2)}, u32[]{:S(2)}) %collective-permute-start.22) | collective-permute-done | bytes 1048608 | tf_op jit(solution)/shard_map/ppermute | solution.py:55
  267.7 13.5 %collective-permute-done.29 = bf16[128,2048]{1,0:T(8,128)(2,1)S(1)} collective-permute-done((bf16[128,2048]{1,0:T(8,128)(2,1)S(1)}, bf16[128,2048]{1,0:T(8,128)(2,1)S(1)}, u32[]{:S(2)}, u32[]{:S(2)}) %collective-permute-start.29) | collective-permute-done | bytes 524320 | tf_op jit(solution)/shard_map/ppermute | solution.py:55
  285.5 21.5 %feed.1 = (f32[1024,2816]{1,0:T(8,128)}, bf16[1024,1408]{1,0:T(8,128)(2,1)S(1)}) custom-call(bf16[1024,2048]{1,0:T(8,128)(2,1)S(1)} %constant_dynamic-update-slice_fusion.12.x_ref, bf16[2048,2816]{1,0:T(8,128)(2,1)} %constant_dynamic-update-slice_fusion.26.w_ref), custom_call_target="tpu_custom_call" | custom-call | flops 11811160064 | bytes 30146560 | tf_op jit(solution)/shard_map/feed/pallas_call | solution.py:667
  307.3 11.3 %feed_back.1 = bf16[1024,2816]{1,0:T(8,128)(2,1)S(1)} custom-call(bf16[1024,2048]{1,0:T(8,128)(2,1)S(1)} %constant_dynamic-update-slice_fusion.17.c_ref, bf16[1408,2048]{1,0:T(8,128)(2,1)S(1)} %bitcast.90, f32[1024,2816]{1,0:T(8,128)} %get-tuple-element.164.values_ref), custom_call_target="tpu_custom_call" | custom-call | flops 5905580032 | bytes 27262976 | tf_op jit(solution)/shard_map/feed_back/pallas_call | solution.py:696
  318.6 18.4 %convolution_convert_fusion.2 = bf16[1024,2048]{1,0:T(8,128)(2,1)} fusion(bf16[1024,2816]{1,0:T(8,128)(2,1)S(1)} %feed_back.1, bf16[2048,2816]{1,0:T(8,128)(2,1)} %constant_dynamic-update-slice_fusion.26.w_ref), kind=kOutput, calls=%fused_computation.19 | convolution fusion | flops 11813257216 | bytes 21495808 | tf_op jit(solution)/shard_map/dot_general | solution.py:28
  341.5 6.5 convolution_convert_fusion.1
  348.0 4.3 collective-permute-done.36
  353.6 5.3 collective-permute-done.40
  361.7 16.0 %convolution_convert_fusion = bf16[2048,2816]{1,0:T(8,128)(2,1)S(1)} fusion(bf16[1024,2048]{1,0:T(8,128)(2,1)} %copy-done.15, bf16[1024,2816]{1,0:T(8,128)(2,1)} %copy-done.8), kind=kOutput, calls=%fused_computation | convolution fusion | flops 11816927232 | bytes 21495808 | tf_op jit(solution)/shard_map/dot_general | solution.py:28
  388.7 5.3 fusion.38
  394.0 4.2 pad_maximum_fusion
  398.2 9.2 %collective-permute-done.38 = bf16[256,2048]{1,0:T(8,128)(2,1)} collective-permute-done((bf16[256,2048]{1,0:T(8,128)(2,1)}, bf16[256,2048]{1,0:T(8,128)(2,1)}, u32[]{:S(2)}, u32[]{:S(2)}) %collective-permute-start.38) | collective-permute-done | bytes 1048608 | tf_op jit(solution)/shard_map/ppermute | solution.py:55
  414.0 4.7 fusion.71
  418.7 3.8 fusion.37
  422.5 5.9 convolution_convert_fusion.4.do_ref
  432.0 70.2 %attend_backward.1 = (bf16[256,2048]{1,0:T(8,128)(2,1)S(1)}, bf16[16,16,16,512]{3,2,1,0:T(8,128)(2,1)S(1)}) custom-call(bf16[256,2048]{1,0:T(8,128)(2,1)S(1)} %project.2.q_ref, bf16[256,2048]{1,0:T(8,128)(2,1)S(1)} %convolution_convert_fusion.4.do_ref, bf16[16,16,16,512]{3,2,1,0:T(8,128)(2,1)S(1)} %bitcast.92, f32[8,4,64,256]{3,2,1,0:T(8,128)S(1)} %copy-done.11, ...), custom_call_target="tpu_custom_call" | custom-call | flops 285212672 | bytes 8388608 | tf_op jit(solution)/shard_map/attend_backward/pallas_call | solution.py:534
  507.5 3.8 fusion.74
  512.8 4.2 turn_back.2
  518.5 2.9 fusion.11
  528.3 3.7 fusion.16
  532.0 3.7 fusion.77
  535.7 11.3 %collective-permute-done.49 = bf16[4,256,512]{2,1,0:T(8,128)(2,1)S(1)} collective-permute-done((bf16[4,256,512]{2,1,0:T(8,128)(2,1)S(1)}, bf16[4,256,512]{2,1,0:T(8,128)(2,1)S(1)}, u32[]{:S(2)}, u32[]{:S(2)}) %collective-permute-start.49) | collective-permute-done | bytes 1048608 | tf_op jit(solution)/shard_map/ppermute | solution.py:55
  553.1 11.0 %convolution_convert_fusion.3 = bf16[1024,2048]{1,0:T(8,128)(2,1)} fusion(bf16[1024,1408]{1,0:T(8,128)(2,1)S(1)} %copy-done.17, bf16[1408,2048]{1,0:T(8,128)(2,1)} %maximum_select_fusion.d_ref), kind=kOutput, calls=%fused_computation.20 | convolution fusion | flops 5907677184 | bytes 12845056 | tf_op jit(solution)/shard_map/dot_general | solution.py:28
  564.1 9.0 %collective-permute-done.50 = bf16[256,512]{1,0:T(8,128)(2,1)S(1)} collective-permute-done((bf16[256,512]{1,0:T(8,128)(2,1)S(1)}, bf16[256,512]{1,0:T(8,128)(2,1)S(1)}, u32[]{:S(2)}, u32[]{:S(2)}) %collective-permute-start.50) | collective-permute-done | bytes 262176 | tf_op jit(solution)/shard_map/ppermute | solution.py:55
  576.8 4.4 collective-permute-done.51
  581.2 4.9 collective-permute-done.52
  586.1 3.9 collective-permute-done.54
  598.8 3.1 fusion.30
  601.9 3.0 fusion.29
  604.9 12.9 %collective-permute-done.57 = bf16[256,2048]{1,0:T(8,128)(2,1)} collective-permute-done((bf16[256,2048]{1,0:T(8,128)(2,1)}, bf16[256,2048]{1,0:T(8,128)(2,1)}, u32[]{:S(2)}, u32[]{:S(2)}) %collective-permute-start.57) | collective-permute-done | bytes 1048608 | tf_op jit(solution)/shard_map/ppermute | solution.py:55
  617.8 20.8 %collective-permute-done.58 = bf16[256,2048]{1,0:T(8,128)(2,1)} collective-permute-done((bf16[256,2048]{1,0:T(8,128)(2,1)}, bf16[256,2048]{1,0:T(8,128)(2,1)}, u32[]{:S(2)}, u32[]{:S(2)}) %collective-permute-start.58) | collective-permute-done | bytes 1048608 | tf_op jit(solution)/shard_map/ppermute | solution.py:55
  638.6 4.6 fusion.19
  656.2 10.8 %collective-permute-done.65 = bf16[2,512]{0,1:T(8,128)(2,1)S(1)} collective-permute-done((bf16[2,512]{0,1:T(8,128)(2,1)}, bf16[2,512]{0,1:T(8,128)(2,1)S(1)}, u32[]{:S(2)}, u32[]{:S(2)}) %collective-permute-start.65) | collective-permute-done | bytes 2080 | tf_op jit(solution)/shard_map/ppermute | solution.py:55
  672.3 41.1 %all-gather.11.cloned.1.call-done.values_ref = bf16[4,256,2816]{2,1,0:T(8,128)(2,1)} async-done(((bf16[4,64,2816]{2,1,0:T(8,128)(2,1)}), bf16[4,256,2816]{2,1,0:T(8,128)(2,1)}) %all-gather.11.cloned.1.call-update) | async-done | bytes 5767184 | tf_op jit(solution)/shard_map/all_gather | solution.py:917
  721.0 4.4 place_columns.1
  725.4 16.1 %collective-permute-done.69 = bf16[128,4736]{1,0:T(8,128)(2,1)S(1)} collective-permute-done((bf16[128,4736]{1,0:T(8,128)(2,1)S(1)}, bf16[128,4736]{1,0:T(8,128)(2,1)S(1)}, u32[]{:S(2)}, u32[]{:S(2)}) %collective-permute-start.69) | collective-permute-done | bytes 1212448 | tf_op jit(solution)/shard_map/ppermute | solution.py:177
  745.7 7.0 collective-permute-start.71
  752.6 13.4 %collective-permute-done.73 = bf16[256,2048]{1,0:T(8,128)(2,1)S(1)} collective-permute-done((bf16[256,2048]{1,0:T(8,128)(2,1)S(1)}, bf16[256,2048]{1,0:T(8,128)(2,1)S(1)}, u32[]{:S(2)}, u32[]{:S(2)}) %collective-permute-start.73) | collective-permute-done | bytes 1048608 | tf_op jit(solution)/shard_map/ppermute | solution.py:55
  766.1 3.0 add_convert_fusion.9
  769.1 4.5 all-to-all-start.2
  773.6 4.8 collective-permute-done.71
  785.0 12.1 %all-to-all-done.2 = bf16[16,16,2048]{2,1,0:T(8,128)(2,1)S(1)} async-done(((bf16[16,16,2048]{2,1,0:T(8,128)(2,1)}), bf16[16,16,2048]{2,1,0:T(8,128)(2,1)S(1)}, u32[]{:S(2)}, u32[]{:S(2)}) %all-to-all-start.2) | async-done | bytes 1048608 | tf_op jit(solution)/shard_map/all_to_all | solution.py:249
  797.0 6.8 all-to-all-start.3
  808.2 5.1 convert_element_type.382
  814.8 11.0 %collective-permute-done.75 = bf16[128,4736]{1,0:T(8,128)(2,1)} collective-permute-done((bf16[128,4736]{1,0:T(8,128)(2,1)S(1)}, bf16[128,4736]{1,0:T(8,128)(2,1)}, u32[]{:S(2)}, u32[]{:S(2)}) %collective-permute-start.75) | collective-permute-done | bytes 1212448 | tf_op jit(solution)/shard_map/ppermute | solution.py:185
  825.8 19.3 %all-to-all-done.3 = bf16[16,16,2048]{2,1,0:T(8,128)(2,1)} async-done(((bf16[16,16,2048]{2,1,0:T(8,128)(2,1)}), bf16[16,16,2048]{2,1,0:T(8,128)(2,1)}, u32[]{:S(2)}, u32[]{:S(2)}) %all-to-all-start.3) | async-done | bytes 1048608 | tf_op jit(solution)/shard_map/all_to_all | solution.py:249
  845.1 26.4 %collective-permute-done.77 = bf16[128,4736]{1,0:T(8,128)(2,1)} collective-permute-done((bf16[128,4736]{1,0:T(8,128)(2,1)S(1)}, bf16[128,4736]{1,0:T(8,128)(2,1)}, u32[]{:S(2)}, u32[]{:S(2)}) %collective-permute-start.77) | collective-permute-done | bytes 1212448 | tf_op jit(solution)/shard_map/ppermute | solution.py:185
  (406 shorter events, 208.9 us)
Async XLA Ops:
  7.2 103.5 %all-gather.5.cloned.1.call-start = ((), (), s32[]{:S(2)}) async-start(), calls=%async_computation.6 | async-start | bytes 9437184 | tf_op jit(solution)/shard_map/all_gather | solution.py:754
  7.9 169.3 %all-gather.7.cloned.1.call-start = ((), (), s32[]{:S(2)}) async-start(), calls=%async_computation.7 | async-start | bytes 9437184 | tf_op jit(solution)/shard_map/all_gather | solution.py:755
  13.4 22.7 %collective-permute-start = (bf16[256,640]{1,0:T(8,128)(2,1)}, bf16[256,640]{1,0:T(8,128)(2,1)}, u32[]{:S(2)}, u32[]{:S(2)}) collective-permute-start(bf16[256,640]{1,0:T(8,128)(2,1)} %get-tuple-element.341), channel_id=1, source_target_pairs={{0,1},{1,0},{2,3},{3,2},{16,17},{17,16},{18,19},{19,18},{4,5},{5,4... | collective-permute-start | bytes 983048 | tf_op jit(solution)/shard_map/ppermute | solution.py:55
  13.8 19.6 %collective-permute-start.1 = (bf16[256,640]{1,0:T(8,128)(2,1)}, bf16[256,640]{1,0:T(8,128)(2,1)S(1)}, u32[]{:S(2)}, u32[]{:S(2)}) collective-permute-start(bf16[256,640]{1,0:T(8,128)(2,1)} %get-tuple-element.341), channel_id=1, source_target_pairs={{0,2},{1,3},{2,0},{3,1},{16,18},{17,19},{18,16},{19,17},{4,6},{5,7... | collective-permute-start | bytes 983048 | tf_op jit(solution)/shard_map/ppermute | solution.py:55
  16.3 17.5 %collective-permute-start.3 = (bf16[256,640]{1,0:T(8,128)(2,1)}, bf16[256,640]{1,0:T(8,128)(2,1)S(1)}, u32[]{:S(2)}, u32[]{:S(2)}) collective-permute-start(bf16[256,640]{1,0:T(8,128)(2,1)} %get-tuple-element.341), channel_id=1, source_target_pairs={{0,16},{1,17},{2,18},{3,19},{16,0},{17,1},{18,2},{19,3},{4,20},{5,... | collective-permute-start | bytes 983048 | tf_op jit(solution)/shard_map/ppermute | solution.py:55
  20.5 33.0 %all-to-all-start = ((bf16[16,16,2176]{2,1,0:T(8,128)(2,1)}), bf16[16,16,2176]{2,1,0:T(8,128)(2,1)}, u32[]{:S(2)}, u32[]{:S(2)}) async-start(bf16[16,16,2176]{2,1,0:T(8,128)(2,1)} %bitcast.96), calls=%async_computation | async-start | bytes 2228224 | tf_op jit(solution)/shard_map/all_to_all | solution.py:249
  33.4 17.9 %collective-permute-start.2 = (bf16[256,640]{1,0:T(8,128)(2,1)S(1)}, bf16[256,640]{1,0:T(8,128)(2,1)S(1)}, u32[]{:S(2)}, u32[]{:S(2)}) collective-permute-start(bf16[256,640]{1,0:T(8,128)(2,1)S(1)} %collective-permute-done.1), channel_id=1, source_target_pairs={{0,1},{1,0},{2,3},{3,2},{16,17},{17,16},{18,19},{19,18},{4,5},{5,4... | collective-permute-start | bytes 983048 | tf_op jit(solution)/shard_map/ppermute | solution.py:55
  33.8 17.0 %collective-permute-start.5 = (bf16[128,640]{1,0:T(8,128)(2,1)S(1)}, bf16[128,640]{1,0:T(8,128)(2,1)S(1)}, u32[]{:S(2)}, u32[]{:S(2)}) collective-permute-start(bf16[128,640]{1,0:T(8,128)(2,1)S(1)} %slice.215), channel_id=1, source_target_pairs={{0,2},{1,3},{2,0},{3,1},{16,18},{17,19},{18,16},{19,17},{4,6},{5,7... | collective-permute-start | bytes 491528 | tf_op jit(solution)/shard_map/ppermute | solution.py:55
  35.6 15.2 %collective-permute-start.7 = (bf16[128,640]{1,0:T(8,128)(2,1)S(1)}, bf16[128,640]{1,0:T(8,128)(2,1)S(1)}, u32[]{:S(2)}, u32[]{:S(2)}) collective-permute-start(bf16[128,640]{1,0:T(8,128)(2,1)S(1)} %slice.216), channel_id=1, source_target_pairs={{0,16},{1,17},{2,18},{3,19},{16,0},{17,1},{18,2},{19,3},{4,20},{5,... | collective-permute-start | bytes 491528 | tf_op jit(solution)/shard_map/ppermute | solution.py:55
  36.1 15.4 %collective-permute-start.4 = (bf16[256,640]{1,0:T(8,128)(2,1)S(1)}, bf16[256,640]{1,0:T(8,128)(2,1)S(1)}, u32[]{:S(2)}, u32[]{:S(2)}) collective-permute-start(bf16[256,640]{1,0:T(8,128)(2,1)S(1)} %collective-permute-done.3), channel_id=1, source_target_pairs={{0,1},{1,0},{2,3},{3,2},{16,17},{17,16},{18,19},{19,18},{4,5},{5,4... | collective-permute-start | bytes 983048 | tf_op jit(solution)/shard_map/ppermute | solution.py:55
  63.8 24.5 %collective-permute-start.14 = (bf16[256,512]{1,0:T(8,128)(2,1)S(1)}, bf16[256,512]{1,0:T(8,128)(2,1)S(1)}, u32[]{:S(2)}, u32[]{:S(2)}) collective-permute-start(bf16[256,512]{1,0:T(8,128)(2,1)S(1)} %project.3), channel_id=1, source_target_pairs={{0,8},{4,12},{8,0},{12,4},{1,9},{5,13},{9,1},{13,5},{2,10},{6,14},... | collective-permute-start | bytes 786440 | tf_op jit(solution)/shard_map/ppermute | solution.py:55
  67.2 22.1 %collective-permute-start.17 = (bf16[256,512]{1,0:T(8,128)(2,1)S(1)}, bf16[256,512]{1,0:T(8,128)(2,1)S(1)}, u32[]{:S(2)}, u32[]{:S(2)}) collective-permute-start(bf16[256,512]{1,0:T(8,128)(2,1)S(1)} %project.3), channel_id=1, source_target_pairs={{0,12},{4,8},{8,4},{12,0},{1,13},{5,9},{9,5},{13,1},{2,14},{6,10},... | collective-permute-start | bytes 786440 | tf_op jit(solution)/shard_map/ppermute | solution.py:55
  77.0 18.0 %collective-permute-start.12 = (bf16[256,512]{1,0:T(8,128)(2,1)S(1)}, bf16[256,512]{1,0:T(8,128)(2,1)S(1)}, u32[]{:S(2)}, u32[]{:S(2)}) collective-permute-start(bf16[256,512]{1,0:T(8,128)(2,1)S(1)} %collective-permute-done.11), channel_id=1, source_target_pairs={{0,2},{1,3},{2,0},{3,1},{4,6},{5,7},{6,4},{7,5},{8,10},{9,11},{10,... | collective-permute-start | bytes 786440 | tf_op jit(solution)/shard_map/ppermute | solution.py:55
  88.2 18.5 %collective-permute-start.10 = (bf16[512,512]{1,0:T(8,128)(2,1)S(1)}, bf16[512,512]{1,0:T(8,128)(2,1)S(1)}, u32[]{:S(2)}, u32[]{:S(2)}) collective-permute-start(bf16[512,512]{1,0:T(8,128)(2,1)S(1)} %pad_maximum_fusion.12), channel_id=1, source_target_pairs={{0,1},{1,0},{2,3},{3,2},{4,5},{5,4},{6,7},{7,6},{8,9},{9,8},{10,11... | collective-permute-start | bytes 1572872 | tf_op jit(solution)/shard_map/ppermute | solution.py:55
  89.3 17.3 %collective-permute-start.18 = (bf16[256,512]{1,0:T(8,128)(2,1)S(1)}, bf16[256,512]{1,0:T(8,128)(2,1)S(1)}, u32[]{:S(2)}, u32[]{:S(2)}) collective-permute-start(bf16[256,512]{1,0:T(8,128)(2,1)S(1)} %collective-permute-done.17), channel_id=1, source_target_pairs={{0,2},{1,3},{2,0},{3,1},{4,6},{5,7},{6,4},{7,5},{8,10},{9,11},{10,... | collective-permute-start | bytes 786440 | tf_op jit(solution)/shard_map/ppermute | solution.py:55
  118.8 52.0 %collective-permute-start.20 = (bf16[704,2048]{1,0:T(8,128)(2,1)}, bf16[704,2048]{1,0:T(8,128)(2,1)}, u32[]{:S(2)}, u32[]{:S(2)}) collective-permute-start(bf16[704,2048]{1,0:T(8,128)(2,1)} %param.21), channel_id=1, source_target_pairs={{0,1},{1,0},{2,3},{3,2},{16,17},{17,16},{18,19},{19,18},{4,5},{5,4... | collective-permute-start | bytes 8650760 | tf_op jit(solution)/shard_map/ppermute | solution.py:55
  119.0 51.7 %collective-permute-start.21 = (bf16[256,2816]{1,0:T(8,128)(2,1)}, bf16[256,2816]{1,0:T(8,128)(2,1)}, u32[]{:S(2)}, u32[]{:S(2)}) collective-permute-start(bf16[256,2816]{1,0:T(8,128)(2,1)} %pad_maximum_fusion.5), channel_id=1, source_target_pairs={{0,1},{1,0},{2,3},{3,2},{16,17},{17,16},{18,19},{19,18},{4,5},{5,4... | collective-permute-start | bytes 4325384 | tf_op jit(solution)/shard_map/ppermute | solution.py:55
  119.4 66.4 %all-to-all-start.1 = ((bf16[16,16,2048]{2,1,0:T(8,128)(2,1)}), bf16[16,16,2048]{2,1,0:T(8,128)(2,1)}, u32[]{:S(2)}, u32[]{:S(2)}) async-start(bf16[16,16,2048]{2,1,0:T(8,128)(2,1)} %bitcast.101), calls=%async_computation.1 | async-start | bytes 2097152 | tf_op jit(solution)/shard_map/all_to_all | solution.py:249
  124.2 383.3 %reduce-scatter.3.cloned.1.call-start = ((), (), s32[]{:S(2)}) async-start(), calls=%async_computation.8 | async-start | bytes 3604480 | tf_op jit(solution)/shard_map/reduce_scatter | solution.py:871
  124.7 73.6 %collective-permute-start.24 = (bf16[256,2816]{1,0:T(8,128)(2,1)}, bf16[256,2816]{1,0:T(8,128)(2,1)}, u32[]{:S(2)}, u32[]{:S(2)}) collective-permute-start(bf16[256,2816]{1,0:T(8,128)(2,1)} %pad_maximum_fusion.6), channel_id=1, source_target_pairs={{0,2},{1,3},{2,0},{3,1},{16,18},{17,19},{18,16},{19,17},{4,6},{5,7... | collective-permute-start | bytes 4325384 | tf_op jit(solution)/shard_map/ppermute | solution.py:55
  126.6 71.7 %collective-permute-start.25 = (bf16[256,2816]{1,0:T(8,128)(2,1)}, bf16[256,2816]{1,0:T(8,128)(2,1)}, u32[]{:S(2)}, u32[]{:S(2)}) collective-permute-start(bf16[256,2816]{1,0:T(8,128)(2,1)} %pad_maximum_fusion.7), channel_id=1, source_target_pairs={{0,16},{1,17},{2,18},{3,19},{16,0},{17,1},{18,2},{19,3},{4,20},{5,... | collective-permute-start | bytes 4325384 | tf_op jit(solution)/shard_map/ppermute | solution.py:55
  128.1 93.3 %collective-permute-start.26 = (bf16[256,2816]{1,0:T(8,128)(2,1)}, bf16[256,2816]{1,0:T(8,128)(2,1)}, u32[]{:S(2)}, u32[]{:S(2)}) collective-permute-start(bf16[256,2816]{1,0:T(8,128)(2,1)} %pad_maximum_fusion.8), channel_id=1, source_target_pairs={{0,18},{1,19},{2,16},{3,17},{16,2},{17,3},{18,0},{19,1},{4,22},{5,... | collective-permute-start | bytes 4325384 | tf_op jit(solution)/shard_map/ppermute | solution.py:55
  185.8 57.0 %collective-permute-start.22 = (bf16[256,2048]{1,0:T(8,128)(2,1)}, bf16[256,2048]{1,0:T(8,128)(2,1)}, u32[]{:S(2)}, u32[]{:S(2)}) collective-permute-start(bf16[256,2048]{1,0:T(8,128)(2,1)} %multiply_convert_fusion), channel_id=1, source_target_pairs={{0,2},{1,3},{2,0},{3,1},{16,18},{17,19},{18,16},{19,17},{4,6},{5,7... | collective-permute-start | bytes 3145736 | tf_op jit(solution)/shard_map/ppermute | solution.py:55
  186.0 56.8 %collective-permute-start.23 = (bf16[256,2048]{1,0:T(8,128)(2,1)}, bf16[256,2048]{1,0:T(8,128)(2,1)}, u32[]{:S(2)}, u32[]{:S(2)}) collective-permute-start(bf16[256,2048]{1,0:T(8,128)(2,1)} %multiply_convert_fusion), channel_id=1, source_target_pairs={{0,16},{1,17},{2,18},{3,19},{16,0},{17,1},{18,2},{19,3},{4,20},{5,... | collective-permute-start | bytes 3145736 | tf_op jit(solution)/shard_map/ppermute | solution.py:55
  244.1 38.1 %collective-permute-start.27 = (bf16[256,2048]{1,0:T(8,128)(2,1)}, bf16[256,2048]{1,0:T(8,128)(2,1)S(1)}, u32[]{:S(2)}, u32[]{:S(2)}) collective-permute-start(bf16[256,2048]{1,0:T(8,128)(2,1)} %bitcast.9), channel_id=1, source_target_pairs={{0,2},{1,3},{2,0},{3,1},{16,18},{17,19},{18,16},{19,17},{4,6},{5,7... | collective-permute-start | bytes 3145736 | tf_op jit(solution)/shard_map/ppermute | solution.py:55
  245.5 36.7 %collective-permute-start.28 = (bf16[256,2048]{1,0:T(8,128)(2,1)}, bf16[256,2048]{1,0:T(8,128)(2,1)S(1)}, u32[]{:S(2)}, u32[]{:S(2)}) collective-permute-start(bf16[256,2048]{1,0:T(8,128)(2,1)} %bitcast.9), channel_id=1, source_target_pairs={{0,16},{1,17},{2,18},{3,19},{16,0},{17,1},{18,2},{19,3},{4,20},{5,... | collective-permute-start | bytes 3145736 | tf_op jit(solution)/shard_map/ppermute | solution.py:55
  247.3 33.9 %collective-permute-start.29 = (bf16[128,2048]{1,0:T(8,128)(2,1)S(1)}, bf16[128,2048]{1,0:T(8,128)(2,1)S(1)}, u32[]{:S(2)}, u32[]{:S(2)}) collective-permute-start(bf16[128,2048]{1,0:T(8,128)(2,1)S(1)} %slice.174), channel_id=1, source_target_pairs={{0,2},{1,3},{2,0},{3,1},{16,18},{17,19},{18,16},{19,17},{4,6},{5,7... | collective-permute-start | bytes 1572872 | tf_op jit(solution)/shard_map/ppermute | solution.py:55
  262.2 20.0 %collective-permute-start.30 = (bf16[128,2048]{1,0:T(8,128)(2,1)S(1)}, bf16[128,2048]{1,0:T(8,128)(2,1)S(1)}, u32[]{:S(2)}, u32[]{:S(2)}) collective-permute-start(bf16[128,2048]{1,0:T(8,128)(2,1)S(1)} %slice.175), channel_id=1, source_target_pairs={{0,16},{1,17},{2,18},{3,19},{16,0},{17,1},{18,2},{19,3},{4,20},{5,... | collective-permute-start | bytes 1572872 | tf_op jit(solution)/shard_map/ppermute | solution.py:55
  282.2 24.9 %collective-permute-start.34 = (bf16[128,2048]{1,0:T(8,128)(2,1)S(1)}, bf16[128,2048]{1,0:T(8,128)(2,1)S(1)}, u32[]{:S(2)}, u32[]{:S(2)}) collective-permute-start(bf16[128,2048]{1,0:T(8,128)(2,1)S(1)} %slice.176), channel_id=1, source_target_pairs={{0,2},{1,3},{2,0},{3,1},{16,18},{17,19},{18,16},{19,17},{4,6},{5,7... | collective-permute-start | bytes 1572872 | tf_op jit(solution)/shard_map/ppermute | solution.py:55
  283.9 23.3 %collective-permute-start.35 = (bf16[128,2048]{1,0:T(8,128)(2,1)}, bf16[128,2048]{1,0:T(8,128)(2,1)S(1)}, u32[]{:S(2)}, u32[]{:S(2)}) collective-permute-start(bf16[128,2048]{1,0:T(8,128)(2,1)} %slice.177), channel_id=1, source_target_pairs={{0,16},{1,17},{2,18},{3,19},{16,0},{17,1},{18,2},{19,3},{4,20},{5,... | collective-permute-start | bytes 1572872 | tf_op jit(solution)/shard_map/ppermute | solution.py:55
  361.7 185.3 %reduce-scatter.5.cloned.1.call-start = ((), (), s32[]{:S(2)}) async-start(), calls=%async_computation.9 | async-start | bytes 7208960 | tf_op jit(solution)/shard_map/reduce_scatter | solution.py:875
  381.9 25.5 %collective-permute-start.38 = (bf16[256,2048]{1,0:T(8,128)(2,1)}, bf16[256,2048]{1,0:T(8,128)(2,1)}, u32[]{:S(2)}, u32[]{:S(2)}) collective-permute-start(bf16[256,2048]{1,0:T(8,128)(2,1)} %pad_maximum_fusion.10), channel_id=1, source_target_pairs={{0,2},{1,3},{2,0},{3,1},{16,18},{17,19},{18,16},{19,17},{4,6},{5,7... | collective-permute-start | bytes 3145736 | tf_op jit(solution)/shard_map/ppermute | solution.py:55
  384.2 25.2 %collective-permute-start.39 = (bf16[256,2048]{1,0:T(8,128)(2,1)}, bf16[256,2048]{1,0:T(8,128)(2,1)}, u32[]{:S(2)}, u32[]{:S(2)}) collective-permute-start(bf16[256,2048]{1,0:T(8,128)(2,1)} %pad_maximum_fusion.11), channel_id=1, source_target_pairs={{0,16},{1,17},{2,18},{3,19},{16,0},{17,1},{18,2},{19,3},{4,20},{5,... | collective-permute-start | bytes 3145736 | tf_op jit(solution)/shard_map/ppermute | solution.py:55
  409.4 246.8 %all-gather.9.cloned.1.call-start = ((), (), s32[]{:S(2)}) async-start(), calls=%async_computation.10 | async-start | bytes 3604480 | tf_op jit(solution)/shard_map/all_gather | solution.py:898
  428.4 76.8 %collective-permute-start.45 = (bf16[256,3072]{1,0:T(8,128)(2,1)S(1)}, bf16[256,3072]{1,0:T(8,128)(2,1)S(1)}, u32[]{:S(2)}, u32[]{:S(2)}) collective-permute-start(bf16[256,3072]{1,0:T(8,128)(2,1)S(1)} %get-tuple-element.182), channel_id=1, source_target_pairs={{0,2},{1,3},{2,0},{3,1},{16,18},{17,19},{18,16},{19,17},{4,6},{5,7... | collective-permute-start | bytes 4718600 | tf_op jit(solution)/shard_map/ppermute | solution.py:55
  429.3 75.9 %collective-permute-start.46 = (bf16[256,3072]{1,0:T(8,128)(2,1)S(1)}, bf16[256,3072]{1,0:T(8,128)(2,1)S(1)}, u32[]{:S(2)}, u32[]{:S(2)}) collective-permute-start(bf16[256,3072]{1,0:T(8,128)(2,1)S(1)} %get-tuple-element.183), channel_id=1, source_target_pairs={{0,16},{1,17},{2,18},{3,19},{16,0},{17,1},{18,2},{19,3},{4,20},{5,... | collective-permute-start | bytes 4718600 | tf_op jit(solution)/shard_map/ppermute | solution.py:55
  430.7 76.8 %collective-permute-start.47 = (bf16[256,3072]{1,0:T(8,128)(2,1)S(1)}, bf16[256,3072]{1,0:T(8,128)(2,1)}, u32[]{:S(2)}, u32[]{:S(2)}) collective-permute-start(bf16[256,3072]{1,0:T(8,128)(2,1)S(1)} %get-tuple-element.184), channel_id=1, source_target_pairs={{0,18},{1,19},{2,16},{3,17},{16,2},{17,3},{18,0},{19,1},{4,22},{5,... | collective-permute-start | bytes 4718600 | tf_op jit(solution)/shard_map/ppermute | solution.py:55
  512.8 200.7 %all-gather.11.cloned.1.call-start = ((), (), s32[]{:S(2)}) async-start(), calls=%async_computation.11 | async-start | bytes 7208960 | tf_op jit(solution)/shard_map/all_gather | solution.py:917
  521.4 25.5 %collective-permute-start.49 = (bf16[4,256,512]{2,1,0:T(8,128)(2,1)S(1)}, bf16[4,256,512]{2,1,0:T(8,128)(2,1)S(1)}, u32[]{:S(2)}, u32[]{:S(2)}) collective-permute-start(bf16[4,256,512]{2,1,0:T(8,128)(2,1)S(1)} %slice_bitcast_fusion.1), channel_id=1, source_target_pairs={{0,2},{1,3},{2,0},{3,1},{4,6},{5,7},{6,4},{7,5},{8,10},{9,11},{10,... | collective-permute-start | bytes 3145736 | tf_op jit(solution)/shard_map/ppermute | solution.py:55
  547.3 25.8 %collective-permute-start.50 = (bf16[256,512]{1,0:T(8,128)(2,1)S(1)}, bf16[256,512]{1,0:T(8,128)(2,1)S(1)}, u32[]{:S(2)}, u32[]{:S(2)}) collective-permute-start(bf16[256,512]{1,0:T(8,128)(2,1)S(1)} %get-tuple-element.322), channel_id=1, source_target_pairs={{0,4},{4,0},{8,12},{12,8},{1,5},{5,1},{9,13},{13,9},{2,6},{6,2},{1... | collective-permute-start | bytes 786440 | tf_op jit(solution)/shard_map/ppermute | solution.py:55
  548.8 32.3 %collective-permute-start.51 = (bf16[256,512]{1,0:T(8,128)(2,1)S(1)}, bf16[256,512]{1,0:T(8,128)(2,1)S(1)}, u32[]{:S(2)}, u32[]{:S(2)}) collective-permute-start(bf16[256,512]{1,0:T(8,128)(2,1)S(1)} %get-tuple-element.321), channel_id=1, source_target_pairs={{0,8},{4,12},{8,0},{12,4},{1,9},{5,13},{9,1},{13,5},{2,10},{6,14},... | collective-permute-start | bytes 786440 | tf_op jit(solution)/shard_map/ppermute | solution.py:55
  551.3 34.8 %collective-permute-start.52 = (bf16[256,512]{1,0:T(8,128)(2,1)S(1)}, bf16[256,512]{1,0:T(8,128)(2,1)S(1)}, u32[]{:S(2)}, u32[]{:S(2)}) collective-permute-start(bf16[256,512]{1,0:T(8,128)(2,1)S(1)} %get-tuple-element.320), channel_id=1, source_target_pairs={{0,12},{4,8},{8,4},{12,0},{1,13},{5,9},{9,5},{13,1},{2,14},{6,10},... | collective-permute-start | bytes 786440 | tf_op jit(solution)/shard_map/ppermute | solution.py:55
  551.9 34.2 %collective-permute-start.53 = (bf16[64,2816]{1,0:T(8,128)(2,1)S(1)}, bf16[64,2816]{1,0:T(8,128)(2,1)S(1)}, u32[]{:S(2)}, u32[]{:S(2)}) collective-permute-start(bf16[64,2816]{1,0:T(8,128)(2,1)S(1)} %get-tuple-element.318), channel_id=1, source_target_pairs={{0,2},{1,3},{2,0},{3,1},{16,18},{17,19},{18,16},{19,17},{4,6},{5,7... | collective-permute-start | bytes 1081352 | tf_op jit(solution)/shard_map/ppermute | solution.py:55
  553.0 20.9 %collective-permute-start.56 = (bf16[256,2048]{1,0:T(8,128)(2,1)S(1)}, bf16[256,2048]{1,0:T(8,128)(2,1)S(1)}, u32[]{:S(2)}, u32[]{:S(2)}) collective-permute-start(bf16[256,2048]{1,0:T(8,128)(2,1)S(1)} %constant_dynamic-slice_fusion.6), channel_id=1, source_target_pairs={{0,1},{1,0},{2,3},{3,2},{16,17},{17,16},{18,19},{19,18},{4,5},{5,4... | collective-permute-start | bytes 3145736 | tf_op jit(solution)/shard_map/ppermute | solution.py:55
  573.1 16.9 %collective-permute-start.54 = (bf16[64,2816]{1,0:T(8,128)(2,1)S(1)}, bf16[64,2816]{1,0:T(8,128)(2,1)S(1)}, u32[]{:S(2)}, u32[]{:S(2)}) collective-permute-start(bf16[64,2816]{1,0:T(8,128)(2,1)S(1)} %get-tuple-element.317), channel_id=1, source_target_pairs={{0,16},{1,17},{2,18},{3,19},{16,0},{17,1},{18,2},{19,3},{4,20},{5,... | collective-permute-start | bytes 1081352 | tf_op jit(solution)/shard_map/ppermute | solution.py:55
  573.9 16.1 %collective-permute-start.55 = (bf16[64,2816]{1,0:T(8,128)(2,1)S(1)}, bf16[64,2816]{1,0:T(8,128)(2,1)S(1)}, u32[]{:S(2)}, u32[]{:S(2)}) collective-permute-start(bf16[64,2816]{1,0:T(8,128)(2,1)S(1)} %get-tuple-element.316), channel_id=1, source_target_pairs={{0,18},{1,19},{2,16},{3,17},{16,2},{17,3},{18,0},{19,1},{4,22},{5,... | collective-permute-start | bytes 1081352 | tf_op jit(solution)/shard_map/ppermute | solution.py:55
  591.4 26.5 %collective-permute-start.57 = (bf16[256,2048]{1,0:T(8,128)(2,1)}, bf16[256,2048]{1,0:T(8,128)(2,1)}, u32[]{:S(2)}, u32[]{:S(2)}) collective-permute-start(bf16[256,2048]{1,0:T(8,128)(2,1)} %turn_back.2), channel_id=1, source_target_pairs={{0,2},{1,3},{2,0},{3,1},{16,18},{17,19},{18,16},{19,17},{4,6},{5,7... | collective-permute-start | bytes 3145736 | tf_op jit(solution)/shard_map/ppermute | solution.py:55
  592.5 46.2 %collective-permute-start.58 = (bf16[256,2048]{1,0:T(8,128)(2,1)}, bf16[256,2048]{1,0:T(8,128)(2,1)}, u32[]{:S(2)}, u32[]{:S(2)}) collective-permute-start(bf16[256,2048]{1,0:T(8,128)(2,1)} %turn_back.2), channel_id=1, source_target_pairs={{0,16},{1,17},{2,18},{3,19},{16,0},{17,1},{18,2},{19,3},{4,20},{5,... | collective-permute-start | bytes 3145736 | tf_op jit(solution)/shard_map/ppermute | solution.py:55
  593.9 44.7 %collective-permute-start.59 = (bf16[256,2048]{1,0:T(8,128)(2,1)}, bf16[256,2048]{1,0:T(8,128)(2,1)}, u32[]{:S(2)}, u32[]{:S(2)}) collective-permute-start(bf16[256,2048]{1,0:T(8,128)(2,1)} %turn_back.2), channel_id=1, source_target_pairs={{0,18},{1,19},{2,16},{3,17},{16,2},{17,3},{18,0},{19,1},{4,22},{5,... | collective-permute-start | bytes 3145736 | tf_op jit(solution)/shard_map/ppermute | solution.py:55
  646.8 20.2 %collective-permute-start.61 = (bf16[256,512]{1,0:T(8,128)(2,1)}, bf16[256,512]{1,0:T(8,128)(2,1)}, u32[]{:S(2)}, u32[]{:S(2)}) collective-permute-start(bf16[256,512]{1,0:T(8,128)(2,1)} %turn_back.3), channel_id=1, source_target_pairs={{0,2},{1,3},{2,0},{3,1},{16,18},{17,19},{18,16},{19,17},{4,6},{5,7... | collective-permute-start | bytes 786440 | tf_op jit(solution)/shard_map/ppermute | solution.py:55
  647.4 19.6 %collective-permute-start.62 = (bf16[256,512]{1,0:T(8,128)(2,1)}, bf16[256,512]{1,0:T(8,128)(2,1)}, u32[]{:S(2)}, u32[]{:S(2)}) collective-permute-start(bf16[256,512]{1,0:T(8,128)(2,1)} %turn_back.3), channel_id=1, source_target_pairs={{0,16},{1,17},{2,18},{3,19},{16,0},{17,1},{18,2},{19,3},{4,20},{5,... | collective-permute-start | bytes 786440 | tf_op jit(solution)/shard_map/ppermute | solution.py:55
  649.1 17.9 %collective-permute-start.63 = (bf16[256,512]{1,0:T(8,128)(2,1)}, bf16[256,512]{1,0:T(8,128)(2,1)}, u32[]{:S(2)}, u32[]{:S(2)}) collective-permute-start(bf16[256,512]{1,0:T(8,128)(2,1)} %turn_back.3), channel_id=1, source_target_pairs={{0,18},{1,19},{2,16},{3,17},{16,2},{17,3},{18,0},{19,1},{4,22},{5,... | collective-permute-start | bytes 786440 | tf_op jit(solution)/shard_map/ppermute | solution.py:55
  651.7 15.3 %collective-permute-start.65 = (bf16[2,512]{0,1:T(8,128)(2,1)}, bf16[2,512]{0,1:T(8,128)(2,1)S(1)}, u32[]{:S(2)}, u32[]{:S(2)}) collective-permute-start(bf16[2,512]{0,1:T(8,128)(2,1)} %get-tuple-element.338), channel_id=1, source_target_pairs={{0,16},{1,17},{2,18},{3,19},{16,0},{17,1},{18,2},{19,3},{4,20},{5,... | collective-permute-start | bytes 6152 | tf_op jit(solution)/shard_map/ppermute | solution.py:55
  713.6 28.0 %collective-permute-start.69 = (bf16[128,4736]{1,0:T(8,128)(2,1)S(1)}, bf16[128,4736]{1,0:T(8,128)(2,1)S(1)}, u32[]{:S(2)}, u32[]{:S(2)}) collective-permute-start(bf16[128,4736]{1,0:T(8,128)(2,1)S(1)} %slice.200), channel_id=1, source_target_pairs={{0,4},{12,8},{1,5},{13,9},{2,6},{14,10},{3,7},{15,11},{16,20},{28,... | collective-permute-start | bytes 3637256 | tf_op jit(solution)/shard_map/ppermute | solution.py:177
  717.5 35.2 %collective-permute-start.74 = (bf16[256,2048]{1,0:T(8,128)(2,1)S(1)}, bf16[256,2048]{1,0:T(8,128)(2,1)S(1)}, u32[]{:S(2)}, u32[]{:S(2)}) collective-permute-start(bf16[256,2048]{1,0:T(8,128)(2,1)S(1)} %get-tuple-element.298), channel_id=1, source_target_pairs={{0,18},{1,19},{2,16},{3,17},{16,2},{17,3},{18,0},{19,1},{4,22},{5,... | collective-permute-start | bytes 3145736 | tf_op jit(solution)/shard_map/ppermute | solution.py:55
  719.9 46.1 %collective-permute-start.73 = (bf16[256,2048]{1,0:T(8,128)(2,1)S(1)}, bf16[256,2048]{1,0:T(8,128)(2,1)S(1)}, u32[]{:S(2)}, u32[]{:S(2)}) collective-permute-start(bf16[256,2048]{1,0:T(8,128)(2,1)S(1)} %get-tuple-element.299), channel_id=1, source_target_pairs={{0,16},{1,17},{2,18},{3,19},{16,0},{17,1},{18,2},{19,3},{4,20},{5,... | collective-permute-start | bytes 3145736 | tf_op jit(solution)/shard_map/ppermute | solution.py:55
  720.5 45.6 %collective-permute-start.72 = (bf16[256,2048]{1,0:T(8,128)(2,1)S(1)}, bf16[256,2048]{1,0:T(8,128)(2,1)S(1)}, u32[]{:S(2)}, u32[]{:S(2)}) collective-permute-start(bf16[256,2048]{1,0:T(8,128)(2,1)S(1)} %get-tuple-element.297), channel_id=1, source_target_pairs={{0,2},{1,3},{2,0},{3,1},{16,18},{17,19},{18,16},{19,17},{4,6},{5,7... | collective-permute-start | bytes 3145736 | tf_op jit(solution)/shard_map/ppermute | solution.py:55
  742.8 30.8 %collective-permute-start.70 = (bf16[128,4736]{1,0:T(8,128)(2,1)}, bf16[128,4736]{1,0:T(8,128)(2,1)}, u32[]{:S(2)}, u32[]{:S(2)}) collective-permute-start(bf16[128,4736]{1,0:T(8,128)(2,1)} %add_convert_fusion.8), channel_id=1, source_target_pairs={{4,8},{8,4},{5,9},{9,5},{6,10},{10,6},{7,11},{11,7},{20,24},{24,20... | collective-permute-start | bytes 3637256 | tf_op jit(solution)/shard_map/ppermute | solution.py:181
  745.7 32.8 %collective-permute-start.71 = (bf16[128,4736]{1,0:T(8,128)(2,1)}, bf16[128,4736]{1,0:T(8,128)(2,1)}, u32[]{:S(2)}, u32[]{:S(2)}) collective-permute-start(bf16[128,4736]{1,0:T(8,128)(2,1)} %slice.201), channel_id=1, source_target_pairs={{0,4},{12,8},{1,5},{13,9},{2,6},{14,10},{3,7},{15,11},{16,20},{28,... | collective-permute-start | bytes 3637256 | tf_op jit(solution)/shard_map/ppermute | solution.py:177
  769.1 27.9 %all-to-all-start.2 = ((bf16[16,16,2048]{2,1,0:T(8,128)(2,1)}), bf16[16,16,2048]{2,1,0:T(8,128)(2,1)S(1)}, u32[]{:S(2)}, u32[]{:S(2)}) async-start(bf16[16,16,2048]{2,1,0:T(8,128)(2,1)} %bitcast.98), calls=%async_computation.4 | async-start | bytes 2097152 | tf_op jit(solution)/shard_map/all_to_all | solution.py:249
  781.0 22.9 %collective-permute-start.76 = (bf16[128,4736]{1,0:T(8,128)(2,1)}, bf16[128,4736]{1,0:T(8,128)(2,1)S(1)}, u32[]{:S(2)}, u32[]{:S(2)}) collective-permute-start(bf16[128,4736]{1,0:T(8,128)(2,1)} %add_convert_fusion.6), channel_id=1, source_target_pairs={{4,8},{8,4},{5,9},{9,5},{6,10},{10,6},{7,11},{11,7},{20,24},{24,20... | collective-permute-start | bytes 3637256 | tf_op jit(solution)/shard_map/ppermute | solution.py:181
  783.7 42.1 %collective-permute-start.75 = (bf16[128,4736]{1,0:T(8,128)(2,1)S(1)}, bf16[128,4736]{1,0:T(8,128)(2,1)}, u32[]{:S(2)}, u32[]{:S(2)}) collective-permute-start(bf16[128,4736]{1,0:T(8,128)(2,1)S(1)} %add_convert_fusion.7), channel_id=1, source_target_pairs={{4,0},{8,12},{5,1},{9,13},{6,2},{10,14},{7,3},{11,15},{20,16},{24,... | collective-permute-start | bytes 3637256 | tf_op jit(solution)/shard_map/ppermute | solution.py:185
  797.0 48.1 %all-to-all-start.3 = ((bf16[16,16,2048]{2,1,0:T(8,128)(2,1)}), bf16[16,16,2048]{2,1,0:T(8,128)(2,1)}, u32[]{:S(2)}, u32[]{:S(2)}) async-start(bf16[16,16,2048]{2,1,0:T(8,128)(2,1)} %bitcast.36), calls=%async_computation.5 | async-start | bytes 2097152 | tf_op jit(solution)/shard_map/all_to_all | solution.py:249
  806.8 64.7 %collective-permute-start.77 = (bf16[128,4736]{1,0:T(8,128)(2,1)S(1)}, bf16[128,4736]{1,0:T(8,128)(2,1)}, u32[]{:S(2)}, u32[]{:S(2)}) collective-permute-start(bf16[128,4736]{1,0:T(8,128)(2,1)S(1)} %add_convert_fusion.5), channel_id=1, source_target_pairs={{4,0},{8,12},{5,1},{9,13},{6,2},{10,14},{7,3},{11,15},{20,16},{24,... | collective-permute-start | bytes 3637256 | tf_op jit(solution)/shard_map/ppermute | solution.py:185
  (81 other events, 630.0 us)
Sparse Core Ops, SparseCore 0:
  9.9 82.5 all-gather.4
  94.4 82.7 all-gather.6
  361.8 56.1 reduce-scatter.2
  420.7 102.0 reduce-scatter.4
  524.3 81.8 all-gather.8
  608.1 105.3 all-gather.10
